TPU v7x, 32 devices: a whole 2x2x4 slice. The times are simulated.
32 devices in a mesh: ctx: 8 (over z, x), head: 2 (over y), dp: 2 (over core).
Axes of the slice: x: 2, y: 2, z: 4, core: 2. Of those that a mesh axis runs over, the one named last changes fastest.
Arguments:
- query: bfloat16 [2, 4096, 5120], P('dp', 'ctx', 'head'), may hold values from -6 to 6
- key: bfloat16 [2, 4096, 1024], P('dp', 'ctx', 'head'), may hold values from -6 to 6
- value: bfloat16 [2, 4096, 1024], P('dp', 'ctx', 'head'), may hold values from -6 to 6
- output: bfloat16 [2, 4096, 5120], P('dp', 'ctx', 'head'), may hold values from -1.796875 to 1.796875
- output_gradient: bfloat16 [2, 4096, 5120], P('dp', 'ctx', 'head'), may hold values from -96 to 96
- parent: int32 [2, 8], P('dp'), may hold values from -1 to 6, as said below
- owner: int32 [2, 8], P('dp'), may hold values from 0 to 7, each once within a row
Outputs:
- d_query: bfloat16 [2, 4096, 5120], P('dp', 'ctx', 'head')
- d_key: bfloat16 [2, 4096, 1024], P('dp', 'ctx', 'head')
- d_value: bfloat16 [2, 4096, 1024], P('dp', 'ctx', 'head')
- bias_q_grad: float32 [5120], P('head')
- bias_k_grad: float32 [1024], P('head')
- bias_v_grad: float32 [1024], P('head')
Inputs may be any that keep to these rules, and one draw needn't show every extreme that they name: In each tree, tiles 0 to 0 form the prompt, each with parent t - 1 (tile 0 has -1); the later tiles form 4 consecutive runs (responses) of 1 or 2 tiles, some run of 2 in every tree; a run's first tile has as parent the last prompt tile, its second tile has the run's first tile.
All inputs are finite; a program needn't handle non-finite values.
Results may differ from a plain program's by a relative error of at most 0.005.
Values may be sent and summed in bfloat16 or wider, within the bound.
No kernel may reach another device: no remote copies, remote signals or barrier semaphores. Data moves between devices by JAX's collectives and lax.ppermute only.
A program may use at most 128 MiB of HBM per device.

v0:
```python
import jax
import jax.numpy as jnp
from jax import lax
from jax.sharding import PartitionSpec as P

HEAD_WIDTH = 128


NEGATIVE_FILL = -1e30


def passed_along(block, axis, distance):
    devices = range(lax.axis_size(axis))
    route = [((i - distance) % len(devices), i) for i in devices]
    return lax.ppermute(block, axis, route)


def tree_tables(parent_row, owner_row):
    count = parent_row.shape[0]
    tiles = jnp.arange(count, dtype=jnp.int32)
    tile_at = jnp.sum(jnp.where(owner_row[None, :] == tiles[:, None], tiles[None, :], 0), axis=1)

    def climb(step, state):
        reach, current = state
        match = current[:, None] == tiles[None, :]
        reach = jnp.logical_or(reach, match)
        upward = jnp.sum(jnp.where(match, parent_row[None, :], 0), axis=1)
        upward = jnp.where(current < 0, -1, upward)
        return (reach, upward)

    reach, _ = lax.fori_loop(0, count, climb, (jnp.zeros((count, count), bool), tiles))
    select = (tile_at[:, None] == tiles[None, :]).astype(jnp.float32)
    packed = jnp.dot(
        jnp.dot(select, reach.astype(jnp.float32), precision=lax.Precision.HIGHEST),
        select.T,
        precision=lax.Precision.HIGHEST,
    )
    seen = (packed > 0.5).astype(jnp.int32)
    return (tile_at, seen)


def pick_entry(vector, index):
    spots = jnp.arange(vector.shape[0], dtype=jnp.int32)
    return jnp.sum(jnp.where(spots == index, vector, 0), axis=0)


def block_scores(query4, keys3, scale_factor, diagonal):
    scores = (
        jnp.einsum("ignd,jgd->gnij", query4, keys3, preferred_element_type=jnp.float32)
        * scale_factor
    )
    rows = query4.shape[0]
    causal = jnp.arange(rows)[:, None] >= jnp.arange(rows)[None, :]
    keep = jnp.logical_or(jnp.logical_not(diagonal), causal)
    return (scores, keep)


def stats_update(state, query4, keys3, scale_factor, diagonal):
    top, total = state
    scores, keep = block_scores(query4, keys3, scale_factor, diagonal)
    scores = jnp.where(keep, scores, NEGATIVE_FILL)
    top_new = jnp.maximum(top, jnp.max(scores, axis=-1))
    probs = jnp.where(keep, jnp.exp(scores - top_new[..., None]), 0.0)
    return (top_new, total * jnp.exp(top - top_new) + jnp.sum(probs, axis=-1))


def block_grads(query4, upstream4, lse, delta, keys3, values3, scale_factor, diagonal):
    scores, keep = block_scores(query4, keys3, scale_factor, diagonal)
    probs = jnp.where(keep, jnp.exp(scores - lse[..., None]), 0.0)
    value_add = jnp.einsum(
        "gnij,ignd->jgd", probs.astype(jnp.bfloat16), upstream4, preferred_element_type=jnp.float32
    )
    dprobs = jnp.einsum("ignd,jgd->gnij", upstream4, values3, preferred_element_type=jnp.float32)
    dscores = (probs * (dprobs - delta[..., None])).astype(jnp.bfloat16)
    query_add = (
        jnp.einsum("gnij,jgd->ignd", dscores, keys3, preferred_element_type=jnp.float32)
        * scale_factor
    )
    key_add = (
        jnp.einsum("gnij,ignd->jgd", dscores, query4, preferred_element_type=jnp.float32)
        * scale_factor
    )
    return (query_add, key_add, value_add)


def on_device(query, key, value, output, output_gradient, parent, owner):
    count = lax.axis_size("ctx")
    me = lax.axis_index("ctx")
    tile = query.shape[1]
    width = key.shape[2]
    heads_kv = width // HEAD_WIDTH
    group = query.shape[2] // width
    scale_factor = HEAD_WIDTH ** (-0.5)
    prompt_tiles = count // 8
    tile_at, seen = tree_tables(parent[0], owner[0])
    my_tile = pick_entry(tile_at, me)
    spots = jnp.arange(count, dtype=jnp.int32)
    seen_row = jnp.sum(jnp.where((spots == me)[:, None], seen, 0), axis=0)
    trained = my_tile >= prompt_tiles
    query4 = query[0].reshape(tile, heads_kv, group, HEAD_WIDTH)
    upstream4 = output_gradient[0].reshape(tile, heads_kv, group, HEAD_WIDTH)
    output4 = output[0].reshape(tile, heads_kv, group, HEAD_WIDTH)
    delta = jnp.sum(upstream4.astype(jnp.float32) * output4.astype(jnp.float32), axis=-1).transpose(
        1, 2, 0
    )
    stats_start = (
        jnp.full((heads_kv, group, tile), NEGATIVE_FILL, jnp.float32),
        jnp.zeros((heads_kv, group, tile), jnp.float32),
    )
    dq_start = jnp.zeros((tile, heads_kv, group, HEAD_WIDTH), jnp.float32)
    kv_pair = jnp.stack([key[0], value[0]])

    def visible(block):
        return jnp.logical_and(trained, pick_entry(seen_row, block) > 0)

    def stats_step(step, state):
        keys_now, top_total = state
        block = (me - step) % count
        top_total = lax.cond(
            visible(block),
            lambda st: stats_update(
                st, query4, keys_now.reshape(tile, heads_kv, HEAD_WIDTH), scale_factor, block == me
            ),
            lambda st: st,
            top_total,
        )
        keys_now = passed_along(keys_now, "ctx", 1)
        return (keys_now, top_total)

    _, (top, total) = lax.fori_loop(0, count, stats_step, (key[0], stats_start))
    lse = top + jnp.log(total)

    def grad_step(step, state):
        pair_now, partial_value, query_gradient = state
        block = (me - step) % count

        def work(inner):
            partial_in, dq_in = inner
            query_add, key_add, value_add = block_grads(
                query4,
                upstream4,
                lse,
                delta,
                pair_now[0].reshape(tile, heads_kv, HEAD_WIDTH),
                pair_now[1].reshape(tile, heads_kv, HEAD_WIDTH),
                scale_factor,
                block == me,
            )
            terms = jnp.stack([key_add.reshape(tile, width), value_add.reshape(tile, width)])
            return (partial_in + terms, dq_in + query_add)

        partial_value, query_gradient = lax.cond(
            visible(block), work, lambda inner: inner, (partial_value, query_gradient)
        )
        pair_now = passed_along(pair_now, "ctx", 1)
        partial_value = passed_along(partial_value, "ctx", 1)
        return (pair_now, partial_value, query_gradient)

    partial_start = jnp.zeros((2, tile, width), jnp.float32)
    _, grads, query_gradient = lax.fori_loop(
        0, count, grad_step, (kv_pair, partial_start, dq_start)
    )
    dq_rows = query_gradient.reshape(tile, heads_kv * group * HEAD_WIDTH)
    total_rows = lax.axis_size("dp") * query.shape[0] * count * tile
    norm = total_rows ** (-0.5)
    sum_q, sum_k, sum_v = lax.psum(
        (jnp.sum(dq_rows, axis=0), jnp.sum(grads[0], axis=0), jnp.sum(grads[1], axis=0)),
        ("ctx", "dp"),
    )
    return (
        dq_rows.astype(jnp.bfloat16)[None],
        grads[0].astype(jnp.bfloat16)[None],
        grads[1].astype(jnp.bfloat16)[None],
        sum_q * norm,
        sum_k * norm,
        sum_v * norm,
    )


def solution(mesh):
    return jax.shard_map(
        on_device,
        mesh=mesh,
        in_specs=(
            P("dp", "ctx", "head"),
            P("dp", "ctx", "head"),
            P("dp", "ctx", "head"),
            P("dp", "ctx", "head"),
            P("dp", "ctx", "head"),
            P("dp", None),
            P("dp", None),
        ),
        out_specs=(
            P("dp", "ctx", "head"),
            P("dp", "ctx", "head"),
            P("dp", "ctx", "head"),
            P("head"),
            P("head"),
            P("head"),
        ),
        check_vma=False,
    )
```

profile of v0, /device:TPU:0, one launch (start us, length us, event | category | flops | bytes accessed | tf_op | source)
XLA Modules:
  0.0 1145.7 jit_solution(1359577302002087889)
XLA Ops:
  1.4 7.5 while.53
  17.1 133.9 %while.51 = (s32[]{:T(128)}, bf16[512,512]{1,0:T(8,128)(2,1)}, f32[4,5,512]{2,1,0:T(8,128)S(1)}, f32[4,5,512]{2,1,0:T(8,128)S(1)}, s32[]{:T(128)}, /*index=5*/s3...) while((s32[]{:T(128)}, bf16[512,512]{1,0:T(8,128)(2,1)}, ...), condition=%wide.region_12.13_spmd, body=%wide.region_6.12_spmd.sunk | while | flops 1384665088 | bytes 50602416 | solution.py:130
  23.2 12.9 %conditional.4 = ((f32[4,5,512]{2,1,0:T(8,128)S(1)}, f32[4,5,512]{2,1,0:T(8,128)S(1)})) conditional(s32[]{:T(128)} %convert_element_type.91, (f32[4,5,512]{2,1,0:T(8,128)S(1)}, f32[4,5,512]{2,1,0:T(8,128)S(1)}) %tuple.112, (s32[]{:T(128)}, s32[]{:T(128)}, bf16[512,512]{1,0:T(8,128)(2,1)}, bf16[512,4,5,128]{3,0,2,1:T(8,128)(2,1)}, ...), branch_computations={%region_8.8_spmd, %region_9.11_spmd} | conditional | flops 1384665088 | bytes 47456292 | solution.py:119
  25.3 5.5 fusion.2
  30.8 5.2 select_reduce_fusion
  40.4 14.8 %collective-permute-done = bf16[512,512]{1,0:T(8,128)(2,1)} collective-permute-done((bf16[512,512]{1,0:T(8,128)(2,1)}, bf16[512,512]{1,0:T(8,128)(2,1)}, u32[]{:S(2)}, u32[]{:S(2)}) %collective-permute-start) | collective-permute-done | bytes 524320 | tf_op jit(solution)/shard_map/while/body/eval_jaxpr/ppermute | solution.py:15
  58.3 13.9 %collective-permute-done = bf16[512,512]{1,0:T(8,128)(2,1)} collective-permute-done((bf16[512,512]{1,0:T(8,128)(2,1)}, bf16[512,512]{1,0:T(8,128)(2,1)}, u32[]{:S(2)}, u32[]{:S(2)}) %collective-permute-start) | collective-permute-done | bytes 524320 | tf_op jit(solution)/shard_map/while/body/eval_jaxpr/ppermute | solution.py:15
  75.4 13.0 %collective-permute-done = bf16[512,512]{1,0:T(8,128)(2,1)} collective-permute-done((bf16[512,512]{1,0:T(8,128)(2,1)}, bf16[512,512]{1,0:T(8,128)(2,1)}, u32[]{:S(2)}, u32[]{:S(2)}) %collective-permute-start) | collective-permute-done | bytes 524320 | tf_op jit(solution)/shard_map/while/body/eval_jaxpr/ppermute | solution.py:15
  91.6 12.0 %collective-permute-done = bf16[512,512]{1,0:T(8,128)(2,1)} collective-permute-done((bf16[512,512]{1,0:T(8,128)(2,1)}, bf16[512,512]{1,0:T(8,128)(2,1)}, u32[]{:S(2)}, u32[]{:S(2)}) %collective-permute-start) | collective-permute-done | bytes 524320 | tf_op jit(solution)/shard_map/while/body/eval_jaxpr/ppermute | solution.py:15
  106.8 12.9 %collective-permute-done = bf16[512,512]{1,0:T(8,128)(2,1)} collective-permute-done((bf16[512,512]{1,0:T(8,128)(2,1)}, bf16[512,512]{1,0:T(8,128)(2,1)}, u32[]{:S(2)}, u32[]{:S(2)}) %collective-permute-start) | collective-permute-done | bytes 524320 | tf_op jit(solution)/shard_map/while/body/eval_jaxpr/ppermute | solution.py:15
  122.9 12.0 %collective-permute-done = bf16[512,512]{1,0:T(8,128)(2,1)} collective-permute-done((bf16[512,512]{1,0:T(8,128)(2,1)}, bf16[512,512]{1,0:T(8,128)(2,1)}, u32[]{:S(2)}, u32[]{:S(2)}) %collective-permute-start) | collective-permute-done | bytes 524320 | tf_op jit(solution)/shard_map/while/body/eval_jaxpr/ppermute | solution.py:15
  138.1 12.9 %conditional.4 = ((f32[4,5,512]{2,1,0:T(8,128)S(1)}, f32[4,5,512]{2,1,0:T(8,128)S(1)})) conditional(s32[]{:T(128)} %convert_element_type.91, (f32[4,5,512]{2,1,0:T(8,128)S(1)}, f32[4,5,512]{2,1,0:T(8,128)S(1)}) %tuple.112, (s32[]{:T(128)}, s32[]{:T(128)}, bf16[512,512]{1,0:T(8,128)(2,1)}, bf16[512,4,5,128]{3,0,2,1:T(8,128)(2,1)}, ...), branch_computations={%region_8.8_spmd, %region_9.11_spmd} | conditional | flops 1384665088 | bytes 47456292 | solution.py:119
  140.2 5.5 fusion.2
  145.7 5.2 select_reduce_fusion
  173.5 830.0 %while.52 = (s32[]{:T(128)}, bf16[2,512,512]{1,2,0:T(8,128)(2,1)}, f32[2,512,512]{1,2,0:T(8,128)}, f32[512,4,5,128]{3,0,2,1:T(8,128)}, s32[]{:T(128)}, /*index=5...) while((s32[]{:T(128)}, bf16[2,512,512]{1,2,0:T(8,128)(2,1)}, ...), condition=%wide.region_18.19_spmd, body=%wide.region_14.18_spmd.sunk | while | flops 6767771648 | bytes 163963472 | solution.py:160
  177.0 55.2 %conditional.5 = ((f32[2,512,512]{1,2,0:T(8,128)}, f32[512,4,5,128]{3,0,2,1:T(8,128)})) conditional(s32[]{:T(128)} %convert_element_type.92, (f32[2,512,512]{1,2,0:T(8,128)}, f32[512,4,5,128]{3,0,2,1:T(8,128)}) %tuple.115, (s32[]{:T(128)}, s32[]{:T(128)}, bf16[2,512,512]{1,2,0:T(8,128)(2,1)}, bf16[512,4,5,128]{0,3,2,1:T(8,128)(2,1)S(1)}, ...), branch_computations={%region_16.16_spmd, %region_17.17_spmd} | conditional | flops 6767771648 | bytes 145088608 | solution.py:152
  179.1 8.5 fusion.31
  187.7 13.5 %fusion.8 = bf16[4,5,512,512]{2,3,1,0:T(8,128)(2,1)} fusion(f32[4,512,512,5]{2,1,3,0:T(8,128)} %fusion.31, f32[4,5,512]{2,1,0:T(8,128)S(1)} %get-tuple-element.544, f32[4,5,512]{2,1,0:T(8,128)S(1)} %get-tuple-element.542, pred[512,512]{0,1:T(8,128)(4,1)S(1)} %fusion.16, bf16[512,4,128,1]{0,2,3,1:T(8,128)(2,1)} %bitcast.81, ...), kind=kOutput, calls=%fused_computation.13 | convolution fusion | flops 1373634560 | bytes 34947072 | tf_op jit(solution)/shard_map/while/body/eval_jaxpr/cond/branch_1_fun/ignd,jgd->gnij/dot_general | solution.py:73
  201.2 7.4 fusion.15
  208.7 10.1 fusion.12
  220.7 11.5 %bitcast_add_fusion = f32[512,4,5,128]{3,0,2,1:T(8,128)} fusion(f32[512,4,5,128]{3,0,2,1:T(8,128)} %get-tuple-element.545, bf16[4,5,512,512]{2,3,1,0:T(8,128)(2,1)} %fusion.8, bf16[512,4,128,1]{0,2,3,1:T(8,128)(2,1)S(1)} %bitcast.76), kind=kOutput, calls=%fused_computation.20 | convolution fusion | flops 1344798720 | bytes 21495808 | tf_op jit(solution)/shard_map/while/body/eval_jaxpr/cond/branch_1_fun/gnij,jgd->ignd/dot_general | solution.py:76
  232.2 51.6 %collective-permute-done.2 = f32[2,512,512]{1,2,0:T(8,128)} collective-permute-done((f32[2,512,512]{1,2,0:T(8,128)}, f32[2,512,512]{1,2,0:T(8,128)}, u32[]{:S(2)}, u32[]{:S(2)}) %collective-permute-start.2) | collective-permute-done | bytes 2097184 | tf_op jit(solution)/shard_map/while/body/eval_jaxpr/ppermute | solution.py:15
  286.9 14.8 %collective-permute-done.1 = bf16[2,512,512]{1,2,0:T(8,128)(2,1)} collective-permute-done((bf16[2,512,512]{1,2,0:T(8,128)(2,1)}, bf16[2,512,512]{1,2,0:T(8,128)(2,1)}, u32[]{:S(2)}, u32[]{:S(2)}) %collective-permute-start.1) | collective-permute-done | bytes 1048608 | tf_op jit(solution)/shard_map/while/body/eval_jaxpr/ppermute | solution.py:15
  305.3 54.3 %collective-permute-start.1 = (bf16[2,512,512]{1,2,0:T(8,128)(2,1)}, bf16[2,512,512]{1,2,0:T(8,128)(2,1)}, u32[]{:S(2)}, u32[]{:S(2)}) collective-permute-start(bf16[2,512,512]{1,2,0:T(8,128)(2,1)} %copy.102), channel_id=1, source_target_pairs={{28,0},{0,4},{4,8},{8,12},{12,16},{16,20},{20,24},{24,28},{29,1},{... | collective-permute-start | bytes 3145736 | tf_op jit(solution)/shard_map/while/body/eval_jaxpr/ppermute | solution.py:15
  362.8 20.8 %collective-permute-done.1 = bf16[2,512,512]{1,2,0:T(8,128)(2,1)} collective-permute-done((bf16[2,512,512]{1,2,0:T(8,128)(2,1)}, bf16[2,512,512]{1,2,0:T(8,128)(2,1)}, u32[]{:S(2)}, u32[]{:S(2)}) %collective-permute-start.1) | collective-permute-done | bytes 1048608 | tf_op jit(solution)/shard_map/while/body/eval_jaxpr/ppermute | solution.py:15
  387.2 39.5 %collective-permute-start.2 = (f32[2,512,512]{1,2,0:T(8,128)}, f32[2,512,512]{1,2,0:T(8,128)}, u32[]{:S(2)}, u32[]{:S(2)}) collective-permute-start(f32[2,512,512]{1,2,0:T(8,128)} %get-tuple-element.817), channel_id=1, source_target_pairs={{28,0},{0,4},{4,8},{8,12},{12,16},{16,20},{20,24},{24,28},{29,1},{... | collective-permute-start | bytes 6291464 | tf_op jit(solution)/shard_map/while/body/eval_jaxpr/ppermute | solution.py:15
  430.0 36.6 %collective-permute-done.2 = f32[2,512,512]{1,2,0:T(8,128)} collective-permute-done((f32[2,512,512]{1,2,0:T(8,128)}, f32[2,512,512]{1,2,0:T(8,128)}, u32[]{:S(2)}, u32[]{:S(2)}) %collective-permute-start.2) | collective-permute-done | bytes 2097184 | tf_op jit(solution)/shard_map/while/body/eval_jaxpr/ppermute | solution.py:15
  469.7 8.1 collective-permute-done.1
  481.4 20.7 %collective-permute-start.2 = (f32[2,512,512]{1,2,0:T(8,128)}, f32[2,512,512]{1,2,0:T(8,128)}, u32[]{:S(2)}, u32[]{:S(2)}) collective-permute-start(f32[2,512,512]{1,2,0:T(8,128)} %get-tuple-element.817), channel_id=1, source_target_pairs={{28,0},{0,4},{4,8},{8,12},{12,16},{16,20},{20,24},{24,28},{29,1},{... | collective-permute-start | bytes 6291464 | tf_op jit(solution)/shard_map/while/body/eval_jaxpr/ppermute | solution.py:15
  502.1 44.7 %collective-permute-start.1 = (bf16[2,512,512]{1,2,0:T(8,128)(2,1)}, bf16[2,512,512]{1,2,0:T(8,128)(2,1)}, u32[]{:S(2)}, u32[]{:S(2)}) collective-permute-start(bf16[2,512,512]{1,2,0:T(8,128)(2,1)} %copy.102), channel_id=1, source_target_pairs={{28,0},{0,4},{4,8},{8,12},{12,16},{16,20},{20,24},{24,28},{29,1},{... | collective-permute-start | bytes 3145736 | tf_op jit(solution)/shard_map/while/body/eval_jaxpr/ppermute | solution.py:15
  549.8 9.5 collective-permute-done.1
  562.9 22.5 %collective-permute-start.2 = (f32[2,512,512]{1,2,0:T(8,128)}, f32[2,512,512]{1,2,0:T(8,128)}, u32[]{:S(2)}, u32[]{:S(2)}) collective-permute-start(f32[2,512,512]{1,2,0:T(8,128)} %get-tuple-element.817), channel_id=1, source_target_pairs={{28,0},{0,4},{4,8},{8,12},{12,16},{16,20},{20,24},{24,28},{29,1},{... | collective-permute-start | bytes 6291464 | tf_op jit(solution)/shard_map/while/body/eval_jaxpr/ppermute | solution.py:15
  590.1 41.7 %collective-permute-done.2 = f32[2,512,512]{1,2,0:T(8,128)} collective-permute-done((f32[2,512,512]{1,2,0:T(8,128)}, f32[2,512,512]{1,2,0:T(8,128)}, u32[]{:S(2)}, u32[]{:S(2)}) %collective-permute-start.2) | collective-permute-done | bytes 2097184 | tf_op jit(solution)/shard_map/while/body/eval_jaxpr/ppermute | solution.py:15
  635.0 14.7 %collective-permute-done.1 = bf16[2,512,512]{1,2,0:T(8,128)(2,1)} collective-permute-done((bf16[2,512,512]{1,2,0:T(8,128)(2,1)}, bf16[2,512,512]{1,2,0:T(8,128)(2,1)}, u32[]{:S(2)}, u32[]{:S(2)}) %collective-permute-start.1) | collective-permute-done | bytes 1048608 | tf_op jit(solution)/shard_map/while/body/eval_jaxpr/ppermute | solution.py:15
  655.8 79.4 %collective-permute-start.1 = (bf16[2,512,512]{1,2,0:T(8,128)(2,1)}, bf16[2,512,512]{1,2,0:T(8,128)(2,1)}, u32[]{:S(2)}, u32[]{:S(2)}) collective-permute-start(bf16[2,512,512]{1,2,0:T(8,128)(2,1)} %copy.102), channel_id=1, source_target_pairs={{28,0},{0,4},{4,8},{8,12},{12,16},{16,20},{20,24},{24,28},{29,1},{... | collective-permute-start | bytes 3145736 | tf_op jit(solution)/shard_map/while/body/eval_jaxpr/ppermute | solution.py:15
  738.3 20.8 %collective-permute-done.1 = bf16[2,512,512]{1,2,0:T(8,128)(2,1)} collective-permute-done((bf16[2,512,512]{1,2,0:T(8,128)(2,1)}, bf16[2,512,512]{1,2,0:T(8,128)(2,1)}, u32[]{:S(2)}, u32[]{:S(2)}) %collective-permute-start.1) | collective-permute-done | bytes 1048608 | tf_op jit(solution)/shard_map/while/body/eval_jaxpr/ppermute | solution.py:15
  762.7 37.0 %collective-permute-start.2 = (f32[2,512,512]{1,2,0:T(8,128)}, f32[2,512,512]{1,2,0:T(8,128)}, u32[]{:S(2)}, u32[]{:S(2)}) collective-permute-start(f32[2,512,512]{1,2,0:T(8,128)} %get-tuple-element.817), channel_id=1, source_target_pairs={{28,0},{0,4},{4,8},{8,12},{12,16},{16,20},{20,24},{24,28},{29,1},{... | collective-permute-start | bytes 6291464 | tf_op jit(solution)/shard_map/while/body/eval_jaxpr/ppermute | solution.py:15
  803.1 90.2 %collective-permute-done.2 = f32[2,512,512]{1,2,0:T(8,128)} collective-permute-done((f32[2,512,512]{1,2,0:T(8,128)}, f32[2,512,512]{1,2,0:T(8,128)}, u32[]{:S(2)}, u32[]{:S(2)}) %collective-permute-start.2) | collective-permute-done | bytes 2097184 | tf_op jit(solution)/shard_map/while/body/eval_jaxpr/ppermute | solution.py:15
  896.4 8.1 collective-permute-done.1
  908.0 55.2 %conditional.5 = ((f32[2,512,512]{1,2,0:T(8,128)}, f32[512,4,5,128]{3,0,2,1:T(8,128)})) conditional(s32[]{:T(128)} %convert_element_type.92, (f32[2,512,512]{1,2,0:T(8,128)}, f32[512,4,5,128]{3,0,2,1:T(8,128)}) %tuple.115, (s32[]{:T(128)}, s32[]{:T(128)}, bf16[2,512,512]{1,2,0:T(8,128)(2,1)}, bf16[512,4,5,128]{0,3,2,1:T(8,128)(2,1)S(1)}, ...), branch_computations={%region_16.16_spmd, %region_17.17_spmd} | conditional | flops 6767771648 | bytes 145088608 | solution.py:152
  910.1 8.5 fusion.31
  918.7 13.5 %fusion.8 = bf16[4,5,512,512]{2,3,1,0:T(8,128)(2,1)} fusion(f32[4,512,512,5]{2,1,3,0:T(8,128)} %fusion.31, f32[4,5,512]{2,1,0:T(8,128)S(1)} %get-tuple-element.544, f32[4,5,512]{2,1,0:T(8,128)S(1)} %get-tuple-element.542, pred[512,512]{0,1:T(8,128)(4,1)S(1)} %fusion.16, bf16[512,4,128,1]{0,2,3,1:T(8,128)(2,1)} %bitcast.81, ...), kind=kOutput, calls=%fused_computation.13 | convolution fusion | flops 1373634560 | bytes 34947072 | tf_op jit(solution)/shard_map/while/body/eval_jaxpr/cond/branch_1_fun/ignd,jgd->gnij/dot_general | solution.py:73
  932.2 7.4 fusion.15
  939.6 10.1 fusion.12
  951.7 11.5 %bitcast_add_fusion = f32[512,4,5,128]{3,0,2,1:T(8,128)} fusion(f32[512,4,5,128]{3,0,2,1:T(8,128)} %get-tuple-element.545, bf16[4,5,512,512]{2,3,1,0:T(8,128)(2,1)} %fusion.8, bf16[512,4,128,1]{0,2,3,1:T(8,128)(2,1)S(1)} %bitcast.76), kind=kOutput, calls=%fused_computation.20 | convolution fusion | flops 1344798720 | bytes 21495808 | tf_op jit(solution)/shard_map/while/body/eval_jaxpr/cond/branch_1_fun/gnij,jgd->ignd/dot_general | solution.py:76
  963.2 29.0 %collective-permute-done.2 = f32[2,512,512]{1,2,0:T(8,128)} collective-permute-done((f32[2,512,512]{1,2,0:T(8,128)}, f32[2,512,512]{1,2,0:T(8,128)}, u32[]{:S(2)}, u32[]{:S(2)}) %collective-permute-start.2) | collective-permute-done | bytes 2097184 | tf_op jit(solution)/shard_map/while/body/eval_jaxpr/ppermute | solution.py:15
  995.4 8.1 collective-permute-done.1
  1008.3 128.7 %all-reduce = (f32[2560]{0:T(1024)S(1)}, f32[512]{0:T(512)S(1)}, f32[512]{0:T(512)S(1)}) all-reduce(f32[2560]{0:T(1024)S(1)} %reduce_sum.120, f32[512]{0:T(512)S(1)} %get-tuple-element.616, f32[512]{0:T(512)S(1)} %get-tuple-element.615), channel_id=1, replica_groups=mesh['ctx'=8,'head'=2,'dp'=2] {'ctx','dp'}, use_global_device_ids=true, to_apply=%region_20.21 | all-reduce | flops 3584 | bytes 28672 | tf_op jit(solution)/shard_map/psum | solution.py:166
  (156 shorter events, 150.2 us)
Async XLA Ops:
  10.6 5.6 copy-start.2
  19.0 18.2 %collective-permute-start = (bf16[512,512]{1,0:T(8,128)(2,1)}, bf16[512,512]{1,0:T(8,128)(2,1)}, u32[]{:S(2)}, u32[]{:S(2)}) collective-permute-start(bf16[512,512]{1,0:T(8,128)(2,1)} %copy.90), channel_id=1, source_target_pairs={{28,0},{0,4},{4,8},{8,12},{12,16},{16,20},{20,24},{24,28},{29,1},{... | collective-permute-start | bytes 1572872 | tf_op jit(solution)/shard_map/while/body/eval_jaxpr/ppermute | solution.py:15
  39.0 16.1 %collective-permute-start = (bf16[512,512]{1,0:T(8,128)(2,1)}, bf16[512,512]{1,0:T(8,128)(2,1)}, u32[]{:S(2)}, u32[]{:S(2)}) collective-permute-start(bf16[512,512]{1,0:T(8,128)(2,1)} %copy.90), channel_id=1, source_target_pairs={{28,0},{0,4},{4,8},{8,12},{12,16},{16,20},{20,24},{24,28},{29,1},{... | collective-permute-start | bytes 1572872 | tf_op jit(solution)/shard_map/while/body/eval_jaxpr/ppermute | solution.py:15
  57.0 15.2 %collective-permute-start = (bf16[512,512]{1,0:T(8,128)(2,1)}, bf16[512,512]{1,0:T(8,128)(2,1)}, u32[]{:S(2)}, u32[]{:S(2)}) collective-permute-start(bf16[512,512]{1,0:T(8,128)(2,1)} %copy.90), channel_id=1, source_target_pairs={{28,0},{0,4},{4,8},{8,12},{12,16},{16,20},{20,24},{24,28},{29,1},{... | collective-permute-start | bytes 1572872 | tf_op jit(solution)/shard_map/while/body/eval_jaxpr/ppermute | solution.py:15
  74.1 14.3 %collective-permute-start = (bf16[512,512]{1,0:T(8,128)(2,1)}, bf16[512,512]{1,0:T(8,128)(2,1)}, u32[]{:S(2)}, u32[]{:S(2)}) collective-permute-start(bf16[512,512]{1,0:T(8,128)(2,1)} %copy.90), channel_id=1, source_target_pairs={{28,0},{0,4},{4,8},{8,12},{12,16},{16,20},{20,24},{24,28},{29,1},{... | collective-permute-start | bytes 1572872 | tf_op jit(solution)/shard_map/while/body/eval_jaxpr/ppermute | solution.py:15
  90.3 13.4 %collective-permute-start = (bf16[512,512]{1,0:T(8,128)(2,1)}, bf16[512,512]{1,0:T(8,128)(2,1)}, u32[]{:S(2)}, u32[]{:S(2)}) collective-permute-start(bf16[512,512]{1,0:T(8,128)(2,1)} %copy.90), channel_id=1, source_target_pairs={{28,0},{0,4},{4,8},{8,12},{12,16},{16,20},{20,24},{24,28},{29,1},{... | collective-permute-start | bytes 1572872 | tf_op jit(solution)/shard_map/while/body/eval_jaxpr/ppermute | solution.py:15
  105.5 14.2 %collective-permute-start = (bf16[512,512]{1,0:T(8,128)(2,1)}, bf16[512,512]{1,0:T(8,128)(2,1)}, u32[]{:S(2)}, u32[]{:S(2)}) collective-permute-start(bf16[512,512]{1,0:T(8,128)(2,1)} %copy.90), channel_id=1, source_target_pairs={{28,0},{0,4},{4,8},{8,12},{12,16},{16,20},{20,24},{24,28},{29,1},{... | collective-permute-start | bytes 1572872 | tf_op jit(solution)/shard_map/while/body/eval_jaxpr/ppermute | solution.py:15
  121.6 13.3 %collective-permute-start = (bf16[512,512]{1,0:T(8,128)(2,1)}, bf16[512,512]{1,0:T(8,128)(2,1)}, u32[]{:S(2)}, u32[]{:S(2)}) collective-permute-start(bf16[512,512]{1,0:T(8,128)(2,1)} %copy.90), channel_id=1, source_target_pairs={{28,0},{0,4},{4,8},{8,12},{12,16},{16,20},{20,24},{24,28},{29,1},{... | collective-permute-start | bytes 1572872 | tf_op jit(solution)/shard_map/while/body/eval_jaxpr/ppermute | solution.py:15
  136.8 14.2 %collective-permute-start = (bf16[512,512]{1,0:T(8,128)(2,1)}, bf16[512,512]{1,0:T(8,128)(2,1)}, u32[]{:S(2)}, u32[]{:S(2)}) collective-permute-start(bf16[512,512]{1,0:T(8,128)(2,1)} %copy.90), channel_id=1, source_target_pairs={{28,0},{0,4},{4,8},{8,12},{12,16},{16,20},{20,24},{24,28},{29,1},{... | collective-permute-start | bytes 1572872 | tf_op jit(solution)/shard_map/while/body/eval_jaxpr/ppermute | solution.py:15
  160.3 4.3 copy-start.3
  208.7 10.1 copy-start
  219.3 1.4 copy-start.1
  232.2 51.6 %collective-permute-start.2 = (f32[2,512,512]{1,2,0:T(8,128)}, f32[2,512,512]{1,2,0:T(8,128)}, u32[]{:S(2)}, u32[]{:S(2)}) collective-permute-start(f32[2,512,512]{1,2,0:T(8,128)} %get-tuple-element.817), channel_id=1, source_target_pairs={{28,0},{0,4},{4,8},{8,12},{12,16},{16,20},{20,24},{24,28},{29,1},{... | collective-permute-start | bytes 6291464 | tf_op jit(solution)/shard_map/while/body/eval_jaxpr/ppermute | solution.py:15
  232.2 69.5 %collective-permute-start.1 = (bf16[2,512,512]{1,2,0:T(8,128)(2,1)}, bf16[2,512,512]{1,2,0:T(8,128)(2,1)}, u32[]{:S(2)}, u32[]{:S(2)}) collective-permute-start(bf16[2,512,512]{1,2,0:T(8,128)(2,1)} %copy.102), channel_id=1, source_target_pairs={{28,0},{0,4},{4,8},{8,12},{12,16},{16,20},{20,24},{24,28},{29,1},{... | collective-permute-start | bytes 3145736 | tf_op jit(solution)/shard_map/while/body/eval_jaxpr/ppermute | solution.py:15
  305.3 54.4 %collective-permute-start.2 = (f32[2,512,512]{1,2,0:T(8,128)}, f32[2,512,512]{1,2,0:T(8,128)}, u32[]{:S(2)}, u32[]{:S(2)}) collective-permute-start(f32[2,512,512]{1,2,0:T(8,128)} %get-tuple-element.817), channel_id=1, source_target_pairs={{28,0},{0,4},{4,8},{8,12},{12,16},{16,20},{20,24},{24,28},{29,1},{... | collective-permute-start | bytes 6291464 | tf_op jit(solution)/shard_map/while/body/eval_jaxpr/ppermute | solution.py:15
  305.3 78.3 %collective-permute-start.1 = (bf16[2,512,512]{1,2,0:T(8,128)(2,1)}, bf16[2,512,512]{1,2,0:T(8,128)(2,1)}, u32[]{:S(2)}, u32[]{:S(2)}) collective-permute-start(bf16[2,512,512]{1,2,0:T(8,128)(2,1)} %copy.102), channel_id=1, source_target_pairs={{28,0},{0,4},{4,8},{8,12},{12,16},{16,20},{20,24},{24,28},{29,1},{... | collective-permute-start | bytes 3145736 | tf_op jit(solution)/shard_map/while/body/eval_jaxpr/ppermute | solution.py:15
  387.2 79.4 %collective-permute-start.2 = (f32[2,512,512]{1,2,0:T(8,128)}, f32[2,512,512]{1,2,0:T(8,128)}, u32[]{:S(2)}, u32[]{:S(2)}) collective-permute-start(f32[2,512,512]{1,2,0:T(8,128)} %get-tuple-element.817), channel_id=1, source_target_pairs={{28,0},{0,4},{4,8},{8,12},{12,16},{16,20},{20,24},{24,28},{29,1},{... | collective-permute-start | bytes 6291464 | tf_op jit(solution)/shard_map/while/body/eval_jaxpr/ppermute | solution.py:15
  426.6 51.2 %collective-permute-start.1 = (bf16[2,512,512]{1,2,0:T(8,128)(2,1)}, bf16[2,512,512]{1,2,0:T(8,128)(2,1)}, u32[]{:S(2)}, u32[]{:S(2)}) collective-permute-start(bf16[2,512,512]{1,2,0:T(8,128)(2,1)} %copy.102), channel_id=1, source_target_pairs={{28,0},{0,4},{4,8},{8,12},{12,16},{16,20},{20,24},{24,28},{29,1},{... | collective-permute-start | bytes 3145736 | tf_op jit(solution)/shard_map/while/body/eval_jaxpr/ppermute | solution.py:15
  481.4 65.3 %collective-permute-start.2 = (f32[2,512,512]{1,2,0:T(8,128)}, f32[2,512,512]{1,2,0:T(8,128)}, u32[]{:S(2)}, u32[]{:S(2)}) collective-permute-start(f32[2,512,512]{1,2,0:T(8,128)} %get-tuple-element.817), channel_id=1, source_target_pairs={{28,0},{0,4},{4,8},{8,12},{12,16},{16,20},{20,24},{24,28},{29,1},{... | collective-permute-start | bytes 6291464 | tf_op jit(solution)/shard_map/while/body/eval_jaxpr/ppermute | solution.py:15
  502.1 57.3 %collective-permute-start.1 = (bf16[2,512,512]{1,2,0:T(8,128)(2,1)}, bf16[2,512,512]{1,2,0:T(8,128)(2,1)}, u32[]{:S(2)}, u32[]{:S(2)}) collective-permute-start(bf16[2,512,512]{1,2,0:T(8,128)(2,1)} %copy.102), channel_id=1, source_target_pairs={{28,0},{0,4},{4,8},{8,12},{12,16},{16,20},{20,24},{24,28},{29,1},{... | collective-permute-start | bytes 3145736 | tf_op jit(solution)/shard_map/while/body/eval_jaxpr/ppermute | solution.py:15
  562.9 68.9 %collective-permute-start.2 = (f32[2,512,512]{1,2,0:T(8,128)}, f32[2,512,512]{1,2,0:T(8,128)}, u32[]{:S(2)}, u32[]{:S(2)}) collective-permute-start(f32[2,512,512]{1,2,0:T(8,128)} %get-tuple-element.817), channel_id=1, source_target_pairs={{28,0},{0,4},{4,8},{8,12},{12,16},{16,20},{20,24},{24,28},{29,1},{... | collective-permute-start | bytes 6291464 | tf_op jit(solution)/shard_map/while/body/eval_jaxpr/ppermute | solution.py:15
  585.4 64.3 %collective-permute-start.1 = (bf16[2,512,512]{1,2,0:T(8,128)(2,1)}, bf16[2,512,512]{1,2,0:T(8,128)(2,1)}, u32[]{:S(2)}, u32[]{:S(2)}) collective-permute-start(bf16[2,512,512]{1,2,0:T(8,128)(2,1)} %copy.102), channel_id=1, source_target_pairs={{28,0},{0,4},{4,8},{8,12},{12,16},{16,20},{20,24},{24,28},{29,1},{... | collective-permute-start | bytes 3145736 | tf_op jit(solution)/shard_map/while/body/eval_jaxpr/ppermute | solution.py:15
  653.3 81.9 %collective-permute-start.2 = (f32[2,512,512]{1,2,0:T(8,128)}, f32[2,512,512]{1,2,0:T(8,128)}, u32[]{:S(2)}, u32[]{:S(2)}) collective-permute-start(f32[2,512,512]{1,2,0:T(8,128)} %get-tuple-element.817), channel_id=1, source_target_pairs={{28,0},{0,4},{4,8},{8,12},{12,16},{16,20},{20,24},{24,28},{29,1},{... | collective-permute-start | bytes 6291464 | tf_op jit(solution)/shard_map/while/body/eval_jaxpr/ppermute | solution.py:15
  655.8 103.3 %collective-permute-start.1 = (bf16[2,512,512]{1,2,0:T(8,128)(2,1)}, bf16[2,512,512]{1,2,0:T(8,128)(2,1)}, u32[]{:S(2)}, u32[]{:S(2)}) collective-permute-start(bf16[2,512,512]{1,2,0:T(8,128)(2,1)} %copy.102), channel_id=1, source_target_pairs={{28,0},{0,4},{4,8},{8,12},{12,16},{16,20},{20,24},{24,28},{29,1},{... | collective-permute-start | bytes 3145736 | tf_op jit(solution)/shard_map/while/body/eval_jaxpr/ppermute | solution.py:15
  762.7 130.6 %collective-permute-start.2 = (f32[2,512,512]{1,2,0:T(8,128)}, f32[2,512,512]{1,2,0:T(8,128)}, u32[]{:S(2)}, u32[]{:S(2)}) collective-permute-start(f32[2,512,512]{1,2,0:T(8,128)} %get-tuple-element.817), channel_id=1, source_target_pairs={{28,0},{0,4},{4,8},{8,12},{12,16},{16,20},{20,24},{24,28},{29,1},{... | collective-permute-start | bytes 6291464 | tf_op jit(solution)/shard_map/while/body/eval_jaxpr/ppermute | solution.py:15
  799.7 104.8 %collective-permute-start.1 = (bf16[2,512,512]{1,2,0:T(8,128)(2,1)}, bf16[2,512,512]{1,2,0:T(8,128)(2,1)}, u32[]{:S(2)}, u32[]{:S(2)}) collective-permute-start(bf16[2,512,512]{1,2,0:T(8,128)(2,1)} %copy.102), channel_id=1, source_target_pairs={{28,0},{0,4},{4,8},{8,12},{12,16},{16,20},{20,24},{24,28},{29,1},{... | collective-permute-start | bytes 3145736 | tf_op jit(solution)/shard_map/while/body/eval_jaxpr/ppermute | solution.py:15
  939.6 10.1 copy-start
  950.3 1.4 copy-start.1
  963.2 29.0 %collective-permute-start.2 = (f32[2,512,512]{1,2,0:T(8,128)}, f32[2,512,512]{1,2,0:T(8,128)}, u32[]{:S(2)}, u32[]{:S(2)}) collective-permute-start(f32[2,512,512]{1,2,0:T(8,128)} %get-tuple-element.817), channel_id=1, source_target_pairs={{28,0},{0,4},{4,8},{8,12},{12,16},{16,20},{20,24},{24,28},{29,1},{... | collective-permute-start | bytes 6291464 | tf_op jit(solution)/shard_map/while/body/eval_jaxpr/ppermute | solution.py:15
  963.2 40.3 %collective-permute-start.1 = (bf16[2,512,512]{1,2,0:T(8,128)(2,1)}, bf16[2,512,512]{1,2,0:T(8,128)(2,1)}, u32[]{:S(2)}, u32[]{:S(2)}) collective-permute-start(bf16[2,512,512]{1,2,0:T(8,128)(2,1)} %copy.102), channel_id=1, source_target_pairs={{28,0},{0,4},{4,8},{8,12},{12,16},{16,20},{20,24},{24,28},{29,1},{... | collective-permute-start | bytes 3145736 | tf_op jit(solution)/shard_map/while/body/eval_jaxpr/ppermute | solution.py:15
where the time goes:
time: 1130 us; the launch traced here: 1150 us
  waiting for transfers between devices  434 us (38%)
  starting transfers between devices  315 us (28%)
  blocking collectives  129 us (11%)
  matrix products  114 us (10%)
  local copies, waits for them, and re-layouts  101 us (9%)
  other arithmetic  41.5 us (4%)
    ppermute x24, waiting for transfers between devices, passed_along(): return lax.ppermute(block, axis, route)  434 us
    ppermute x24, starting transfers between devices, passed_along(): return lax.ppermute(block, axis, route)  315 us
    psum x1, blocking collectives, on_device(): lax.psum((jnp.sum(dq_rows, axis=0), jnp.sum(grads[0], axis=0), jnp.sum(gr...  129 us
    another operation x16, local copies, waits for them, and re-layouts  32.9 us
    dot_general x4, matrix products, block_scores(): jnp.einsum('ignd,jgd->gnij', query4, keys3, preferred_element_type=jnp.fl...  28.1 us
    dot_general x2, matrix products, block_grads(): jnp.einsum('ignd,jgd->gnij', upstream4, values3, preferred_element_type=j...  26.9 us
    while x8, local copies, waits for them, and re-layouts  25 us
    dot_general x2, matrix products, block_grads(): jnp.einsum('gnij,jgd->ignd', dscores, keys3, preferred_element_type=jnp.f...  23 us
  transfers between devices with their start and end apart: 24, of which 20 were waited for; matrix products, arithmetic and copies ran while one was open for 5% of the time, Pallas kernels for 0%

commit v1 on v0

v1 whole, which is shorter than its diff:
```python
import functools

import jax
import jax.numpy as jnp
from jax import lax
from jax.experimental import pallas as pl
from jax.experimental.pallas import tpu as pltpu
from jax.sharding import PartitionSpec as P

HEAD_WIDTH = 128
SCALE = HEAD_WIDTH**-0.5
LOG2E = 1.4426950408889634
NEGATIVE_FILL = -1e30
BY_LAST = (((1,), (1,)), ((), ()))
f32, bf16 = jnp.float32, jnp.bfloat16


def head_grads(parts, group, q_ref, g_ref, o_ref, kv_refs, dq_ref, sums, sq_ref):
    for total in sums:
        total[...] = jnp.zeros_like(total)

    def widen(row, first, fill):
        if not first:
            return row
        return jnp.concatenate([jnp.full((row.shape[0], first), fill, f32), row], axis=1)

    def one_head(h, carry):
        cols = pl.ds(pl.multiple_of(h * HEAD_WIDTH, HEAD_WIDTH), HEAD_WIDTH)
        qh, gh, oh = q_ref[:, cols], g_ref[:, cols], o_ref[:, cols]
        delta = jnp.sum((gh.astype(f32) * oh.astype(f32)).T, axis=0, keepdims=True)
        scores = []
        for b, k0, kn, q0, diagonal in parts:
            s = lax.dot_general(
                kv_refs[b][0, k0 : k0 + kn, :], qh[q0:], BY_LAST, preferred_element_type=f32
            )
            if diagonal:
                rows = k0 + lax.broadcasted_iota(jnp.int32, s.shape, 0)
                across = q0 + lax.broadcasted_iota(jnp.int32, s.shape, 1)
                s = jnp.where(rows <= across, s, NEGATIVE_FILL)
            scores.append(s)
        top = None
        for (b, k0, kn, q0, diagonal), s in zip(parts, scores):
            m = widen(jnp.max(s, axis=0, keepdims=True), q0, NEGATIVE_FILL)
            top = m if top is None else jnp.maximum(top, m)
        top = top * (SCALE * LOG2E)
        exps, total = [], None
        for (b, k0, kn, q0, diagonal), s in zip(parts, scores):
            e = jnp.exp2(s * (SCALE * LOG2E) - top[:, q0:])
            exps.append(e)
            t = widen(jnp.sum(e, axis=0, keepdims=True), q0, 0.0)
            total = t if total is None else total + t
        inverse = 1.0 / total
        dq_t = None
        for (b, k0, kn, q0, diagonal), e in zip(parts, exps):
            keys, values = kv_refs[b][0, k0 : k0 + kn, :], kv_refs[b][1, k0 : k0 + kn, :]
            p = e * inverse[:, q0:]
            dp = lax.dot_general(values, gh[q0:], BY_LAST, preferred_element_type=f32)
            ds = (p * (dp - delta[:, q0:])).astype(bf16)
            sums[b][1, k0 : k0 + kn, :] += jnp.dot(
                p.astype(bf16), gh[q0:], preferred_element_type=f32
            )
            sums[b][0, k0 : k0 + kn, :] += jnp.dot(ds, qh[q0:], preferred_element_type=f32)
            add = widen(jnp.dot(keys.T, ds, preferred_element_type=f32), q0, 0.0)
            dq_t = add if dq_t is None else dq_t + add
        dq = dq_t.T * SCALE
        dq_ref[:, cols] = dq.astype(bf16)
        sq_ref[:, cols] = jnp.sum(dq, axis=0, keepdims=True)
        return carry

    lax.fori_loop(0, group, one_head, 0)


def grads_kernel(
    group, prompts, mode_ref, q_ref, g_ref, o_ref, own, prompt, before,
    dq_ref, own_out, prompt_out, before_out, sq_ref, skv_ref, own_sum, prompt_sum, before_sum,
):
    tile = q_ref.shape[0]
    half = tile // 2
    kv_refs = [own, before] + [prompt.at[i] for i in range(prompts)]
    sums = [own_sum, before_sum] + [prompt_sum.at[i] for i in range(prompts)]
    parts = [(0, 0, half, 0, True), (0, half, half, half, True)]
    parts += [(2 + i, 0, tile, 0, False) for i in range(prompts)]
    mode = mode_ref[0]
    rest = (group, q_ref, g_ref, o_ref, kv_refs, dq_ref, sums, sq_ref)

    @pl.when(mode == 1)
    def _():
        head_grads(parts, *rest)

    @pl.when(mode == 2)
    def _():
        head_grads(parts + [(1, 0, tile, 0, False)], *rest)

    @pl.when(mode == 0)
    def _():
        dq_ref[...] = jnp.zeros_like(dq_ref)
        sq_ref[...] = jnp.zeros_like(sq_ref)
        for total in sums:
            total[...] = jnp.zeros_like(total)

    def put(out, total):
        dk, dv = total[0] * SCALE, total[1]
        out[0] = dk.astype(out.dtype)
        out[1] = dv.astype(out.dtype)
        return jnp.sum(dk, axis=0, keepdims=True), jnp.sum(dv, axis=0, keepdims=True)

    pairs = [put(own_out, own_sum), put(before_out, before_sum)]
    pairs += [put(prompt_out.at[i], prompt_sum.at[i]) for i in range(prompts)]
    skv_ref[0] = functools.reduce(jnp.add, [k for k, _ in pairs])
    skv_ref[1] = functools.reduce(jnp.add, [v for _, v in pairs])


def block_grads(mode, q, g, o, own, prompt, before):
    tile, q_width = q.shape
    width = own.shape[2]
    heads = width // HEAD_WIDTH
    group = q_width // width
    prompts = prompt.shape[0]
    q_spec = pl.BlockSpec((tile, group * HEAD_WIDTH), lambda h, m: (0, h))
    kv_spec = pl.BlockSpec((2, tile, HEAD_WIDTH), lambda h, m: (0, 0, h))
    p_spec = pl.BlockSpec((prompts, 2, tile, HEAD_WIDTH), lambda h, m: (0, 0, 0, h))
    pair = (2, tile, HEAD_WIDTH)
    return pl.pallas_call(
        functools.partial(grads_kernel, group, prompts),
        grid_spec=pltpu.PrefetchScalarGridSpec(
            num_scalar_prefetch=1,
            grid=(heads,),
            in_specs=[q_spec, q_spec, q_spec, kv_spec, p_spec, kv_spec],
            out_specs=[
                q_spec, kv_spec, p_spec, kv_spec,
                pl.BlockSpec((1, group * HEAD_WIDTH), lambda h, m: (0, h)),
                pl.BlockSpec((2, 1, HEAD_WIDTH), lambda h, m: (0, 0, h)),
            ],
            scratch_shapes=[
                pltpu.VMEM(pair, f32), pltpu.VMEM((prompts, *pair), f32), pltpu.VMEM(pair, f32)
            ],
        ),
        out_shape=[
            jax.ShapeDtypeStruct((tile, q_width), bf16),
            jax.ShapeDtypeStruct((2, tile, width), f32),
            jax.ShapeDtypeStruct((prompts, 2, tile, width), bf16),
            jax.ShapeDtypeStruct((2, tile, width), bf16),
            jax.ShapeDtypeStruct((1, q_width), f32),
            jax.ShapeDtypeStruct((2, 1, width), f32),
        ],
        compiler_params=pltpu.CompilerParams(vmem_limit_bytes=50 * 2**20),
    )(mode, q, g, o, own, prompt, before)


def pick(vector, index):
    spots = jnp.arange(vector.shape[0], dtype=jnp.int32)
    return jnp.sum(jnp.where(spots == index, vector, 0), axis=0)


def shared(chunk, count, me):
    routes = [[(i, (i + d) % count) for i in range(count)] for d in range(1, count)]
    arrived = [chunk] + [lax.ppermute(chunk, "ctx", route) for route in routes]
    arrived = jnp.stack(arrived)
    return jnp.take(arrived, (me - jnp.arange(count)) % count, axis=0)


def swapped(array, partner_bits, count):
    def swap(d):
        return lambda a: lax.ppermute(a, "ctx", [(i, i ^ d) for i in range(count)])

    return lax.switch(partner_bits, [lambda a: a] + [swap(d) for d in range(1, count)], array)


def on_device(query, key, value, output, output_gradient, parent, owner):
    count = lax.axis_size("ctx")
    trees = lax.axis_size("dp")
    me = lax.axis_index("ctx")
    tile = query.shape[1]
    width = key.shape[2]
    prompts = count // 8
    chunk_rows = 2 * tile // count
    parent, owner = parent[0], owner[0]
    spots = jnp.arange(count, dtype=jnp.int32)

    my_tile = pick(spots, jnp.argmax(owner == me))
    my_parent = pick(parent, my_tile)
    answers = my_tile >= prompts
    second = jnp.logical_and(answers, my_parent >= prompts)
    child = jnp.sum(jnp.where(parent == my_tile, spots, 0))
    first = jnp.logical_and(answers, child > 0)
    partner = jnp.where(second, pick(owner, my_parent), jnp.where(first, pick(owner, child), me))
    mode = jnp.where(second, 2, jnp.where(answers, 1, 0)).astype(jnp.int32)

    own = jnp.stack([key[0], value[0]])
    chunks = lax.all_to_all(own.reshape(count, chunk_rows, width), "ctx", 0, 0)
    mine = jnp.stack(
        [lax.dynamic_index_in_dim(chunks, owner[t], 0, keepdims=False) for t in range(prompts)]
    )
    prompt = shared(mine, count, me).transpose(1, 0, 2, 3).reshape(prompts, 2, tile, width)
    before = swapped(own, me ^ partner, count)

    dq, own_part, prompt_part, before_part, sum_q, sum_kv = block_grads(
        mode[None], query[0], output_gradient[0], output[0], own, prompt, before
    )

    sums = jnp.concatenate([sum_q.reshape(-1), sum_kv.reshape(-1)])
    devices = count * trees
    d = 1
    while d < devices:
        sums = sums + lax.ppermute(sums, ("ctx", "dp"), [(i, i ^ d) for i in range(devices)])
        d *= 2

    after = swapped(before_part, me ^ partner, count)
    parts = prompt_part.reshape(prompts, count, chunk_rows, width).transpose(1, 0, 2, 3)
    parts = lax.all_to_all(parts, "ctx", 0, 0)
    total = jnp.sum(parts.astype(f32), axis=0).astype(bf16)
    total = shared(total, count, me).transpose(1, 0, 2, 3).reshape(prompts, 2, tile, width)
    total = lax.dynamic_index_in_dim(
        total, jnp.minimum(my_tile, prompts - 1), 0, keepdims=False
    ).astype(f32)
    extra = jnp.where(answers, jnp.where(first, after.astype(f32), 0.0), total)
    grads = (own_part + extra).astype(bf16)

    norm = (trees * count * tile) ** -0.5
    sums = sums * norm
    q_width = query.shape[2]
    return (
        dq[None],
        grads[0][None],
        grads[1][None],
        sums[:q_width],
        sums[q_width : q_width + width],
        sums[q_width + width :],
    )


def solution(mesh):
    rows = P("dp", "ctx", "head")
    return jax.shard_map(
        on_device,
        mesh=mesh,
        in_specs=(rows, rows, rows, rows, rows, P("dp", None), P("dp", None)),
        out_specs=(rows, rows, rows, P("head"), P("head"), P("head")),
        check_vma=False,
    )
```

time: 1130 us -> 244 us (0.22); the launches traced: 1150 us -> 242 us
  waiting for transfers between devices: 434 us -> 117 us
  starting transfers between devices: 315 us -> 57.5 us
  blocking collectives: 129 us -> 0 us
  matrix products: 114 us -> 0 us
  local copies, waits for them, and re-layouts: 101 us -> 15.1 us
  Pallas kernels: 0 us -> 41.9 us
  other arithmetic: 41.5 us -> 6.17 us
    ppermute x24 -> x20, waiting for transfers between devices: 434 us -> 96 us  [the longest x2 47.3 us: swap(): return lambda a: lax.ppermute(a, 'ctx', [(i, i ^ d) for i in range(count)])]
    ppermute x24 -> x20, starting transfers between devices: 315 us -> 26.2 us  [the longest x14 16.3 us: shared(): arrived = [chunk] + [lax.ppermute(chunk, 'ctx', route) for route in routes]]
    psum x1 -> x0, blocking collectives: 129 us -> none  [on_device(): lax.psum((jnp.sum(dq_rows, axis=0), jnp.sum(grads[0], axis=0), jnp.sum(gr...]
    dot_general x14 -> x0, matrix products: 114 us -> none  [the longest x4 28.1 us: block_scores(): jnp.einsum('ignd,jgd->gnij', query4, keys3, preferred_element_type=jnp.fl...]
    pallas_call x0 -> x1, Pallas kernels: none -> 41.9 us  [block_grads(): pl.pallas_call(functools.partial(grads_kernel, group, prompts), grid_spec...]
    while x11 -> x0, local copies, waits for them, and re-layouts: 33.1 us -> none
    all_to_all x0 -> x2, starting transfers between devices: none -> 31.3 us  [the longest x1 24.1 us: on_device(): parts = lax.all_to_all(parts, 'ctx', 0, 0)]
    reduce_sum x31 -> x4, other arithmetic: 35.8 us -> 4.63 us  [the longest x2 3.2 us: pick(): return jnp.sum(jnp.where(spots == index, vector, 0), axis=0)]
  transfers between devices with their start and end apart: 24 -> 22, of which waited for: 20 -> 12; matrix products, arithmetic and copies ran while one was open for 5% -> 5% of each run, Pallas kernels for 0% -> 0%
where the time goes in v1:
time: 244 us; the launch traced here: 242 us
  waiting for transfers between devices  117 us (48%)
  starting transfers between devices  57.5 us (24%)
  Pallas kernels  41.9 us (17%)
  local copies, waits for them, and re-layouts  15.1 us (6%)
  other arithmetic  6.17 us (3%)
  between operations  4.24 us (2%)
    ppermute x2, waiting for transfers between devices, swap(): return lambda a: lax.ppermute(a, 'ctx', [(i, i ^ d) for i in range(count)])  47.3 us
    pallas_call x1, Pallas kernels, block_grads(): pl.pallas_call(functools.partial(grads_kernel, group, prompts), grid_spec...  41.9 us
    ppermute x14, waiting for transfers between devices, shared(): arrived = [chunk] + [lax.ppermute(chunk, 'ctx', route) for route in routes]  36.1 us
    all_to_all x1, starting transfers between devices, on_device(): parts = lax.all_to_all(parts, 'ctx', 0, 0)  24.1 us
    all_to_all x1, waiting for transfers between devices, on_device(): chunks = lax.all_to_all(own.reshape(count, chunk_rows, width), 'ctx', 0, 0)  20.5 us
    ppermute x14, starting transfers between devices, shared(): arrived = [chunk] + [lax.ppermute(chunk, 'ctx', route) for route in routes]  16.3 us
    ppermute x4, waiting for transfers between devices, on_device(): lax.ppermute(sums, ('ctx', 'dp'), [(i, i ^ d) for i in range(devices)])  12.6 us
    ppermute x4, starting transfers between devices, on_device(): lax.ppermute(sums, ('ctx', 'dp'), [(i, i ^ d) for i in range(devices)])  8.26 us
  transfers between devices with their start and end apart: 22, of which 12 were waited for; matrix products, arithmetic and copies ran while one was open for 5% of the time, Pallas kernels for 0%

profile of v1, /device:TPU:0, one launch (start us, length us, event | category | flops | bytes accessed | tf_op | source)
XLA Modules:
  0.0 241.5 jit_solution(12501448919095105086)
XLA Ops:
  0.7 1.9 constant_dynamic-update-slice_fusion.1
  2.6 1.9 constant_dynamic-update-slice_fusion.own
  4.4 7.3 %all-to-all-start = ((bf16[8,128,512]{2,1,0:T(8,128)(2,1)}), bf16[8,128,512]{2,1,0:T(8,128)(2,1)S(1)}, u32[]{:S(2)}, u32[]{:S(2)}) async-start(bf16[8,128,512]{2,1,0:T(8,128)(2,1)} %bitcast.6), calls=%async_computation | async-start | bytes 2097152 | tf_op jit(solution)/shard_map/all_to_all | solution.py:190
  11.8 0.7 compare_reduce_fusion
  12.5 1.3 fusion.2
  13.8 1.3 fusion.5
  15.0 1.9 fusion.6
  17.0 20.5 %all-to-all-done = bf16[8,128,512]{2,1,0:T(8,128)(2,1)S(1)} async-done(((bf16[8,128,512]{2,1,0:T(8,128)(2,1)}), bf16[8,128,512]{2,1,0:T(8,128)(2,1)S(1)}, u32[]{:S(2)}, u32[]{:S(2)}) %all-to-all-start) | async-done | bytes 1048608 | tf_op jit(solution)/shard_map/all_to_all | solution.py:190
  37.5 1.5 collective-permute-start.14
  42.2 23.0 %conditional.2 = (bf16[2,512,512]{2,1,0:T(8,128)(2,1)}) conditional(s32[]{:T(128)} %clamp.4, bf16[2,512,512]{2,1,0:T(8,128)(2,1)} %constant_dynamic-update-slice_fusion.own, bf16[2,512,512]{2,1,0:T(8,128)(2,1)} %constant_dynamic-update-slice_fusion.own, ...), branch_computations={%region_6.8_spmd, %region_7.9_spmd, %region_8.10_spmd, %region_9.1... | conditional | bytes 4194352 | solution.py:166
  42.3 22.9 %collective-permute-done = bf16[2,512,512]{2,1,0:T(8,128)(2,1)} collective-permute-done((bf16[2,512,512]{2,1,0:T(8,128)(2,1)}, bf16[2,512,512]{2,1,0:T(8,128)(2,1)}, u32[]{:S(2)}, u32[]{:S(2)}) %collective-permute-start) | collective-permute-done | bytes 1048608 | tf_op jit(solution)/shard_map/cond/branch_1_fun/ppermute | solution.py:164
  65.2 4.9 %collective-permute-start.18 = (bf16[1,128,512]{2,1,0:T(8,128)(2,1)S(1)}, bf16[1,128,512]{2,1,0:T(8,128)(2,1)S(1)}, u32[]{:S(2)}, u32[]{:S(2)}) collective-permute-start(bf16[1,128,512]{2,1,0:T(8,128)(2,1)S(1)} %get-tuple-element.66), channel_id=1, source_target_pairs={{0,20},{4,24},{8,28},{12,0},{16,4},{20,8},{24,12},{28,16},{1,21},{... | collective-permute-start | bytes 393224 | tf_op jit(solution)/shard_map/ppermute | solution.py:157
  70.5 1.5 collective-permute-start.15
  72.1 10.1 %collective-permute-done.15 = bf16[1,128,512]{2,1,0:T(8,128)(2,1)S(1)} collective-permute-done((bf16[1,128,512]{2,1,0:T(8,128)(2,1)S(1)}, bf16[1,128,512]{2,1,0:T(8,128)(2,1)S(1)}, u32[]{:S(2)}, u32[]{:S(2)}) %collective-permute-start.15) | collective-permute-done | bytes 131104 | tf_op jit(solution)/shard_map/ppermute | solution.py:157
  82.2 6.4 %collective-permute-done.16 = bf16[1,128,512]{2,1,0:T(8,128)(2,1)S(1)} collective-permute-done((bf16[1,128,512]{2,1,0:T(8,128)(2,1)S(1)}, bf16[1,128,512]{2,1,0:T(8,128)(2,1)S(1)}, u32[]{:S(2)}, u32[]{:S(2)}) %collective-permute-start.16) | collective-permute-done | bytes 131104 | tf_op jit(solution)/shard_map/ppermute | solution.py:157
  88.7 1.0 collective-permute-done.20
  89.7 0.6 gather_fusion
  90.5 41.9 %shard_map.118 = (bf16[512,2560]{1,0:T(8,128)(2,1)}, f32[2,512,512]{2,1,0:T(8,128)}, bf16[1,2,512,512]{3,2,1,0:T(8,128)(2,1)}, bf16[2,512,512]{2,1,0:T(8,128)(2,...) custom-call(s32[1]{0:T(128)} %bitcast.2.mode_ref, bf16[512,2560]{1,0:T(8,128)(2,1)} %bitcast.65, ...), custom_call_target="tpu_custom_call" | custom-call | tf_op jit(solution)/shard_map/pallas_call | solution.py:123
  132.4 24.1 %all-to-all-start.1 = ((bf16[8,1,128,512]{3,2,1,0:T(8,128)(2,1)}), bf16[8,1,128,512]{3,2,1,0:T(8,128)(2,1)S(1)}, u32[]{:S(2)}, u32[]{:S(2)}) async-start(bf16[8,1,128,512]{3,2,1,0:T(8,128)(2,1)} %bitcast.21), calls=%async_computation.1 | async-start | bytes 2097152 | tf_op jit(solution)/shard_map/all_to_all | solution.py:210
  156.6 1.2 collective-permute-done.28
  157.8 2.0 collective-permute-start.29
  159.8 4.4 %collective-permute-done.29 = f32[3584]{0:T(1024)S(1)} collective-permute-done((f32[3584]{0:T(1024)S(1)}, f32[3584]{0:T(1024)S(1)}, u32[]{:S(2)}, u32[]{:S(2)}) %collective-permute-start.29) | collective-permute-done | bytes 14368 | tf_op jit(solution)/shard_map/ppermute | solution.py:205
  164.2 1.4 collective-permute-start.30
  165.5 7.0 %collective-permute-done.30 = f32[3584]{0:T(1024)S(1)} collective-permute-done((f32[3584]{0:T(1024)S(1)}, f32[3584]{0:T(1024)S(1)}, u32[]{:S(2)}, u32[]{:S(2)}) %collective-permute-start.30) | collective-permute-done | bytes 14368 | tf_op jit(solution)/shard_map/ppermute | solution.py:205
  172.6 4.8 %collective-permute-start.31 = (f32[3584]{0:T(1024)S(1)}, f32[3584]{0:T(1024)S(1)}, u32[]{:S(2)}, u32[]{:S(2)}) collective-permute-start(f32[3584]{0:T(1024)S(1)} %add.37), channel_id=1, source_target_pairs={{0,16},{1,17},{4,20},{5,21},{8,24},{9,25},{12,28},{13,29},{16,0},{... | collective-permute-start | bytes 43016 | tf_op jit(solution)/shard_map/ppermute | solution.py:205
  177.4 26.0 %conditional.3 = (bf16[2,512,512]{2,1,0:T(8,128)(2,1)S(1)}) conditional(s32[]{:T(128)} %clamp.4, bf16[2,512,512]{2,1,0:T(8,128)(2,1)S(1)} %get-tuple-element.57, bf16[2,512,512]{2,1,0:T(8,128)(2,1)S(1)} %get-tuple-element.57, bf16[2,512,512]{2,1,0:T(8,128)(2,1)S(1)} %get-tuple-element.57, ...), branch_computations={%region_14.16_spmd, %region_15.17_spmd, %region_16.18_spmd, %regio... | conditional | bytes 6291504 | solution.py:166
  177.4 1.5 collective-permute-start.7
  178.9 24.4 %collective-permute-done.7 = bf16[2,512,512]{2,1,0:T(8,128)(2,1)S(1)} collective-permute-done((bf16[2,512,512]{2,1,0:T(8,128)(2,1)S(1)}, bf16[2,512,512]{2,1,0:T(8,128)(2,1)S(1)}, u32[]{:S(2)}, u32[]{:S(2)}) %collective-permute-start.7) | collective-permute-done | bytes 1048608 | tf_op jit(solution)/shard_map/cond/branch_1_fun/ppermute | solution.py:164
  203.4 0.7 slice.31
  204.1 0.6 fusion.10
  205.1 5.3 %collective-permute-start.24 = (bf16[1,128,512]{2,1,0:T(8,128)(2,1)S(1)}, bf16[1,128,512]{2,1,0:T(8,128)(2,1)S(1)}, u32[]{:S(2)}, u32[]{:S(2)}) collective-permute-start(bf16[1,128,512]{2,1,0:T(8,128)(2,1)S(1)} %bitcast.72), channel_id=1, source_target_pairs={{0,16},{4,20},{8,24},{12,28},{16,0},{20,4},{24,8},{28,12},{1,17},{... | collective-permute-start | bytes 393224 | tf_op jit(solution)/shard_map/ppermute | solution.py:157
  210.3 1.5 collective-permute-start.21
  211.8 0.7 bitcast_dynamic-update-slice_fusion.7
  212.5 6.1 %collective-permute-done.21 = bf16[1,128,512]{2,1,0:T(8,128)(2,1)S(1)} collective-permute-done((bf16[1,128,512]{2,1,0:T(8,128)(2,1)S(1)}, bf16[1,128,512]{2,1,0:T(8,128)(2,1)S(1)}, u32[]{:S(2)}, u32[]{:S(2)}) %collective-permute-start.21) | collective-permute-done | bytes 131104 | tf_op jit(solution)/shard_map/ppermute | solution.py:157
  218.9 0.6 bitcast_dynamic-update-slice_fusion.6
  219.5 5.8 %collective-permute-done.22 = bf16[1,128,512]{2,1,0:T(8,128)(2,1)S(1)} collective-permute-done((bf16[1,128,512]{2,1,0:T(8,128)(2,1)S(1)}, bf16[1,128,512]{2,1,0:T(8,128)(2,1)S(1)}, u32[]{:S(2)}, u32[]{:S(2)}) %collective-permute-start.22) | collective-permute-done | bytes 131104 | tf_op jit(solution)/shard_map/ppermute | solution.py:157
  225.3 0.7 collective-permute-start.23
  226.0 0.6 bitcast_dynamic-update-slice_fusion.5
  226.7 6.8 %collective-permute-done.23 = bf16[1,128,512]{2,1,0:T(8,128)(2,1)S(1)} collective-permute-done((bf16[1,128,512]{2,1,0:T(8,128)(2,1)S(1)}, bf16[1,128,512]{2,1,0:T(8,128)(2,1)S(1)}, u32[]{:S(2)}, u32[]{:S(2)}) %collective-permute-start.23) | collective-permute-done | bytes 131104 | tf_op jit(solution)/shard_map/ppermute | solution.py:157
  233.5 0.7 bitcast_dynamic-update-slice_fusion.4
  234.2 0.7 bitcast_dynamic-update-slice_fusion.3
  234.8 0.6 bitcast_dynamic-update-slice_fusion.2
  235.5 0.7 bitcast_dynamic-update-slice_fusion.1
  236.1 0.7 bitcast_dynamic-update-slice_fusion
  236.8 2.0 gather_fusion.1
  239.0 1.0 copy-done.2
  240.0 0.5 fusion.1
  240.5 1.0 fusion.9
  (50 shorter events, 1.9 us)
Async XLA Ops:
  0.6 11.1 %copy-start.3 = (s32[1,8]{1,0:T(1,128)S(1)}, s32[1,8]{1,0:T(1,128)}, u32[]{:S(2)}) copy-start(s32[1,8]{1,0:T(1,128)} %param.31) | copy-start | bytes 100
  0.6 13.1 %copy-start.4 = (s32[1,8]{1,0:T(1,128)S(1)}, s32[1,8]{1,0:T(1,128)}, u32[]{:S(2)}) copy-start(s32[1,8]{1,0:T(1,128)} %param.30) | copy-start | bytes 100
  4.4 33.0 %all-to-all-start = ((bf16[8,128,512]{2,1,0:T(8,128)(2,1)}), bf16[8,128,512]{2,1,0:T(8,128)(2,1)S(1)}, u32[]{:S(2)}, u32[]{:S(2)}) async-start(bf16[8,128,512]{2,1,0:T(8,128)(2,1)} %bitcast.6), calls=%async_computation | async-start | bytes 2097152 | tf_op jit(solution)/shard_map/all_to_all | solution.py:190
  37.5 33.0 %collective-permute-start.14 = (bf16[1,128,512]{2,1,0:T(8,128)(2,1)S(1)}, bf16[1,128,512]{2,1,0:T(8,128)(2,1)S(1)}, u32[]{:S(2)}, u32[]{:S(2)}) collective-permute-start(bf16[1,128,512]{2,1,0:T(8,128)(2,1)S(1)} %get-tuple-element.66), channel_id=1, source_target_pairs={{0,4},{4,8},{8,12},{12,16},{16,20},{20,24},{24,28},{28,0},{1,5},{5... | collective-permute-start | bytes 393224 | tf_op jit(solution)/shard_map/ppermute | solution.py:157
  42.2 22.9 %collective-permute-start = (bf16[2,512,512]{2,1,0:T(8,128)(2,1)}, bf16[2,512,512]{2,1,0:T(8,128)(2,1)}, u32[]{:S(2)}, u32[]{:S(2)}) collective-permute-start(bf16[2,512,512]{2,1,0:T(8,128)(2,1)} %param.3), channel_id=1, source_target_pairs={{0,4},{4,0},{8,12},{12,8},{16,20},{20,16},{24,28},{28,24},{1,5},{5... | collective-permute-start | bytes 3145736 | tf_op jit(solution)/shard_map/cond/branch_1_fun/ppermute | solution.py:164
  65.2 23.5 %collective-permute-start.19 = (bf16[1,128,512]{2,1,0:T(8,128)(2,1)S(1)}, bf16[1,128,512]{2,1,0:T(8,128)(2,1)S(1)}, u32[]{:S(2)}, u32[]{:S(2)}) collective-permute-start(bf16[1,128,512]{2,1,0:T(8,128)(2,1)S(1)} %get-tuple-element.66), channel_id=1, source_target_pairs={{0,24},{4,28},{8,0},{12,4},{16,8},{20,12},{24,16},{28,20},{1,25},{... | collective-permute-start | bytes 393224 | tf_op jit(solution)/shard_map/ppermute | solution.py:157
  65.2 23.4 %collective-permute-start.18 = (bf16[1,128,512]{2,1,0:T(8,128)(2,1)S(1)}, bf16[1,128,512]{2,1,0:T(8,128)(2,1)S(1)}, u32[]{:S(2)}, u32[]{:S(2)}) collective-permute-start(bf16[1,128,512]{2,1,0:T(8,128)(2,1)S(1)} %get-tuple-element.66), channel_id=1, source_target_pairs={{0,20},{4,24},{8,28},{12,0},{16,4},{20,8},{24,12},{28,16},{1,21},{... | collective-permute-start | bytes 393224 | tf_op jit(solution)/shard_map/ppermute | solution.py:157
  70.1 18.5 %collective-permute-start.17 = (bf16[1,128,512]{2,1,0:T(8,128)(2,1)S(1)}, bf16[1,128,512]{2,1,0:T(8,128)(2,1)S(1)}, u32[]{:S(2)}, u32[]{:S(2)}) collective-permute-start(bf16[1,128,512]{2,1,0:T(8,128)(2,1)S(1)} %get-tuple-element.66), channel_id=1, source_target_pairs={{0,16},{4,20},{8,24},{12,28},{16,0},{20,4},{24,8},{28,12},{1,17},{... | collective-permute-start | bytes 393224 | tf_op jit(solution)/shard_map/ppermute | solution.py:157
  70.5 18.0 %collective-permute-start.16 = (bf16[1,128,512]{2,1,0:T(8,128)(2,1)S(1)}, bf16[1,128,512]{2,1,0:T(8,128)(2,1)S(1)}, u32[]{:S(2)}, u32[]{:S(2)}) collective-permute-start(bf16[1,128,512]{2,1,0:T(8,128)(2,1)S(1)} %get-tuple-element.66), channel_id=1, source_target_pairs={{0,12},{4,16},{8,20},{12,24},{16,28},{20,0},{24,4},{28,8},{1,13},{... | collective-permute-start | bytes 393224 | tf_op jit(solution)/shard_map/ppermute | solution.py:157
  70.5 11.6 %collective-permute-start.15 = (bf16[1,128,512]{2,1,0:T(8,128)(2,1)S(1)}, bf16[1,128,512]{2,1,0:T(8,128)(2,1)S(1)}, u32[]{:S(2)}, u32[]{:S(2)}) collective-permute-start(bf16[1,128,512]{2,1,0:T(8,128)(2,1)S(1)} %get-tuple-element.66), channel_id=1, source_target_pairs={{0,8},{4,12},{8,16},{12,20},{16,24},{20,28},{24,0},{28,4},{1,9},{5... | collective-permute-start | bytes 393224 | tf_op jit(solution)/shard_map/ppermute | solution.py:157
  82.1 7.5 %collective-permute-start.20 = (bf16[1,128,512]{2,1,0:T(8,128)(2,1)S(1)}, bf16[1,128,512]{2,1,0:T(8,128)(2,1)S(1)}, u32[]{:S(2)}, u32[]{:S(2)}) collective-permute-start(bf16[1,128,512]{2,1,0:T(8,128)(2,1)S(1)} %get-tuple-element.66), channel_id=1, source_target_pairs={{0,28},{4,0},{8,4},{12,8},{16,12},{20,16},{24,20},{28,24},{1,29},{... | collective-permute-start | bytes 393224 | tf_op jit(solution)/shard_map/ppermute | solution.py:157
  132.4 72.3 %all-to-all-start.1 = ((bf16[8,1,128,512]{3,2,1,0:T(8,128)(2,1)}), bf16[8,1,128,512]{3,2,1,0:T(8,128)(2,1)S(1)}, u32[]{:S(2)}, u32[]{:S(2)}) async-start(bf16[8,1,128,512]{3,2,1,0:T(8,128)(2,1)} %bitcast.21), calls=%async_computation.1 | async-start | bytes 2097152 | tf_op jit(solution)/shard_map/all_to_all | solution.py:210
  156.5 1.2 collective-permute-start.28
  157.8 6.4 %collective-permute-start.29 = (f32[3584]{0:T(1024)S(1)}, f32[3584]{0:T(1024)S(1)}, u32[]{:S(2)}, u32[]{:S(2)}) collective-permute-start(f32[3584]{0:T(1024)S(1)} %fusion.8), channel_id=1, source_target_pairs={{0,4},{1,5},{4,0},{5,1},{8,12},{9,13},{12,8},{13,9},{16,20},{17,21... | collective-permute-start | bytes 43016 | tf_op jit(solution)/shard_map/ppermute | solution.py:205
  164.2 8.4 %collective-permute-start.30 = (f32[3584]{0:T(1024)S(1)}, f32[3584]{0:T(1024)S(1)}, u32[]{:S(2)}, u32[]{:S(2)}) collective-permute-start(f32[3584]{0:T(1024)S(1)} %add.36), channel_id=1, source_target_pairs={{0,8},{1,9},{4,12},{5,13},{8,0},{9,1},{12,4},{13,5},{16,24},{17,25... | collective-permute-start | bytes 43016 | tf_op jit(solution)/shard_map/ppermute | solution.py:205
  172.6 30.8 %collective-permute-start.31 = (f32[3584]{0:T(1024)S(1)}, f32[3584]{0:T(1024)S(1)}, u32[]{:S(2)}, u32[]{:S(2)}) collective-permute-start(f32[3584]{0:T(1024)S(1)} %add.37), channel_id=1, source_target_pairs={{0,16},{1,17},{4,20},{5,21},{8,24},{9,25},{12,28},{13,29},{16,0},{... | collective-permute-start | bytes 43016 | tf_op jit(solution)/shard_map/ppermute | solution.py:205
  177.4 25.9 %collective-permute-start.7 = (bf16[2,512,512]{2,1,0:T(8,128)(2,1)S(1)}, bf16[2,512,512]{2,1,0:T(8,128)(2,1)S(1)}, u32[]{:S(2)}, u32[]{:S(2)}) collective-permute-start(bf16[2,512,512]{2,1,0:T(8,128)(2,1)S(1)} %param.11), channel_id=1, source_target_pairs={{0,4},{4,0},{8,12},{12,8},{16,20},{20,16},{24,28},{28,24},{1,5},{5... | collective-permute-start | bytes 3145736 | tf_op jit(solution)/shard_map/cond/branch_1_fun/ppermute | solution.py:164
  203.4 33.4 %copy-start.1 = (bf16[2,512,512]{2,1,0:T(8,128)(2,1)}, bf16[2,512,512]{2,1,0:T(8,128)(2,1)S(1)}, u32[]{:S(2)}) copy-start(bf16[2,512,512]{2,1,0:T(8,128)(2,1)S(1)} %get-tuple-element.72) | copy-start | bytes 3145732
  204.9 31.3 %collective-permute-start.27 = (bf16[1,128,512]{2,1,0:T(8,128)(2,1)S(1)}, bf16[1,128,512]{2,1,0:T(8,128)(2,1)S(1)}, u32[]{:S(2)}, u32[]{:S(2)}) collective-permute-start(bf16[1,128,512]{2,1,0:T(8,128)(2,1)S(1)} %bitcast.69), channel_id=1, source_target_pairs={{0,28},{4,0},{8,4},{12,8},{16,12},{20,16},{24,20},{28,24},{1,29},{... | collective-permute-start | bytes 393224 | tf_op jit(solution)/shard_map/ppermute | solution.py:157
  204.9 30.5 %collective-permute-start.26 = (bf16[1,128,512]{2,1,0:T(8,128)(2,1)S(1)}, bf16[1,128,512]{2,1,0:T(8,128)(2,1)S(1)}, u32[]{:S(2)}, u32[]{:S(2)}) collective-permute-start(bf16[1,128,512]{2,1,0:T(8,128)(2,1)S(1)} %bitcast.70), channel_id=1, source_target_pairs={{0,24},{4,28},{8,0},{12,4},{16,8},{20,12},{24,16},{28,20},{1,25},{... | collective-permute-start | bytes 393224 | tf_op jit(solution)/shard_map/ppermute | solution.py:157
  205.0 29.8 %collective-permute-start.25 = (bf16[1,128,512]{2,1,0:T(8,128)(2,1)S(1)}, bf16[1,128,512]{2,1,0:T(8,128)(2,1)S(1)}, u32[]{:S(2)}, u32[]{:S(2)}) collective-permute-start(bf16[1,128,512]{2,1,0:T(8,128)(2,1)S(1)} %bitcast.71), channel_id=1, source_target_pairs={{0,20},{4,24},{8,28},{12,0},{16,4},{20,8},{24,12},{28,16},{1,21},{... | collective-permute-start | bytes 393224 | tf_op jit(solution)/shard_map/ppermute | solution.py:157
  205.1 29.1 %collective-permute-start.24 = (bf16[1,128,512]{2,1,0:T(8,128)(2,1)S(1)}, bf16[1,128,512]{2,1,0:T(8,128)(2,1)S(1)}, u32[]{:S(2)}, u32[]{:S(2)}) collective-permute-start(bf16[1,128,512]{2,1,0:T(8,128)(2,1)S(1)} %bitcast.72), channel_id=1, source_target_pairs={{0,16},{4,20},{8,24},{12,28},{16,0},{20,4},{24,8},{28,12},{1,17},{... | collective-permute-start | bytes 393224 | tf_op jit(solution)/shard_map/ppermute | solution.py:157
  210.3 8.2 %collective-permute-start.21 = (bf16[1,128,512]{2,1,0:T(8,128)(2,1)S(1)}, bf16[1,128,512]{2,1,0:T(8,128)(2,1)S(1)}, u32[]{:S(2)}, u32[]{:S(2)}) collective-permute-start(bf16[1,128,512]{2,1,0:T(8,128)(2,1)S(1)} %bitcast.73), channel_id=1, source_target_pairs={{0,4},{4,8},{8,12},{12,16},{16,20},{20,24},{24,28},{28,0},{1,5},{5... | collective-permute-start | bytes 393224 | tf_op jit(solution)/shard_map/ppermute | solution.py:157
  218.6 6.8 %collective-permute-start.22 = (bf16[1,128,512]{2,1,0:T(8,128)(2,1)S(1)}, bf16[1,128,512]{2,1,0:T(8,128)(2,1)S(1)}, u32[]{:S(2)}, u32[]{:S(2)}) collective-permute-start(bf16[1,128,512]{2,1,0:T(8,128)(2,1)S(1)} %bitcast.74), channel_id=1, source_target_pairs={{0,8},{4,12},{8,16},{12,20},{16,24},{20,28},{24,0},{28,4},{1,9},{5... | collective-permute-start | bytes 393224 | tf_op jit(solution)/shard_map/ppermute | solution.py:157
  225.3 8.2 %collective-permute-start.23 = (bf16[1,128,512]{2,1,0:T(8,128)(2,1)S(1)}, bf16[1,128,512]{2,1,0:T(8,128)(2,1)S(1)}, u32[]{:S(2)}, u32[]{:S(2)}) collective-permute-start(bf16[1,128,512]{2,1,0:T(8,128)(2,1)S(1)} %bitcast.75), channel_id=1, source_target_pairs={{0,12},{4,16},{8,20},{12,24},{16,28},{20,0},{24,4},{28,8},{1,13},{... | collective-permute-start | bytes 393224 | tf_op jit(solution)/shard_map/ppermute | solution.py:157
  236.8 2.2 copy-start
  238.8 1.2 copy-start.2

commit v2 on v1

v2 whole, which is shorter than its diff:
```python
import functools

import jax
import jax.numpy as jnp
from jax import lax
from jax.experimental import pallas as pl
from jax.experimental.pallas import tpu as pltpu
from jax.sharding import PartitionSpec as P

HEAD_WIDTH = 128
SCALE = HEAD_WIDTH**-0.5
TO_LOG2 = SCALE * 1.4426950408889634
NEGATIVE_FILL = -1e30
BY_LAST = (((1,), (1,)), ((), ()))
STAGES = (2, 2)
f32, bf16 = jnp.float32, jnp.bfloat16


def widened(row, first, fill):
    if not first:
        return row
    return jnp.concatenate([jnp.full((row.shape[0], first), fill, f32), row], axis=1)


def added(total, term):
    return term if total is None else total + term


def columns(h):
    return pl.ds(pl.multiple_of(h * HEAD_WIDTH, HEAD_WIDTH), HEAD_WIDTH)


def diagonal_scores(keys, qh, k0, q0):
    s = lax.dot_general(keys, qh, BY_LAST, preferred_element_type=f32)
    rows = k0 + lax.broadcasted_iota(jnp.int32, s.shape, 0)
    across = q0 + lax.broadcasted_iota(jnp.int32, s.shape, 1)
    return jnp.where(rows <= across, s, NEGATIVE_FILL)


def halves(tile):
    half = tile // 2
    return [(0, half, 0), (half, half, half)]


def over_keys(a, fn):
    return fn(a, axis=0, keepdims=True)


def own_stats_kernel(mode_ref, q_ref, g_ref, o_ref, k_ref, top_ref, total_ref, delta_ref):
    tile = q_ref.shape[0]
    group = q_ref.shape[1] // HEAD_WIDTH

    def one_head(h, carry):
        cols = columns(h)
        qh, gh, oh = q_ref[:, cols], g_ref[:, cols], o_ref[:, cols]
        delta_ref[0, pl.ds(h, 1), :] = over_keys((gh.astype(f32) * oh.astype(f32)).T, jnp.sum)
        scores = [
            diagonal_scores(k_ref[k0 : k0 + kn], qh[q0:], k0, q0) for k0, kn, q0 in halves(tile)
        ]
        top = None
        for (k0, kn, q0), s in zip(halves(tile), scores):
            m = widened(over_keys(s, jnp.max), q0, NEGATIVE_FILL)
            top = m if top is None else jnp.maximum(top, m)
        top = top * TO_LOG2
        total = None
        for (k0, kn, q0), s in zip(halves(tile), scores):
            e = jnp.exp2(s * TO_LOG2 - top[:, q0:])
            total = added(total, widened(over_keys(e, jnp.sum), q0, 0.0))
        top_ref[0, pl.ds(h, 1), :] = top
        total_ref[0, pl.ds(h, 1), :] = total
        return carry

    @pl.when(mode_ref[0] > 0)
    def _():
        lax.fori_loop(0, group, one_head, 0, unroll=True)

    @pl.when(mode_ref[0] == 0)
    def _():
        for ref in (top_ref, total_ref, delta_ref):
            ref[...] = jnp.zeros_like(ref)


def far_kernel(
    mode_ref, q_ref, g_ref, top_ref, total_ref, delta_ref, far_ref,
    dq_ref, lse_ref, far_out, skv_ref, sums, turned,
):
    tile = q_ref.shape[0]
    group = q_ref.shape[1] // HEAD_WIDTH
    count, others = far_ref.shape[:2]
    mode = mode_ref[0]
    blocks = [
        [far_ref[:, i, kv].reshape(tile, HEAD_WIDTH) for kv in range(2)] for i in range(others)
    ]

    def work(used):
        sums[...] = jnp.zeros_like(sums)
        for b in range(used):
            turned[b] = blocks[b][0].T

        def one_head(h, carry):
            cols = columns(h)
            row = pl.ds(h, 1)
            qh, gh = q_ref[:, cols], g_ref[:, cols]
            scores = [
                lax.dot_general(blocks[b][0], qh, BY_LAST, preferred_element_type=f32)
                for b in range(used)
            ]
            own_top = top_ref[0, row, :]
            top = own_top
            for s in scores:
                top = jnp.maximum(top, over_keys(s, jnp.max) * TO_LOG2)
            total = total_ref[0, row, :] * jnp.exp2(own_top - top)
            exps = []
            for s in scores:
                exps.append(jnp.exp2(s * TO_LOG2 - top))
                total = total + over_keys(exps[-1], jnp.sum)
            inverse = 1.0 / total
            lse_ref[0, row, :] = top + jnp.log2(total)
            delta = delta_ref[0, row, :]
            dq_t = None
            for b in range(used):
                p = exps[b] * inverse
                dp = lax.dot_general(blocks[b][1], gh, BY_LAST, preferred_element_type=f32)
                ds = (p * (dp - delta)).astype(bf16)
                sums[b, 1] += jnp.dot(p.astype(bf16), gh, preferred_element_type=f32)
                sums[b, 0] += jnp.dot(ds, qh, preferred_element_type=f32)
                dq_t = added(dq_t, jnp.dot(turned[b], ds, preferred_element_type=f32))
            dq_ref[:, cols] = dq_t.T
            return carry

        lax.fori_loop(0, group, one_head, 0, unroll=True)

    @pl.when(mode == 1)
    def _():
        work(others - 1)

    @pl.when(mode == 2)
    def _():
        work(others)

    @pl.when(mode == 0)
    def _():
        for ref in (dq_ref, lse_ref, sums):
            ref[...] = jnp.zeros_like(ref)

    over = [0.0, 0.0]
    for kv in range(2):
        for b in range(others):
            grad = sums[b, kv] * SCALE if kv == 0 else sums[b, kv]
            over[kv] += over_keys(grad, jnp.sum)
            far_out[:, b, kv] = grad.astype(bf16).reshape(count, tile // count, HEAD_WIDTH)
        skv_ref[kv] = over[kv]


def own_grads_kernel(
    mode_ref, q_ref, g_ref, lse_ref, delta_ref, k_ref, v_ref, dq_part,
    dq_ref, own_out, sq_ref, skv_ref, sums, turned,
):
    tile = q_ref.shape[0]
    group = q_ref.shape[1] // HEAD_WIDTH

    def one_head(h, carry):
        cols = columns(h)
        row = pl.ds(h, 1)
        qh, gh = q_ref[:, cols], g_ref[:, cols]
        lse, delta = lse_ref[0, row, :], delta_ref[0, row, :]
        dq_t = None
        for k0, kn, q0 in halves(tile):
            s = diagonal_scores(k_ref[k0 : k0 + kn], qh[q0:], k0, q0)
            p = jnp.exp2(s * TO_LOG2 - lse[:, q0:])
            dp = lax.dot_general(v_ref[k0 : k0 + kn], gh[q0:], BY_LAST, preferred_element_type=f32)
            ds = (p * (dp - delta[:, q0:])).astype(bf16)
            sums[1, k0 : k0 + kn] += jnp.dot(p.astype(bf16), gh[q0:], preferred_element_type=f32)
            sums[0, k0 : k0 + kn] += jnp.dot(ds, qh[q0:], preferred_element_type=f32)
            add = jnp.dot(turned[:, k0 : k0 + kn], ds, preferred_element_type=f32)
            dq_t = added(dq_t, widened(add, q0, 0.0))
        dq = (dq_t.T + dq_part[:, cols]) * SCALE
        dq_ref[:, cols] = dq.astype(bf16)
        sq_ref[:, cols] = over_keys(dq, jnp.sum)
        return carry

    sums[...] = jnp.zeros_like(sums)

    @pl.when(mode_ref[0] > 0)
    def _():
        turned[...] = k_ref[...].T
        lax.fori_loop(0, group, one_head, 0, unroll=True)

    @pl.when(mode_ref[0] == 0)
    def _():
        dq_ref[...] = jnp.zeros_like(dq_ref)
        sq_ref[...] = jnp.zeros_like(sq_ref)

    for kv in range(2):
        grad = sums[kv] * SCALE if kv == 0 else sums[kv]
        own_out[kv] = grad
        skv_ref[kv] = over_keys(grad, jnp.sum)


def call(kernel, heads, first, units, in_specs, out_specs, out_shape, scratch, args, aliases={}):
    tile = args[1].shape[0]
    group = in_specs[0].block_shape[1] // HEAD_WIDTH
    macs = int(heads * group * units * tile * tile * HEAD_WIDTH)
    return pl.pallas_call(
        kernel,
        grid_spec=pltpu.PrefetchScalarGridSpec(
            num_scalar_prefetch=1, grid=(heads,), in_specs=in_specs, out_specs=out_specs,
            scratch_shapes=scratch,
        ),
        out_shape=out_shape,
        input_output_aliases=aliases,
        cost_estimate=pl.CostEstimate(
            flops=4 * macs, bytes_accessed=8 * tile * group * heads * HEAD_WIDTH, transcendentals=0
        ),
        compiler_params=pltpu.CompilerParams(vmem_limit_bytes=50 * 2**20),
    )(*args)


def specs(tile, group, first):
    q = pl.BlockSpec((tile, group * HEAD_WIDTH), lambda h, m: (0, first + h))
    kv = pl.BlockSpec((tile, HEAD_WIDTH), lambda h, m: (0, first + h))
    row = pl.BlockSpec((1, group, tile), lambda h, m: (first + h, 0, 0))
    return q, kv, row


def own_stats(mode, q, g, o, keys):
    tile, q_width = q.shape
    heads = keys.shape[1] // HEAD_WIDTH
    group = q_width // keys.shape[1]
    q_spec, kv_spec, row = specs(tile, group, 0)
    stat = jax.ShapeDtypeStruct((heads, group, tile), f32)
    return call(
        own_stats_kernel, heads, 0, 0.75, [q_spec, q_spec, q_spec, kv_spec], [row] * 3, [stat] * 3,
        [], (mode, q, g, o, keys),
    )


def far_grads(first, mode, q, g, stats, far, made):
    tile, q_width = q.shape
    group = stats[0].shape[1]
    count, others, _, rows, part = far.shape
    q_spec, kv_spec, row = specs(tile, group, first)
    far_spec = pl.BlockSpec((count, others, 2, rows, HEAD_WIDTH), lambda h, m: (0, 0, 0, 0, h))
    whole = pl.BlockSpec(memory_space=pl.ANY)

    def kernel(*refs):
        far_kernel(*refs[:7], *refs[7 + len(made) :])

    return call(
        kernel, part // HEAD_WIDTH, first, 5 * others,
        [q_spec, q_spec, row, row, row, far_spec] + [whole] * len(made),
        [q_spec, row, far_spec, pl.BlockSpec((2, 1, HEAD_WIDTH), lambda h, m: (0, 0, h))],
        [
            jax.ShapeDtypeStruct((tile, q_width), f32),
            jax.ShapeDtypeStruct(stats[0].shape, f32),
            jax.ShapeDtypeStruct(far.shape, bf16),
            jax.ShapeDtypeStruct((2, 1, part), f32),
        ],
        [
            pltpu.VMEM((others, 2, tile, HEAD_WIDTH), f32),
            pltpu.VMEM((others, HEAD_WIDTH, tile), bf16),
        ],
        (mode, q, g, *stats, far, *made),
        {7 + i: i for i in range(len(made))},
    )


def own_grads(mode, q, g, lse, delta, keys, values, dq):
    tile, q_width = q.shape
    width = keys.shape[1]
    heads = width // HEAD_WIDTH
    group = q_width // width
    q_spec, kv_spec, row = specs(tile, group, 0)
    return call(
        own_grads_kernel, heads, 0, 3.75, [q_spec, q_spec, row, row, kv_spec, kv_spec, q_spec],
        [q_spec, pl.BlockSpec((2, tile, HEAD_WIDTH), lambda h, m: (0, 0, h)),
         pl.BlockSpec((1, group * HEAD_WIDTH), lambda h, m: (0, h)),
         pl.BlockSpec((2, 1, HEAD_WIDTH), lambda h, m: (0, 0, h))],
        [
            jax.ShapeDtypeStruct((tile, q_width), bf16),
            jax.ShapeDtypeStruct((2, tile, width), f32),
            jax.ShapeDtypeStruct((1, q_width), f32),
            jax.ShapeDtypeStruct((2, 1, width), f32),
        ],
        [pltpu.VMEM((2, tile, HEAD_WIDTH), f32), pltpu.VMEM((HEAD_WIDTH, tile), bf16)],
        (mode, q, g, lse, delta, keys, values, dq),
    )


def pass_on_kernel(sources_ref, chunks, *outs):
    count, others = outs[0].shape[:2]
    for j in range(count):
        for i in range(others):
            source = sources_ref[j * others + i]
            end = 0
            for out in outs:
                first, end = end, end + out.shape[4]
                out[j, i] = chunks[source, :, :, first:end]


def passed_on(sources, chunks, stages):
    count, _, rows, _ = chunks.shape
    others = sources.shape[1]
    in_vmem = pl.BlockSpec(memory_space=pltpu.VMEM)
    return pl.pallas_call(
        pass_on_kernel,
        grid_spec=pltpu.PrefetchScalarGridSpec(
            num_scalar_prefetch=1, in_specs=[in_vmem], out_specs=[in_vmem] * len(stages)
        ),
        out_shape=[
            jax.ShapeDtypeStruct((count, others, 2, rows, n * HEAD_WIDTH), bf16) for n in stages
        ],
        compiler_params=pltpu.CompilerParams(vmem_limit_bytes=50 * 2**20),
    )(sources.reshape(-1), chunks)


def collect_kernel(wanted_ref, *refs):
    *parts, terms, out = refs
    count, others, _, rows, _ = parts[0].shape
    prompts = others - 1
    for i, part in enumerate(parts):
        first = 2 * i * rows
        totals = [part[0, t].astype(f32) for t in range(prompts)]
        for t in range(prompts):
            for source in range(1, count):
                totals[t] += part[source, t].astype(f32)

        for j in range(count):
            w = wanted_ref[j]
            for t in range(prompts):

                @pl.when(w == t)
                def _():
                    for kv in range(2):
                        out[j, first + kv * rows : first + (kv + 1) * rows] = totals[t][kv].astype(bf16)

            @pl.when(w >= prompts)
            def _():
                for kv in range(2):
                    out[j, first + kv * rows : first + (kv + 1) * rows] = part[w - prompts, prompts, kv]

    for j in range(count):
        out[j, 2 * len(parts) * rows :] = terms[...]


def collected(wanted, parts, terms):
    count, _, _, rows, width = parts[0].shape
    shape = (count, 2 * len(parts) * rows + terms.shape[0], width)
    return pl.pallas_call(
        collect_kernel,
        grid_spec=pltpu.PrefetchScalarGridSpec(
            num_scalar_prefetch=1,
            in_specs=[pl.BlockSpec(memory_space=pltpu.VMEM)] * (len(parts) + 1),
            out_specs=pl.BlockSpec(memory_space=pltpu.VMEM),
        ),
        out_shape=jax.ShapeDtypeStruct(shape, bf16),
        compiler_params=pltpu.CompilerParams(vmem_limit_bytes=50 * 2**20),
    )(wanted, *parts, terms)


def pick(vector, index):
    spots = jnp.arange(vector.shape[-1], dtype=jnp.int32)
    return jnp.sum(jnp.where(spots == index, vector, 0), axis=-1)


def tree_routes(parent, owner, prompts):
    count = parent.shape[0]
    spots = jnp.arange(count, dtype=jnp.int32)
    tile_at = jnp.sum(jnp.where(owner[None] == spots[:, None], spots[None], 0), axis=1)
    above = pick(parent[None], tile_at[:, None])
    second = jnp.logical_and(tile_at >= prompts, above >= prompts)
    before = jnp.where(second, pick(owner[None], above[:, None]), -1)
    after = jnp.sum(jnp.where(before[None] == spots[:, None], spots[None] + 1, 0), axis=1) - 1
    return tile_at, before, after


def on_device(query, key, value, output, output_gradient, parent, owner):
    count = lax.axis_size("ctx")
    trees = lax.axis_size("dp")
    me = lax.axis_index("ctx")
    query, key, value, output, upstream = (a[0] for a in (query, key, value, output, output_gradient))
    tile, q_width = query.shape
    width = key.shape[1]
    heads = width // HEAD_WIDTH
    prompts = count // 8
    rows = tile // count
    owner = owner[0]
    tile_at, before_at, after_at = tree_routes(parent[0], owner, prompts)
    mine, before_me, after_me = (pick(a, me) for a in (tile_at, before_at, after_at))
    mode = jnp.where(mine < prompts, 0, jnp.where(before_me < 0, 1, 2)).astype(jnp.int32)[None]

    def exchange(a):
        return lax.all_to_all(a, "ctx", 0, 0)

    sources = jnp.concatenate(
        [jnp.broadcast_to(owner[:prompts], (count, prompts)), jnp.maximum(before_at, 0)[:, None]], axis=1
    )
    stages = STAGES if sum(STAGES) == heads else (1,) * heads
    ends = [sum(stages[: i + 1]) * HEAD_WIDTH for i in range(len(stages))]
    chunks = exchange(jnp.stack([a.reshape(count, rows, width) for a in (key, value)], axis=1))
    stats = own_stats(mode, query, upstream, output, key)
    chunks, stats = lax.optimization_barrier((chunks, stats))
    far = [exchange(block) for block in passed_on(sources, chunks, stages)]

    made, parts, sums_kv = [], [], []
    for end, n, block in zip(ends, stages, far):
        *made, part, skv = far_grads(end // HEAD_WIDTH - n, mode, query, upstream, stats, block, made)
        parts.append(exchange(part))
        sums_kv.append(skv)
    dq, lse = made
    parts[0], lse = lax.optimization_barrier((parts[0], lse))
    dq, own, sq, own_skv = own_grads(mode, query, upstream, lse, stats[2], key, value, dq)

    sums = jnp.concatenate([sq.reshape(-1), (jnp.concatenate(sums_kv, axis=2) + own_skv).reshape(-1)])
    routes = [(i, i ^ 1) for i in range(trees)]
    sums = sums + lax.ppermute(sums, "dp", routes)
    high = lax.reduce_precision(sums, 8, 7)
    low = (sums - high).astype(bf16)
    high = high.astype(bf16)
    part = stages[0] * HEAD_WIDTH
    extra = -(-2 * sums.shape[0] // (16 * part)) * 16
    terms = jnp.concatenate([high, low])
    terms = jnp.pad(terms, (0, extra * part - terms.shape[0])).reshape(extra, part)

    wanted = jnp.where(tile_at < prompts, tile_at, prompts + jnp.maximum(after_at, 0))
    last = exchange(collected(wanted, parts, terms))
    takes = jnp.logical_or(mine < prompts, after_me >= 0)

    terms = last[:, -extra:].reshape(count, -1).astype(f32)
    size = sums.shape[0]
    sums = jnp.sum(terms[:, :size] + terms[:, size : 2 * size], axis=0) * (trees * count * tile) ** -0.5
    outs = []
    for kv in range(2):
        add = [
            last[:, (2 * i + kv) * rows : (2 * i + kv + 1) * rows].reshape(tile, part)
            for i in range(len(stages))
        ]
        add = jnp.where(takes, jnp.concatenate(add, axis=1), 0)
        outs.append((own[kv] + add.astype(f32)).astype(bf16))
    return (
        dq[None],
        outs[0][None],
        outs[1][None],
        sums[:q_width],
        sums[q_width : q_width + width],
        sums[q_width + width :],
    )


def solution(mesh):
    rows = P("dp", "ctx", "head")
    return jax.shard_map(
        on_device,
        mesh=mesh,
        in_specs=(rows, rows, rows, rows, rows, P("dp", None), P("dp", None)),
        out_specs=(rows, rows, rows, P("head"), P("head"), P("head")),
        check_vma=False,
    )
```

time: 244 us -> 194 us (0.80)
  waiting for transfers between devices: 117 us -> 73 us
  starting transfers between devices: 57.5 us -> 22.5 us
  blocking collectives: 0 us -> 29.3 us
  Pallas kernels: 41.9 us -> 51.7 us
  local copies, waits for them, and re-layouts: 15.1 us -> 7.99 us
    ppermute x20 -> x1, waiting for transfers between devices: 96 us -> 1.17 us  [on_device(): sums = sums + lax.ppermute(sums, 'dp', routes)]
    all_to_all x2 -> x5, waiting for transfers between devices: 20.5 us -> 71.8 us  [exchange(): return lax.all_to_all(a, 'ctx', 0, 0)]
    all_to_all x0 -> x1, blocking collectives: none -> 29.3 us  [exchange(): return lax.all_to_all(a, 'ctx', 0, 0)]
    ppermute x20 -> x1, starting transfers between devices: 26.2 us -> 0.07 us  [on_device(): sums = sums + lax.ppermute(sums, 'dp', routes)]
    pallas_call x1 -> x6, Pallas kernels: 41.9 us -> 51.7 us  [the longest x4 49 us: call(): pl.pallas_call(kernel, grid_spec=pltpu.PrefetchScalarGridSpec(num_scalar_...]
    all_to_all x2 -> x5, starting transfers between devices: 31.3 us -> 22.5 us  [exchange(): return lax.all_to_all(a, 'ctx', 0, 0)]
    reduce_sum x4 -> x7, other arithmetic: 4.63 us -> 1.91 us  [the longest x4 1.64 us: pick(): return jnp.sum(jnp.where(spots == index, vector, 0), axis=-1)]
    gather x2 -> x0, local copies, waits for them, and re-layouts: 2.6 us -> none  [shared(): return jnp.take(arrived, (me - jnp.arange(count)) % count, axis=0)]
  transfers between devices with their start and end apart: 22 -> 6, of which waited for: 12 -> 6; matrix products, arithmetic and copies ran while one was open for 5% -> 1% of each run, Pallas kernels for 0% -> 25%
where the time goes in v2:
time: 194 us
  waiting for transfers between devices  73 us (38%)
  Pallas kernels  51.7 us (27%)
  blocking collectives  29.3 us (15%)
  starting transfers between devices  22.5 us (12%)
  local copies, waits for them, and re-layouts  7.99 us (4%)
  other arithmetic  6.59 us (3%)
  between operations  2.8 us (1%)
    all_to_all x5, waiting for transfers between devices, exchange(): return lax.all_to_all(a, 'ctx', 0, 0)  71.8 us
    pallas_call x4, Pallas kernels, call(): pl.pallas_call(kernel, grid_spec=pltpu.PrefetchScalarGridSpec(num_scalar_...  49 us
    all_to_all x1, blocking collectives, exchange(): return lax.all_to_all(a, 'ctx', 0, 0)  29.3 us
    all_to_all x5, starting transfers between devices, exchange(): return lax.all_to_all(a, 'ctx', 0, 0)  22.5 us
    unnamed x22, local copies, waits for them, and re-layouts  5.34 us
  transfers between devices with their start and end apart: 6, of which 6 were waited for; matrix products, arithmetic and copies ran while one was open for 1% of the time, Pallas kernels for 25%

profile of v2, /device:TPU:0, one launch (start us, length us, event | category | flops | bytes accessed | tf_op | source)
XLA Modules:
  0.0 193.8 jit_solution(9968325080314997303)
XLA Ops:
  0.6 0.0 copy-start.3
  0.6 0.0 copy-start.8
  0.7 0.0 copy-start.9
  0.7 2.3 %pad_maximum_fusion = bf16[8,2,64,512]{3,2,1,0:T(8,128)(2,1)} fusion(bf16[8,1,64,512]{3,2,1,0:T(8,128)(2,1)} %bitcast.30, bf16[8,1,64,512]{3,2,1,0:T(8,128)(2,1)} %bitcast.27), kind=kLoop, calls=%fused_computation | loop fusion | flops 524288 | bytes 2097152 | tf_op jit(solution)/shard_map/stack | solution.py:400
  3.0 7.3 %all-to-all-start = ((bf16[8,2,64,512]{3,2,1,0:T(8,128)(2,1)}), bf16[8,2,64,512]{3,2,1,0:T(8,128)(2,1)S(1)}, u32[]{:S(2)}, u32[]{:S(2)}) async-start(bf16[8,2,64,512]{3,2,1,0:T(8,128)(2,1)} %pad_maximum_fusion), calls=%async_computation | async-start | bytes 2097152 | tf_op jit(solution)/shard_map/all_to_all | solution.py:393
  10.2 0.1 select_reduce_fusion.3
  10.4 0.0 copy-done.9
  10.4 0.2 select_reduce_fusion.2
  10.5 0.2 select_reduce_fusion.1
  10.7 0.1 copy.18
  10.8 0.1 concatenate.40.clone
  10.9 0.1 reshape.155.sources_ref
  11.0 0.6 select_reduce_fusion.5
  12.3 0.1 select_reduce_fusion
  12.4 0.6 select_reduce_fusion.4
  13.7 0.0 copy-done.3
  13.7 0.0 copy-start
  13.7 1.7 copy-done
  15.5 6.8 %shard_map.118 = (f32[4,5,512]{2,1,0:T(8,128)S(1)}, f32[4,5,512]{2,1,0:T(8,128)S(1)}, f32[4,5,512]{2,1,0:T(8,128)S(1)}) custom-call(s32[1]{0:T(128)} %bitcast.2.mode_ref.refs_0_, bf16[512,2560]{1,0:T(8,128)(2,1)S(1)} %bitcast.26, bf16[512,2560]{1,0:T(8,128)(2,1)} %bitcast.33, bf16[512,2560]{1,0:T(8,128)(2,1)} %bitcast.32, bf16[512,512]{1,0:T(8,128)(2,1)S(1)} %bitcast.28), custom_call_target="tpu_custom_call" | custom-call | flops 2013265920 | bytes 10485760 | tf_op jit(solution)/shard_map/pallas_call | solution.py:204
  22.3 13.7 %all-to-all-done.chunks = bf16[8,2,64,512]{3,2,1,0:T(8,128)(2,1)S(1)} async-done(((bf16[8,2,64,512]{3,2,1,0:T(8,128)(2,1)}), bf16[8,2,64,512]{3,2,1,0:T(8,128)(2,1)S(1)}, u32[]{:S(2)}, u32[]{:S(2)}) %all-to-all-start) | async-done | bytes 1048608 | tf_op jit(solution)/shard_map/all_to_all | solution.py:393
  36.0 0.7 shard_map.119
  36.7 0.0 copy-start.6
  36.7 29.3 %all_to_all.30.refs_6_ = bf16[8,2,2,64,256]{4,3,2,1,0:T(8,128)(2,1)S(1)} all-to-all(bf16[8,2,2,64,256]{4,3,2,1,0:T(8,128)(2,1)S(1)} %get-tuple-element.36), channel_id=1, replica_groups=mesh['ctx'=8,'head'=2,'dp'=2] {'ctx'}, dimensions={0} | all-to-all | bytes 2097152 | tf_op jit(solution)/shard_map/all_to_all | solution.py:393
  66.0 3.6 %all-to-all-start.3 = ((bf16[8,2,2,64,256]{4,3,2,1,0:T(8,128)(2,1)}), bf16[8,2,2,64,256]{4,3,2,1,0:T(8,128)(2,1)S(1)}, u32[]{:S(2)}, u32[]{:S(2)}) async-start(bf16[8,2,2,64,256]{4,3,2,1,0:T(8,128)(2,1)} %copy-done.6), calls=%async_computation.3 | async-start | bytes 2097152 | tf_op jit(solution)/shard_map/all_to_all | solution.py:393
  69.6 13.2 %shard_map.120 = (f32[512,2560]{1,0:T(8,128)}, f32[4,5,512]{2,1,0:T(8,128)S(1)}, bf16[8,2,2,64,256]{4,3,2,1,0:T(8,128)(2,1)S(1)}, f32[2,1,256]{2,1,0:T(1,128)S(1)}) custom-call(s32[1]{0:T(128)} %bitcast.2.mode_ref.refs_0_, bf16[512,2560]{1,0:T(8,128)(2,1)} %bitcast.23, bf16[512,2560]{1,0:T(8,128)(2,1)} %bitcast.34, ...), custom_call_target="tpu_custom_call" | custom-call | flops 13421772800 | bytes 5242880 | tf_op jit(solution)/shard_map/pallas_call | solution.py:204
  82.9 1.0 copy-done.5
  83.9 11.3 %all-to-all-done.3.refs_6_ = bf16[8,2,2,64,256]{4,3,2,1,0:T(8,128)(2,1)S(1)} async-done(((bf16[8,2,2,64,256]{4,3,2,1,0:T(8,128)(2,1)}), bf16[8,2,2,64,256]{4,3,2,1,0:T(8,128)(2,1)S(1)}, u32[]{:S(2)}, u32[]{:S(2)}) %all-to-all-start.3) | async-done | bytes 1048608 | tf_op jit(solution)/shard_map/all_to_all | solution.py:393
  95.2 3.6 %all-to-all-start.2 = ((bf16[8,2,2,64,256]{4,3,2,1,0:T(8,128)(2,1)}), bf16[8,2,2,64,256]{4,3,2,1,0:T(8,128)(2,1)S(1)}, u32[]{:S(2)}, u32[]{:S(2)}) async-start(bf16[8,2,2,64,256]{4,3,2,1,0:T(8,128)(2,1)} %copy-done.5), calls=%async_computation.2 | async-start | bytes 2097152 | tf_op jit(solution)/shard_map/all_to_all | solution.py:393
  98.8 0.0 copy-start.7
  98.8 13.3 %shard_map.121 = (f32[512,2560]{1,0:T(8,128)}, f32[4,5,512]{2,1,0:T(8,128)S(1)}, bf16[8,2,2,64,256]{4,3,2,1,0:T(8,128)(2,1)S(1)}, f32[2,1,256]{2,1,0:T(1,128)S(1)}) custom-call(s32[1]{0:T(128)} %bitcast.2.mode_ref.refs_0_, bf16[512,2560]{1,0:T(8,128)(2,1)} %bitcast.24, bf16[512,2560]{1,0:T(8,128)(2,1)} %bitcast.35, ...), custom_call_target="tpu_custom_call", output_to_operand_aliasing={{0}: (7, {}), {1}: (8, {})} | custom-call | flops 13421772800 | bytes 5242880 | tf_op jit(solution)/shard_map/pallas_call | solution.py:204
  112.2 1.0 copy-done.4
  113.2 11.4 %all-to-all-done.2.refs_0_ = bf16[8,2,2,64,256]{4,3,2,1,0:T(8,128)(2,1)S(1)} async-done(((bf16[8,2,2,64,256]{4,3,2,1,0:T(8,128)(2,1)}), bf16[8,2,2,64,256]{4,3,2,1,0:T(8,128)(2,1)S(1)}, u32[]{:S(2)}, u32[]{:S(2)}) %all-to-all-start.2) | async-done | bytes 1048608 | tf_op jit(solution)/shard_map/all_to_all | solution.py:393
  124.6 3.6 %all-to-all-start.4 = ((bf16[8,2,2,64,256]{4,3,2,1,0:T(8,128)(2,1)}), bf16[8,2,2,64,256]{4,3,2,1,0:T(8,128)(2,1)S(1)}, u32[]{:S(2)}, u32[]{:S(2)}) async-start(bf16[8,2,2,64,256]{4,3,2,1,0:T(8,128)(2,1)} %copy-done.4), calls=%async_computation.4 | async-start | bytes 2097152 | tf_op jit(solution)/shard_map/all_to_all | solution.py:393
  128.2 0.0 copy-done.7
  128.2 15.6 %shard_map.122 = (bf16[512,2560]{1,0:T(8,128)(2,1)}, f32[2,512,512]{2,1,0:T(8,128)S(1)}, f32[1,2560]{1,0:T(1,128)S(1)}, f32[2,1,512]{2,1,0:T(1,128)S(1)}) custom-call(s32[1]{0:T(128)} %bitcast.2.mode_ref.refs_0_, bf16[512,2560]{1,0:T(8,128)(2,1)} %bitcast.25, bf16[512,2560]{1,0:T(8,128)(2,1)} %bitcast.36, f32[4,5,512]{2,1,0:T(8,128)S(1)} %get-tuple-element.42.lse_ref, ...), custom_call_target="tpu_custom_call" | custom-call | flops 10066329600 | bytes 10485760 | tf_op jit(solution)/shard_map/pallas_call | solution.py:204
  143.9 1.3 copy-done.1
  145.3 0.1 collective-permute-start
  145.3 1.2 collective-permute-done
  146.6 7.6 %all-to-all-done.4.refs_1_ = bf16[8,2,2,64,256]{4,3,2,1,0:T(8,128)(2,1)S(1)} async-done(((bf16[8,2,2,64,256]{4,3,2,1,0:T(8,128)(2,1)}), bf16[8,2,2,64,256]{4,3,2,1,0:T(8,128)(2,1)S(1)}, u32[]{:S(2)}, u32[]{:S(2)}) %all-to-all-start.4) | async-done | bytes 1048608 | tf_op jit(solution)/shard_map/all_to_all | solution.py:393
  154.2 1.9 %shard_map.123 = bf16[8,288,256]{2,1,0:T(8,128)(2,1)} custom-call(s32[8]{0:T(128)S(1)} %get-tuple-element.65.wanted_ref, bf16[8,2,2,64,256]{4,3,2,1,0:T(8,128)(2,1)S(1)} %all-to-all-done.2.refs_0_, bf16[8,2,2,64,256]{4,3,2,1,0:T(8,128)(2,1)S(1)} %all-to-all-done.4.refs_1_, bf16[32,256]{1,0:T(8,128)(2,1)S(1)} %reshape.158.refs_2_), custom_call_target="tpu_custom_call" | custom-call | tf_op jit(solution)/shard_map/pallas_call | solution.py:349
  156.1 4.4 %all-to-all-start.5 = ((bf16[8,288,256]{2,1,0:T(8,128)(2,1)}), bf16[8,288,256]{2,1,0:T(8,128)(2,1)}, u32[]{:S(2)}, u32[]{:S(2)}) async-start(bf16[8,288,256]{2,1,0:T(8,128)(2,1)} %shard_map.123), calls=%async_computation.5 | async-start | bytes 2359296 | tf_op jit(solution)/shard_map/all_to_all | solution.py:393
  161.2 27.7 %all-to-all-done.5 = bf16[8,288,256]{2,1,0:T(8,128)(2,1)} async-done(((bf16[8,288,256]{2,1,0:T(8,128)(2,1)}), bf16[8,288,256]{2,1,0:T(8,128)(2,1)}, u32[]{:S(2)}, u32[]{:S(2)}) %all-to-all-start.5) | async-done | bytes 1179680 | tf_op jit(solution)/shard_map/all_to_all | solution.py:393
  188.9 0.9 convert_bitcast_fusion
  189.8 0.2 copy.19
  190.0 0.6 fusion.6
  190.6 0.6 slice.63
  191.2 1.3 fusion.5
  192.5 1.4 add_convert_fusion
  (16 shorter events, 0.1 us)
Async XLA Ops:
  0.6 13.1 %copy-start.3 = (bf16[1,512,512]{2,1,0:T(8,128)(2,1)S(1)}, bf16[1,512,512]{2,1,0:T(8,128)(2,1)}, u32[]{:S(2)}) copy-start(bf16[1,512,512]{2,1,0:T(8,128)(2,1)} %param.8) | copy-start | bytes 1572868
  0.6 9.6 %copy-start.8 = (s32[1,8]{1,0:T(1,128)S(1)}, s32[1,8]{1,0:T(1,128)}, u32[]{:S(2)}) copy-start(s32[1,8]{1,0:T(1,128)} %param.13) | copy-start | bytes 100
  0.7 9.7 %copy-start.9 = (s32[1,8]{1,0:T(1,128)S(1)}, s32[1,8]{1,0:T(1,128)}, u32[]{:S(2)}) copy-start(s32[1,8]{1,0:T(1,128)} %param.12) | copy-start | bytes 100
  3.0 33.0 %all-to-all-start = ((bf16[8,2,64,512]{3,2,1,0:T(8,128)(2,1)}), bf16[8,2,64,512]{3,2,1,0:T(8,128)(2,1)S(1)}, u32[]{:S(2)}, u32[]{:S(2)}) async-start(bf16[8,2,64,512]{3,2,1,0:T(8,128)(2,1)} %pad_maximum_fusion), calls=%async_computation | async-start | bytes 2097152 | tf_op jit(solution)/shard_map/all_to_all | solution.py:393
  13.7 1.7 copy-start
  36.7 29.3 %copy-start.6 = (bf16[8,2,2,64,256]{4,3,2,1,0:T(8,128)(2,1)}, bf16[8,2,2,64,256]{4,3,2,1,0:T(8,128)(2,1)S(1)}, u32[]{:S(2)}) copy-start(bf16[8,2,2,64,256]{4,3,2,1,0:T(8,128)(2,1)S(1)} %get-tuple-element.38) | copy-start | bytes 3145732
  66.0 29.2 %all-to-all-start.3 = ((bf16[8,2,2,64,256]{4,3,2,1,0:T(8,128)(2,1)}), bf16[8,2,2,64,256]{4,3,2,1,0:T(8,128)(2,1)S(1)}, u32[]{:S(2)}, u32[]{:S(2)}) async-start(bf16[8,2,2,64,256]{4,3,2,1,0:T(8,128)(2,1)} %copy-done.6), calls=%async_computation.3 | async-start | bytes 2097152 | tf_op jit(solution)/shard_map/all_to_all | solution.py:393
  82.9 1.0 copy-start.5
  95.2 29.4 %all-to-all-start.2 = ((bf16[8,2,2,64,256]{4,3,2,1,0:T(8,128)(2,1)}), bf16[8,2,2,64,256]{4,3,2,1,0:T(8,128)(2,1)S(1)}, u32[]{:S(2)}, u32[]{:S(2)}) async-start(bf16[8,2,2,64,256]{4,3,2,1,0:T(8,128)(2,1)} %copy-done.5), calls=%async_computation.2 | async-start | bytes 2097152 | tf_op jit(solution)/shard_map/all_to_all | solution.py:393
  98.8 29.4 %copy-start.7 = (bf16[1,512,512]{2,1,0:T(8,128)(2,1)S(1)}, bf16[1,512,512]{2,1,0:T(8,128)(2,1)}, u32[]{:S(2)}) copy-start(bf16[1,512,512]{2,1,0:T(8,128)(2,1)} %param.9) | copy-start | bytes 1572868
  112.2 1.0 copy-start.4
  124.6 29.6 %all-to-all-start.4 = ((bf16[8,2,2,64,256]{4,3,2,1,0:T(8,128)(2,1)}), bf16[8,2,2,64,256]{4,3,2,1,0:T(8,128)(2,1)S(1)}, u32[]{:S(2)}, u32[]{:S(2)}) async-start(bf16[8,2,2,64,256]{4,3,2,1,0:T(8,128)(2,1)} %copy-done.4), calls=%async_computation.4 | async-start | bytes 2097152 | tf_op jit(solution)/shard_map/all_to_all | solution.py:393
  143.9 1.3 copy-start.1
  145.3 1.2 collective-permute-start
  156.1 36.3 %copy-start.2 = (f32[2,512,512]{2,1,0:T(8,128)S(1)}, f32[2,512,512]{2,1,0:T(8,128)}, u32[]{:S(2)}) copy-start(f32[2,512,512]{2,1,0:T(8,128)} %copy-done.1) | copy-start | bytes 6291460
  156.1 32.7 %all-to-all-start.5 = ((bf16[8,288,256]{2,1,0:T(8,128)(2,1)}), bf16[8,288,256]{2,1,0:T(8,128)(2,1)}, u32[]{:S(2)}, u32[]{:S(2)}) async-start(bf16[8,288,256]{2,1,0:T(8,128)(2,1)} %shard_map.123), calls=%async_computation.5 | async-start | bytes 2359296 | tf_op jit(solution)/shard_map/all_to_all | solution.py:393

commit v3 on v2

--- a/solution.py
+++ b/solution.py
@@ -13,6 +13,7 @@
 NEGATIVE_FILL = -1e30
 BY_LAST = (((1,), (1,)), ((), ()))
 STAGES = (2, 2)
+TERM_ROWS = 16
 f32, bf16 = jnp.float32, jnp.bfloat16
 
 
@@ -81,15 +82,19 @@
 
 
 def far_kernel(
-    mode_ref, q_ref, g_ref, top_ref, total_ref, delta_ref, far_ref,
+    mode_ref, q_ref, g_ref, top_ref, total_ref, delta_ref, far_refs,
     dq_ref, lse_ref, far_out, skv_ref, sums, turned,
 ):
     tile = q_ref.shape[0]
     group = q_ref.shape[1] // HEAD_WIDTH
-    count, others = far_ref.shape[:2]
-    mode = mode_ref[0]
+    by_distance = len(far_refs) > 1
+    chunks = far_refs if by_distance else [far_refs[0].at[i] for i in range(far_refs[0].shape[0])]
+    count, others = len(chunks), chunks[0].shape[0]
+    rows = tile // count
+    mode, me = mode_ref[0], mode_ref[1]
     blocks = [
-        [far_ref[:, i, kv].reshape(tile, HEAD_WIDTH) for kv in range(2)] for i in range(others)
+        [jnp.concatenate([ref[i, kv] for ref in chunks], axis=0) for kv in range(2)]
+        for i in range(others)
     ]
 
     def work(used):
@@ -148,7 +153,10 @@
         for b in range(others):
             grad = sums[b, kv] * SCALE if kv == 0 else sums[b, kv]
             over[kv] += over_keys(grad, jnp.sum)
-            far_out[:, b, kv] = grad.astype(bf16).reshape(count, tile // count, HEAD_WIDTH)
+            grad = grad.astype(bf16)
+            for d in range(count):
+                at = around(me, -d, count) if by_distance else d
+                far_out[at, b, kv] = grad[d * rows : (d + 1) * rows]
         skv_ref[kv] = over[kv]
 
 
@@ -238,30 +246,34 @@
 def far_grads(first, mode, q, g, stats, far, made):
     tile, q_width = q.shape
     group = stats[0].shape[1]
-    count, others, _, rows, part = far.shape
+    given = len(far)
+    others, _, rows, part = far[0].shape[-4:]
+    count = tile // rows
     q_spec, kv_spec, row = specs(tile, group, first)
+    chunk_spec = pl.BlockSpec((others, 2, rows, HEAD_WIDTH), lambda h, m: (0, 0, 0, h))
     far_spec = pl.BlockSpec((count, others, 2, rows, HEAD_WIDTH), lambda h, m: (0, 0, 0, 0, h))
     whole = pl.BlockSpec(memory_space=pl.ANY)
 
     def kernel(*refs):
-        far_kernel(*refs[:7], *refs[7 + len(made) :])
+        far_kernel(*refs[:6], refs[6 : 6 + given], *refs[6 + given + len(made) :])
 
     return call(
         kernel, part // HEAD_WIDTH, first, 5 * others,
-        [q_spec, q_spec, row, row, row, far_spec] + [whole] * len(made),
+        [q_spec, q_spec, row, row, row]
+        + ([far_spec] if given == 1 else [chunk_spec] * given) + [whole] * len(made),
         [q_spec, row, far_spec, pl.BlockSpec((2, 1, HEAD_WIDTH), lambda h, m: (0, 0, h))],
         [
             jax.ShapeDtypeStruct((tile, q_width), f32),
             jax.ShapeDtypeStruct(stats[0].shape, f32),
-            jax.ShapeDtypeStruct(far.shape, bf16),
+            jax.ShapeDtypeStruct((count, others, 2, rows, part), bf16),
             jax.ShapeDtypeStruct((2, 1, part), f32),
         ],
         [
             pltpu.VMEM((others, 2, tile, HEAD_WIDTH), f32),
             pltpu.VMEM((others, HEAD_WIDTH, tile), bf16),
         ],
-        (mode, q, g, *stats, far, *made),
-        {7 + i: i for i in range(len(made))},
+        (mode, q, g, *stats, *far, *made),
+        {6 + given + i: i for i in range(len(made))},
     )
 
 
@@ -287,75 +299,106 @@
     )
 
 
-def pass_on_kernel(sources_ref, chunks, *outs):
-    count, others = outs[0].shape[:2]
-    for j in range(count):
+def around(me, d, count):
+    return lax.rem(me + (count + d), count)
+
+
+def chunk_kernel(me_ref, key, value, *outs):
+    count, rows = len(outs), outs[0].shape[1]
+    for d, out in enumerate(outs):
+        at = pl.ds(pl.multiple_of(around(me_ref[0], d, count) * rows, rows), rows)
+        out[0] = key[at]
+        out[1] = value[at]
+
+
+def pass_on_kernel(sources_ref, *refs):
+    count = refs[-1].shape[0]
+    chunks, outs, table = refs[:count], refs[count:-1], refs[-1]
+    others = outs[0].shape[0]
+    me = sources_ref[count * others]
+    for d in range(count):
+        table[around(me, -d, count)] = chunks[d][...]
+    for d in range(count):
+        to = around(me, d, count)
         for i in range(others):
-            source = sources_ref[j * others + i]
-            end = 0
-            for out in outs:
+            source = sources_ref[to * others + i]
+            end = outs[0].shape[3]
+            outs[d][i] = table[source, :, :, :end]
+            for out in outs[count:]:
                 first, end = end, end + out.shape[4]
-                out[j, i] = chunks[source, :, :, first:end]
-
-
-def passed_on(sources, chunks, stages):
-    count, _, rows, _ = chunks.shape
-    others = sources.shape[1]
-    in_vmem = pl.BlockSpec(memory_space=pltpu.VMEM)
-    return pl.pallas_call(
-        pass_on_kernel,
-        grid_spec=pltpu.PrefetchScalarGridSpec(
-            num_scalar_prefetch=1, in_specs=[in_vmem], out_specs=[in_vmem] * len(stages)
-        ),
-        out_shape=[
-            jax.ShapeDtypeStruct((count, others, 2, rows, n * HEAD_WIDTH), bf16) for n in stages
-        ],
-        compiler_params=pltpu.CompilerParams(vmem_limit_bytes=50 * 2**20),
-    )(sources.reshape(-1), chunks)
-
-
-def collect_kernel(wanted_ref, *refs):
-    *parts, terms, out = refs
-    count, others, _, rows, _ = parts[0].shape
+                out[to, i] = table[source, :, :, first:end]
+
+
+def collect_kernel(wanted_ref, sums, *refs):
+    count, others, _, rows, part = refs[0].shape
+    parts, outs = refs[:-count], refs[-count:]
     prompts = others - 1
-    for i, part in enumerate(parts):
-        first = 2 * i * rows
-        totals = [part[0, t].astype(f32) for t in range(prompts)]
+    me = wanted_ref[count]
+    for n, source_parts in enumerate(parts):
+        totals = [source_parts[0, t].astype(f32) for t in range(prompts)]
         for t in range(prompts):
             for source in range(1, count):
-                totals[t] += part[source, t].astype(f32)
-
-        for j in range(count):
-            w = wanted_ref[j]
+                totals[t] += source_parts[source, t].astype(f32)
+        for d, out in enumerate(outs):
+            w = wanted_ref[around(me, d, count)]
+            first = 2 * n * rows
             for t in range(prompts):
 
                 @pl.when(w == t)
                 def _():
                     for kv in range(2):
-                        out[j, first + kv * rows : first + (kv + 1) * rows] = totals[t][kv].astype(bf16)
+                        out[first + kv * rows : first + (kv + 1) * rows] = totals[t][kv].astype(bf16)
 
             @pl.when(w >= prompts)
             def _():
                 for kv in range(2):
-                    out[j, first + kv * rows : first + (kv + 1) * rows] = part[w - prompts, prompts, kv]
-
-    for j in range(count):
-        out[j, 2 * len(parts) * rows :] = terms[...]
-
-
-def collected(wanted, parts, terms):
-    count, _, _, rows, width = parts[0].shape
-    shape = (count, 2 * len(parts) * rows + terms.shape[0], width)
+                    out[first + kv * rows : first + (kv + 1) * rows] = source_parts[
+                        w - prompts, prompts, kv
+                    ]
+
+    high = sums[...].astype(bf16)
+    low = (sums[...] - high.astype(f32)).astype(bf16)
+    first = 2 * len(parts) * rows
+    for out in outs:
+        out[first : first + TERM_ROWS] = high
+        out[first + TERM_ROWS :] = low
+
+
+def finish_kernel(norm, at_ref, own, *refs):
+    chunks, outs, total, table = refs[:-4], refs[-4:-2], refs[-2], refs[-1]
+    count = len(chunks)
+    part = chunks[0].shape[1]
+    rows = own.shape[1] // count
+    stages = own.shape[2] // part
+    for d in range(count):
+        source = around(at_ref[0], -d, count)
+        at = pl.ds(pl.multiple_of(source * rows, rows), rows)
+        for n in range(stages):
+            cols = slice(n * part, (n + 1) * part)
+            for kv in range(2):
+                first = (2 * n + kv) * rows
+                add = jnp.where(at_ref[1] == 1, chunks[d][first : first + rows].astype(f32), 0.0)
+                outs[kv][at, cols] = (own[kv, at, cols] + add).astype(bf16)
+        first = 2 * stages * rows
+        high, low = chunks[d][first : first + TERM_ROWS], chunks[d][first + TERM_ROWS :]
+        table[source] = high.astype(f32) + low.astype(f32)
+    over = table[0]
+    for i in range(1, count):
+        over += table[i]
+    total[...] = over * norm
+
+
+def layout(kernel, scalars, args, out_shape, scratch=()):
+    in_vmem = pl.BlockSpec(memory_space=pltpu.VMEM)
     return pl.pallas_call(
-        collect_kernel,
+        kernel,
         grid_spec=pltpu.PrefetchScalarGridSpec(
-            num_scalar_prefetch=1,
-            in_specs=[pl.BlockSpec(memory_space=pltpu.VMEM)] * (len(parts) + 1),
-            out_specs=pl.BlockSpec(memory_space=pltpu.VMEM),
+            num_scalar_prefetch=1, in_specs=[in_vmem] * len(args), out_specs=[in_vmem] * len(out_shape),
+            scratch_shapes=list(scratch),
         ),
-        out_shape=jax.ShapeDtypeStruct(shape, bf16),
+        out_shape=out_shape,
         compiler_params=pltpu.CompilerParams(vmem_limit_bytes=50 * 2**20),
-    )(wanted, *parts, terms)
+    )(scalars, *args)
 
 
 def pick(vector, index):
@@ -387,7 +430,8 @@
     owner = owner[0]
     tile_at, before_at, after_at = tree_routes(parent[0], owner, prompts)
     mine, before_me, after_me = (pick(a, me) for a in (tile_at, before_at, after_at))
-    mode = jnp.where(mine < prompts, 0, jnp.where(before_me < 0, 1, 2)).astype(jnp.int32)[None]
+    mode = jnp.where(mine < prompts, 0, jnp.where(before_me < 0, 1, 2))
+    mode = jnp.stack([mode, me]).astype(jnp.int32)
 
     def exchange(a):
         return lax.all_to_all(a, "ctx", 0, 0)
@@ -397,10 +441,28 @@
     )
     stages = STAGES if sum(STAGES) == heads else (1,) * heads
     ends = [sum(stages[: i + 1]) * HEAD_WIDTH for i in range(len(stages))]
-    chunks = exchange(jnp.stack([a.reshape(count, rows, width) for a in (key, value)], axis=1))
+    routes = [[(i, (i + d) % count) for i in range(count)] for d in range(count)]
+
+    def around_ring(by_distance):
+        sent = [lax.ppermute(a, "ctx", route) for a, route in zip(by_distance[1:], routes[1:])]
+        return [by_distance[0], *sent]
+
+    here = me.astype(jnp.int32)[None]
+    chunk = jax.ShapeDtypeStruct((2, rows, width), bf16)
+    chunks = around_ring(layout(chunk_kernel, here, (key, value), [chunk] * count))
     stats = own_stats(mode, query, upstream, output, key)
     chunks, stats = lax.optimization_barrier((chunks, stats))
-    far = [exchange(block) for block in passed_on(sources, chunks, stages)]
+    sizes = [(prompts + 1, 2, rows, n * HEAD_WIDTH) for n in stages]
+    pieces = layout(
+        pass_on_kernel, jnp.concatenate([sources.reshape(-1), here]), chunks,
+        [jax.ShapeDtypeStruct(sizes[0], bf16)] * count
+        + [jax.ShapeDtypeStruct((count, *size), bf16) for size in sizes[1:]],
+        [pltpu.VMEM((count, 2, rows, width), bf16)],
+    )
+    far = [around_ring(pieces[:count])]
+    if len(stages) > 1:
+        pieces, far = lax.optimization_barrier((pieces[count:], far))
+        far += [[exchange(piece)] for piece in pieces]
 
     made, parts, sums_kv = [], [], []
     for end, n, block in zip(ends, stages, far):
@@ -411,39 +473,31 @@
     parts[0], lse = lax.optimization_barrier((parts[0], lse))
     dq, own, sq, own_skv = own_grads(mode, query, upstream, lse, stats[2], key, value, dq)
 
+    part = stages[0] * HEAD_WIDTH
     sums = jnp.concatenate([sq.reshape(-1), (jnp.concatenate(sums_kv, axis=2) + own_skv).reshape(-1)])
-    routes = [(i, i ^ 1) for i in range(trees)]
-    sums = sums + lax.ppermute(sums, "dp", routes)
-    high = lax.reduce_precision(sums, 8, 7)
-    low = (sums - high).astype(bf16)
-    high = high.astype(bf16)
-    part = stages[0] * HEAD_WIDTH
-    extra = -(-2 * sums.shape[0] // (16 * part)) * 16
-    terms = jnp.concatenate([high, low])
-    terms = jnp.pad(terms, (0, extra * part - terms.shape[0])).reshape(extra, part)
-
+    sums = sums + lax.ppermute(sums, "dp", [(i, i ^ 1) for i in range(trees)])
+    size = sums.shape[0]
+    sums = jnp.pad(sums, (0, TERM_ROWS * part - size)).reshape(TERM_ROWS, part)
     wanted = jnp.where(tile_at < prompts, tile_at, prompts + jnp.maximum(after_at, 0))
-    last = exchange(collected(wanted, parts, terms))
+    chunk = jax.ShapeDtypeStruct((2 * len(stages) * rows + 2 * TERM_ROWS, part), bf16)
+    last = around_ring(
+        layout(collect_kernel, jnp.concatenate([wanted, here]), (sums, *parts), [chunk] * count)
+    )
     takes = jnp.logical_or(mine < prompts, after_me >= 0)
-
-    terms = last[:, -extra:].reshape(count, -1).astype(f32)
-    size = sums.shape[0]
-    sums = jnp.sum(terms[:, :size] + terms[:, size : 2 * size], axis=0) * (trees * count * tile) ** -0.5
-    outs = []
-    for kv in range(2):
-        add = [
-            last[:, (2 * i + kv) * rows : (2 * i + kv + 1) * rows].reshape(tile, part)
-            for i in range(len(stages))
-        ]
-        add = jnp.where(takes, jnp.concatenate(add, axis=1), 0)
-        outs.append((own[kv] + add.astype(f32)).astype(bf16))
+    *outs, sums = layout(
+        functools.partial(finish_kernel, (trees * count * tile) ** -0.5),
+        jnp.stack([me, takes.astype(me.dtype)]).astype(jnp.int32), (own, *last),
+        [jax.ShapeDtypeStruct((tile, width), bf16)] * 2 + [jax.ShapeDtypeStruct(sums.shape, f32)],
+        [pltpu.VMEM((count, TERM_ROWS, part), f32)],
+    )
+    sums = sums.reshape(-1)
     return (
         dq[None],
         outs[0][None],
         outs[1][None],
         sums[:q_width],
         sums[q_width : q_width + width],
-        sums[q_width + width :],
+        sums[q_width + width : size],
     )
 
 

time: 194 us -> 178 us (0.918)
  the two profiles are of different devices: /device:TPU:0 before, /device:TPU:15 now
where the time goes in v3:
time: 178 us; the launch traced here: 177 us
  Pallas kernels  70.6 us (40%)
  waiting for transfers between devices  44.3 us (25%)
  starting transfers between devices  42.7 us (24%)
  local copies, waits for them, and re-layouts  13 us (7%)
  other arithmetic  3.6 us (2%)
  between operations  2.72 us (2%)
    pallas_call x4, Pallas kernels, call(): pl.pallas_call(kernel, grid_spec=pltpu.PrefetchScalarGridSpec(num_scalar_...  66.1 us
    ppermute x21, waiting for transfers between devices, around_ring(): lax.ppermute(a, 'ctx', route)  43.1 us
    ppermute x21, starting transfers between devices, around_ring(): lax.ppermute(a, 'ctx', route)  22.8 us
    all_to_all x3, starting transfers between devices, exchange(): return lax.all_to_all(a, 'ctx', 0, 0)  15 us
    unnamed x28, local copies, waits for them, and re-layouts  12.2 us
    ppermute x1, starting transfers between devices, on_device(): sums = sums + lax.ppermute(sums, 'dp', [(i, i ^ 1) for i in range(trees)])  4.83 us
    pallas_call x4, Pallas kernels, layout(): pl.pallas_call(kernel, grid_spec=pltpu.PrefetchScalarGridSpec(num_scalar_...  4.48 us
  transfers between devices with their start and end apart: 25, of which 12 were waited for; matrix products, arithmetic and copies ran while one was open for 2% of the time, Pallas kernels for 37%

profile of v3, /device:TPU:15, one launch (start us, length us, event | category | flops | bytes accessed | tf_op | source)
XLA Modules:
  0.0 177.0 jit_solution(14460278149972446657)
XLA Ops:
  0.6 1.0 copy-done.1
  1.7 1.0 copy-done.9
  2.8 1.3 collective-permute-start
  4.1 1.3 collective-permute-start.1
  5.4 0.9 collective-permute-start.2
  6.3 1.3 collective-permute-start.3
  7.7 1.0 collective-permute-start.4
  8.7 0.8 select_reduce_fusion.3
  9.5 0.8 select_reduce_fusion.2
  10.3 0.8 select_reduce_fusion.1
  13.4 1.2 collective-permute-start.5
  14.6 1.4 collective-permute-start.6
  16.0 1.7 copy-done
  17.7 1.0 copy-done.2
  18.8 7.4 %shard_map.119 = (f32[4,5,512]{2,1,0:T(8,128)S(1)}, f32[4,5,512]{2,1,0:T(8,128)S(1)}, f32[4,5,512]{2,1,0:T(8,128)S(1)}) custom-call(s32[2]{0:T(128)S(1)} %pad_add_fusion.mode_ref.refs_0_, bf16[512,2560]{1,0:T(8,128)(2,1)S(1)} %bitcast.28, bf16[512,2560]{1,0:T(8,128)(2,1)} %bitcast.36, bf16[512,2560]{1,0:T(8,128)(2,1)} %bitcast.35, bf16[512,512]{1,0:T(8,128)(2,1)S(1)} %bitcast.30), custom_call_target="tpu_custom_call" | custom-call | flops 2013265920 | bytes 10485760 | tf_op jit(solution)/shard_map/pallas_call | solution.py:212
  26.5 2.3 %collective-permute-done.5.refs_6_ = bf16[2,64,512]{2,1,0:T(8,128)(2,1)S(1)} collective-permute-done((bf16[2,64,512]{2,1,0:T(8,128)(2,1)S(1)}, bf16[2,64,512]{2,1,0:T(8,128)(2,1)S(1)}, u32[]{:S(2)}, u32[]{:S(2)}) %collective-permute-start.5) | collective-permute-done | bytes 131104 | tf_op jit(solution)/shard_map/ppermute | solution.py:447
  28.8 1.2 collective-permute-done.6.refs_7_
  30.0 1.7 shard_map.120
  31.7 0.9 collective-permute-start.9
  32.6 2.6 %collective-permute-start.10 = (bf16[2,2,64,256]{3,2,1,0:T(8,128)(2,1)S(1)}, bf16[2,2,64,256]{3,2,1,0:T(8,128)(2,1)S(1)}, u32[]{:S(2)}, u32[]{:S(2)}) collective-permute-start(bf16[2,2,64,256]{3,2,1,0:T(8,128)(2,1)S(1)} %get-tuple-element.98), channel_id=1, source_target_pairs={{0,16},{4,20},{8,24},{12,28},{16,0},{20,4},{24,8},{28,12},{1,17},{... | collective-permute-start | bytes 393224 | tf_op jit(solution)/shard_map/ppermute | solution.py:447
  35.5 1.8 %collective-permute-start.12 = (bf16[2,2,64,256]{3,2,1,0:T(8,128)(2,1)S(1)}, bf16[2,2,64,256]{3,2,1,0:T(8,128)(2,1)S(1)}, u32[]{:S(2)}, u32[]{:S(2)}) collective-permute-start(bf16[2,2,64,256]{3,2,1,0:T(8,128)(2,1)S(1)} %get-tuple-element.100), channel_id=1, source_target_pairs={{0,24},{4,28},{8,0},{12,4},{16,8},{20,12},{24,16},{28,20},{1,25},{... | collective-permute-start | bytes 393224 | tf_op jit(solution)/shard_map/ppermute | solution.py:447
  38.5 12.5 %collective-permute-done.10.refs_10_ = bf16[2,2,64,256]{3,2,1,0:T(8,128)(2,1)S(1)} collective-permute-done((bf16[2,2,64,256]{3,2,1,0:T(8,128)(2,1)S(1)}, bf16[2,2,64,256]{3,2,1,0:T(8,128)(2,1)S(1)}, u32[]{:S(2)}, u32[]{:S(2)}) %collective-permute-start.10) | collective-permute-done | bytes 131104 | tf_op jit(solution)/shard_map/ppermute | solution.py:447
  51.0 5.0 %collective-permute-done.12.refs_12_ = bf16[2,2,64,256]{3,2,1,0:T(8,128)(2,1)S(1)} collective-permute-done((bf16[2,2,64,256]{3,2,1,0:T(8,128)(2,1)S(1)}, bf16[2,2,64,256]{3,2,1,0:T(8,128)(2,1)S(1)}, u32[]{:S(2)}, u32[]{:S(2)}) %collective-permute-start.12) | collective-permute-done | bytes 131104 | tf_op jit(solution)/shard_map/ppermute | solution.py:447
  56.1 3.6 %all-to-all-start.1 = ((bf16[8,2,2,64,256]{4,3,2,1,0:T(8,128)(2,1)}), bf16[8,2,2,64,256]{4,3,2,1,0:T(8,128)(2,1)S(1)}, u32[]{:S(2)}, u32[]{:S(2)}) async-start(bf16[8,2,2,64,256]{4,3,2,1,0:T(8,128)(2,1)} %get-tuple-element.111), calls=%async_computation.1 | async-start | bytes 2097152 | tf_op jit(solution)/shard_map/all_to_all | solution.py:437
  59.7 21.3 %shard_map.121 = (f32[512,2560]{1,0:T(8,128)}, f32[4,5,512]{2,1,0:T(8,128)S(1)}, bf16[8,2,2,64,256]{4,3,2,1,0:T(8,128)(2,1)}, f32[2,1,256]{2,1,0:T(1,128)S(1)}) custom-call(s32[2]{0:T(128)S(1)} %pad_add_fusion.mode_ref.refs_0_, bf16[512,2560]{1,0:T(8,128)(2,1)} %bitcast.25, bf16[512,2560]{1,0:T(8,128)(2,1)} %bitcast.37, ...), custom_call_target="tpu_custom_call" | custom-call | flops 13421772800 | bytes 5242880 | tf_op jit(solution)/shard_map/pallas_call | solution.py:212
  81.5 1.0 copy-done.7
  82.5 6.3 %all-to-all-start = ((bf16[8,2,2,64,256]{4,3,2,1,0:T(8,128)(2,1)}), bf16[8,2,2,64,256]{4,3,2,1,0:T(8,128)(2,1)S(1)}, u32[]{:S(2)}, u32[]{:S(2)}) async-start(bf16[8,2,2,64,256]{4,3,2,1,0:T(8,128)(2,1)} %get-tuple-element.110), calls=%async_computation | async-start | bytes 2097152 | tf_op jit(solution)/shard_map/all_to_all | solution.py:437
  88.8 1.2 copy-done.8
  90.0 21.2 %shard_map.122 = (f32[512,2560]{1,0:T(8,128)}, f32[4,5,512]{2,1,0:T(8,128)S(1)}, bf16[8,2,2,64,256]{4,3,2,1,0:T(8,128)(2,1)S(1)}, f32[2,1,256]{2,1,0:T(1,128)S(1)}) custom-call(s32[2]{0:T(128)S(1)} %pad_add_fusion.mode_ref.refs_0_, bf16[512,2560]{1,0:T(8,128)(2,1)} %bitcast.26, ...), custom_call_target="tpu_custom_call", output_to_operand_aliasing={{0}: (7, {}), {1}: (8, {})} | custom-call | flops 13421772800 | bytes 5242880 | tf_op jit(solution)/shard_map/pallas_call | solution.py:212
  111.3 1.0 copy-done.6
  112.2 5.1 %all-to-all-start.2 = ((bf16[8,2,2,64,256]{4,3,2,1,0:T(8,128)(2,1)}), bf16[8,2,2,64,256]{4,3,2,1,0:T(8,128)(2,1)S(1)}, u32[]{:S(2)}, u32[]{:S(2)}) async-start(bf16[8,2,2,64,256]{4,3,2,1,0:T(8,128)(2,1)} %copy-done.6), calls=%async_computation.2 | async-start | bytes 2097152 | tf_op jit(solution)/shard_map/all_to_all | solution.py:437
  117.3 16.2 %shard_map.123 = (bf16[512,2560]{1,0:T(8,128)(2,1)}, f32[2,512,512]{2,1,0:T(8,128)S(1)}, f32[1,2560]{1,0:T(1,128)S(1)}, f32[2,1,512]{2,1,0:T(1,128)S(1)}) custom-call(s32[2]{0:T(128)S(1)} %pad_add_fusion.mode_ref.refs_0_, bf16[512,2560]{1,0:T(8,128)(2,1)} %bitcast.27, bf16[512,2560]{1,0:T(8,128)(2,1)} %bitcast.39, ...), custom_call_target="tpu_custom_call" | custom-call | flops 10066329600 | bytes 10485760 | tf_op jit(solution)/shard_map/pallas_call | solution.py:212
  133.5 1.3 copy-done.4
  134.8 4.8 %collective-permute-start.14 = (f32[3584]{0:T(1024)S(1)}, f32[3584]{0:T(1024)S(1)}, u32[]{:S(2)}, u32[]{:S(2)}) collective-permute-start(f32[3584]{0:T(1024)S(1)} %pad_maximum_fusion), channel_id=1, source_target_pairs={{0,1},{1,0},{2,3},{3,2},{4,5},{5,4},{6,7},{7,6},{8,9},{9,8},{10,11... | collective-permute-start | bytes 43016 | tf_op jit(solution)/shard_map/ppermute | solution.py:478
  139.8 0.8 collective-permute-done.14
  140.6 0.9 shard_map.124
  141.6 2.4 %collective-permute-start.16 = (bf16[288,256]{1,0:T(8,128)(2,1)S(1)}, bf16[288,256]{1,0:T(8,128)(2,1)S(1)}, u32[]{:S(2)}, u32[]{:S(2)}) collective-permute-start(bf16[288,256]{1,0:T(8,128)(2,1)S(1)} %get-tuple-element.127), channel_id=1, source_target_pairs={{0,8},{4,12},{8,16},{12,20},{16,24},{20,28},{24,0},{28,4},{1,9},{5... | collective-permute-start | bytes 442376 | tf_op jit(solution)/shard_map/ppermute | solution.py:447
  143.9 1.4 collective-permute-start.17
  145.3 1.0 collective-permute-start.18
  146.3 1.2 collective-permute-start.19
  147.5 1.0 collective-permute-start.20
  148.4 1.4 collective-permute-start.21
  150.6 12.7 %collective-permute-done.17.refs_3_ = bf16[288,256]{1,0:T(8,128)(2,1)S(1)} collective-permute-done((bf16[288,256]{1,0:T(8,128)(2,1)S(1)}, bf16[288,256]{1,0:T(8,128)(2,1)S(1)}, u32[]{:S(2)}, u32[]{:S(2)}) %collective-permute-start.17) | collective-permute-done | bytes 147488 | tf_op jit(solution)/shard_map/ppermute | solution.py:447
  163.2 3.2 %collective-permute-done.18.refs_4_ = bf16[288,256]{1,0:T(8,128)(2,1)S(1)} collective-permute-done((bf16[288,256]{1,0:T(8,128)(2,1)S(1)}, bf16[288,256]{1,0:T(8,128)(2,1)S(1)}, u32[]{:S(2)}, u32[]{:S(2)}) %collective-permute-start.18) | collective-permute-done | bytes 147488 | tf_op jit(solution)/shard_map/ppermute | solution.py:447
  166.4 3.8 %collective-permute-done.20.refs_6_ = bf16[288,256]{1,0:T(8,128)(2,1)S(1)} collective-permute-done((bf16[288,256]{1,0:T(8,128)(2,1)S(1)}, bf16[288,256]{1,0:T(8,128)(2,1)S(1)}, u32[]{:S(2)}, u32[]{:S(2)}) %collective-permute-start.20) | collective-permute-done | bytes 147488 | tf_op jit(solution)/shard_map/ppermute | solution.py:447
  170.2 1.7 collective-permute-done.21.refs_7_
  171.8 1.6 copy-done.5
  173.4 1.8 shard_map.125
  (58 shorter events, 5.2 us)
Async XLA Ops:
  0.6 1.0 copy-start.1
  1.7 1.0 copy-start.9
  2.8 10.6 %collective-permute-start = (bf16[2,64,512]{2,1,0:T(8,128)(2,1)S(1)}, bf16[2,64,512]{2,1,0:T(8,128)(2,1)S(1)}, u32[]{:S(2)}, u32[]{:S(2)}) collective-permute-start(bf16[2,64,512]{2,1,0:T(8,128)(2,1)S(1)} %get-tuple-element.72), channel_id=1, source_target_pairs={{0,4},{4,8},{8,12},{12,16},{16,20},{20,24},{24,28},{28,0},{1,5},{5... | collective-permute-start | bytes 393224 | tf_op jit(solution)/shard_map/ppermute | solution.py:447
  4.1 10.5 %collective-permute-start.1 = (bf16[2,64,512]{2,1,0:T(8,128)(2,1)S(1)}, bf16[2,64,512]{2,1,0:T(8,128)(2,1)S(1)}, u32[]{:S(2)}, u32[]{:S(2)}) collective-permute-start(bf16[2,64,512]{2,1,0:T(8,128)(2,1)S(1)} %get-tuple-element.73), channel_id=1, source_target_pairs={{0,8},{4,12},{8,16},{12,20},{16,24},{20,28},{24,0},{28,4},{1,9},{5... | collective-permute-start | bytes 393224 | tf_op jit(solution)/shard_map/ppermute | solution.py:447
  5.4 21.1 %collective-permute-start.2 = (bf16[2,64,512]{2,1,0:T(8,128)(2,1)S(1)}, bf16[2,64,512]{2,1,0:T(8,128)(2,1)S(1)}, u32[]{:S(2)}, u32[]{:S(2)}) collective-permute-start(bf16[2,64,512]{2,1,0:T(8,128)(2,1)S(1)} %get-tuple-element.74), channel_id=1, source_target_pairs={{0,12},{4,16},{8,20},{12,24},{16,28},{20,0},{24,4},{28,8},{1,13},{... | collective-permute-start | bytes 393224 | tf_op jit(solution)/shard_map/ppermute | solution.py:447
  6.3 20.2 %collective-permute-start.3 = (bf16[2,64,512]{2,1,0:T(8,128)(2,1)S(1)}, bf16[2,64,512]{2,1,0:T(8,128)(2,1)S(1)}, u32[]{:S(2)}, u32[]{:S(2)}) collective-permute-start(bf16[2,64,512]{2,1,0:T(8,128)(2,1)S(1)} %get-tuple-element.75), channel_id=1, source_target_pairs={{0,16},{4,20},{8,24},{12,28},{16,0},{20,4},{24,8},{28,12},{1,17},{... | collective-permute-start | bytes 393224 | tf_op jit(solution)/shard_map/ppermute | solution.py:447
  7.7 18.8 %collective-permute-start.4 = (bf16[2,64,512]{2,1,0:T(8,128)(2,1)S(1)}, bf16[2,64,512]{2,1,0:T(8,128)(2,1)S(1)}, u32[]{:S(2)}, u32[]{:S(2)}) collective-permute-start(bf16[2,64,512]{2,1,0:T(8,128)(2,1)S(1)} %get-tuple-element.76), channel_id=1, source_target_pairs={{0,20},{4,24},{8,28},{12,0},{16,4},{20,8},{24,12},{28,16},{1,21},{... | collective-permute-start | bytes 393224 | tf_op jit(solution)/shard_map/ppermute | solution.py:447
  13.4 15.5 %collective-permute-start.5 = (bf16[2,64,512]{2,1,0:T(8,128)(2,1)S(1)}, bf16[2,64,512]{2,1,0:T(8,128)(2,1)S(1)}, u32[]{:S(2)}, u32[]{:S(2)}) collective-permute-start(bf16[2,64,512]{2,1,0:T(8,128)(2,1)S(1)} %get-tuple-element.77), channel_id=1, source_target_pairs={{0,24},{4,28},{8,0},{12,4},{16,8},{20,12},{24,16},{28,20},{1,25},{... | collective-permute-start | bytes 393224 | tf_op jit(solution)/shard_map/ppermute | solution.py:447
  14.6 15.4 %collective-permute-start.6 = (bf16[2,64,512]{2,1,0:T(8,128)(2,1)S(1)}, bf16[2,64,512]{2,1,0:T(8,128)(2,1)S(1)}, u32[]{:S(2)}, u32[]{:S(2)}) collective-permute-start(bf16[2,64,512]{2,1,0:T(8,128)(2,1)S(1)} %get-tuple-element.78), channel_id=1, source_target_pairs={{0,28},{4,0},{8,4},{12,8},{16,12},{20,16},{24,20},{28,24},{1,29},{... | collective-permute-start | bytes 393224 | tf_op jit(solution)/shard_map/ppermute | solution.py:447
  16.0 1.7 copy-start
  17.7 1.0 copy-start.2
  18.8 7.5 %copy-start.11 = (s32[1,8]{1,0:T(1,128)S(1)}, s32[1,8]{1,0:T(1,128)}, u32[]{:S(2)}) copy-start(s32[1,8]{1,0:T(1,128)} %param.13) | copy-start | bytes 100
  31.7 3.8 %collective-permute-start.7 = (bf16[2,2,64,256]{3,2,1,0:T(8,128)(2,1)S(1)}, bf16[2,2,64,256]{3,2,1,0:T(8,128)(2,1)S(1)}, u32[]{:S(2)}, u32[]{:S(2)}) collective-permute-start(bf16[2,2,64,256]{3,2,1,0:T(8,128)(2,1)S(1)} %get-tuple-element.95), channel_id=1, source_target_pairs={{0,4},{4,8},{8,12},{12,16},{16,20},{20,24},{24,28},{28,0},{1,5},{5... | collective-permute-start | bytes 393224 | tf_op jit(solution)/shard_map/ppermute | solution.py:447
  31.7 5.6 %collective-permute-start.8 = (bf16[2,2,64,256]{3,2,1,0:T(8,128)(2,1)S(1)}, bf16[2,2,64,256]{3,2,1,0:T(8,128)(2,1)S(1)}, u32[]{:S(2)}, u32[]{:S(2)}) collective-permute-start(bf16[2,2,64,256]{3,2,1,0:T(8,128)(2,1)S(1)} %get-tuple-element.96), channel_id=1, source_target_pairs={{0,8},{4,12},{8,16},{12,20},{16,24},{20,28},{24,0},{28,4},{1,9},{5... | collective-permute-start | bytes 393224 | tf_op jit(solution)/shard_map/ppermute | solution.py:447
  31.7 6.8 %collective-permute-start.9 = (bf16[2,2,64,256]{3,2,1,0:T(8,128)(2,1)S(1)}, bf16[2,2,64,256]{3,2,1,0:T(8,128)(2,1)S(1)}, u32[]{:S(2)}, u32[]{:S(2)}) collective-permute-start(bf16[2,2,64,256]{3,2,1,0:T(8,128)(2,1)S(1)} %get-tuple-element.97), channel_id=1, source_target_pairs={{0,12},{4,16},{8,20},{12,24},{16,28},{20,0},{24,4},{28,8},{1,13},{... | collective-permute-start | bytes 393224 | tf_op jit(solution)/shard_map/ppermute | solution.py:447
  32.6 18.4 %collective-permute-start.10 = (bf16[2,2,64,256]{3,2,1,0:T(8,128)(2,1)S(1)}, bf16[2,2,64,256]{3,2,1,0:T(8,128)(2,1)S(1)}, u32[]{:S(2)}, u32[]{:S(2)}) collective-permute-start(bf16[2,2,64,256]{3,2,1,0:T(8,128)(2,1)S(1)} %get-tuple-element.98), channel_id=1, source_target_pairs={{0,16},{4,20},{8,24},{12,28},{16,0},{20,4},{24,8},{28,12},{1,17},{... | collective-permute-start | bytes 393224 | tf_op jit(solution)/shard_map/ppermute | solution.py:447
  35.3 15.8 %collective-permute-start.11 = (bf16[2,2,64,256]{3,2,1,0:T(8,128)(2,1)S(1)}, bf16[2,2,64,256]{3,2,1,0:T(8,128)(2,1)S(1)}, u32[]{:S(2)}, u32[]{:S(2)}) collective-permute-start(bf16[2,2,64,256]{3,2,1,0:T(8,128)(2,1)S(1)} %get-tuple-element.99), channel_id=1, source_target_pairs={{0,20},{4,24},{8,28},{12,0},{16,4},{20,8},{24,12},{28,16},{1,21},{... | collective-permute-start | bytes 393224 | tf_op jit(solution)/shard_map/ppermute | solution.py:447
  35.5 20.5 %collective-permute-start.12 = (bf16[2,2,64,256]{3,2,1,0:T(8,128)(2,1)S(1)}, bf16[2,2,64,256]{3,2,1,0:T(8,128)(2,1)S(1)}, u32[]{:S(2)}, u32[]{:S(2)}) collective-permute-start(bf16[2,2,64,256]{3,2,1,0:T(8,128)(2,1)S(1)} %get-tuple-element.100), channel_id=1, source_target_pairs={{0,24},{4,28},{8,0},{12,4},{16,8},{20,12},{24,16},{28,20},{1,25},{... | collective-permute-start | bytes 393224 | tf_op jit(solution)/shard_map/ppermute | solution.py:447
  37.4 18.7 %collective-permute-start.13 = (bf16[2,2,64,256]{3,2,1,0:T(8,128)(2,1)S(1)}, bf16[2,2,64,256]{3,2,1,0:T(8,128)(2,1)S(1)}, u32[]{:S(2)}, u32[]{:S(2)}) collective-permute-start(bf16[2,2,64,256]{3,2,1,0:T(8,128)(2,1)S(1)} %get-tuple-element.101), channel_id=1, source_target_pairs={{0,28},{4,0},{8,4},{12,8},{16,12},{20,16},{24,20},{28,24},{1,29},{... | collective-permute-start | bytes 393224 | tf_op jit(solution)/shard_map/ppermute | solution.py:447
  56.1 25.4 %all-to-all-start.1 = ((bf16[8,2,2,64,256]{4,3,2,1,0:T(8,128)(2,1)}), bf16[8,2,2,64,256]{4,3,2,1,0:T(8,128)(2,1)S(1)}, u32[]{:S(2)}, u32[]{:S(2)}) async-start(bf16[8,2,2,64,256]{4,3,2,1,0:T(8,128)(2,1)} %get-tuple-element.111), calls=%async_computation.1 | async-start | bytes 2097152 | tf_op jit(solution)/shard_map/all_to_all | solution.py:437
  81.5 1.0 copy-start.7
  82.5 29.8 %all-to-all-start = ((bf16[8,2,2,64,256]{4,3,2,1,0:T(8,128)(2,1)}), bf16[8,2,2,64,256]{4,3,2,1,0:T(8,128)(2,1)S(1)}, u32[]{:S(2)}, u32[]{:S(2)}) async-start(bf16[8,2,2,64,256]{4,3,2,1,0:T(8,128)(2,1)} %get-tuple-element.110), calls=%async_computation | async-start | bytes 2097152 | tf_op jit(solution)/shard_map/all_to_all | solution.py:437
  88.8 1.2 copy-start.8
  90.0 27.3 %copy-start.3 = (bf16[1,512,512]{2,1,0:T(8,128)(2,1)S(1)}, bf16[1,512,512]{2,1,0:T(8,128)(2,1)}, u32[]{:S(2)}) copy-start(bf16[1,512,512]{2,1,0:T(8,128)(2,1)} %param.8) | copy-start | bytes 1572868
  90.0 27.3 %copy-start.10 = (bf16[1,512,512]{2,1,0:T(8,128)(2,1)S(1)}, bf16[1,512,512]{2,1,0:T(8,128)(2,1)}, u32[]{:S(2)}) copy-start(bf16[1,512,512]{2,1,0:T(8,128)(2,1)} %param.9) | copy-start | bytes 1572868
  111.3 1.0 copy-start.6
  112.2 28.3 %all-to-all-start.2 = ((bf16[8,2,2,64,256]{4,3,2,1,0:T(8,128)(2,1)}), bf16[8,2,2,64,256]{4,3,2,1,0:T(8,128)(2,1)S(1)}, u32[]{:S(2)}, u32[]{:S(2)}) async-start(bf16[8,2,2,64,256]{4,3,2,1,0:T(8,128)(2,1)} %copy-done.6), calls=%async_computation.2 | async-start | bytes 2097152 | tf_op jit(solution)/shard_map/all_to_all | solution.py:437
  133.5 1.3 copy-start.4
  134.8 5.7 %collective-permute-start.14 = (f32[3584]{0:T(1024)S(1)}, f32[3584]{0:T(1024)S(1)}, u32[]{:S(2)}, u32[]{:S(2)}) collective-permute-start(f32[3584]{0:T(1024)S(1)} %pad_maximum_fusion), channel_id=1, source_target_pairs={{0,1},{1,0},{2,3},{3,2},{4,5},{5,4},{6,7},{7,6},{8,9},{9,8},{10,11... | collective-permute-start | bytes 43016 | tf_op jit(solution)/shard_map/ppermute | solution.py:478
  141.5 6.0 %collective-permute-start.15 = (bf16[288,256]{1,0:T(8,128)(2,1)S(1)}, bf16[288,256]{1,0:T(8,128)(2,1)S(1)}, u32[]{:S(2)}, u32[]{:S(2)}) collective-permute-start(bf16[288,256]{1,0:T(8,128)(2,1)S(1)} %get-tuple-element.126), channel_id=1, source_target_pairs={{0,4},{4,8},{8,12},{12,16},{16,20},{20,24},{24,28},{28,0},{1,5},{5... | collective-permute-start | bytes 442376 | tf_op jit(solution)/shard_map/ppermute | solution.py:447
  141.6 6.9 %collective-permute-start.16 = (bf16[288,256]{1,0:T(8,128)(2,1)S(1)}, bf16[288,256]{1,0:T(8,128)(2,1)S(1)}, u32[]{:S(2)}, u32[]{:S(2)}) collective-permute-start(bf16[288,256]{1,0:T(8,128)(2,1)S(1)} %get-tuple-element.127), channel_id=1, source_target_pairs={{0,8},{4,12},{8,16},{12,20},{16,24},{20,28},{24,0},{28,4},{1,9},{5... | collective-permute-start | bytes 442376 | tf_op jit(solution)/shard_map/ppermute | solution.py:447
  143.9 19.3 %collective-permute-start.17 = (bf16[288,256]{1,0:T(8,128)(2,1)S(1)}, bf16[288,256]{1,0:T(8,128)(2,1)S(1)}, u32[]{:S(2)}, u32[]{:S(2)}) collective-permute-start(bf16[288,256]{1,0:T(8,128)(2,1)S(1)} %get-tuple-element.128), channel_id=1, source_target_pairs={{0,12},{4,16},{8,20},{12,24},{16,28},{20,0},{24,4},{28,8},{1,13},{... | collective-permute-start | bytes 442376 | tf_op jit(solution)/shard_map/ppermute | solution.py:447
  145.3 21.1 %collective-permute-start.18 = (bf16[288,256]{1,0:T(8,128)(2,1)S(1)}, bf16[288,256]{1,0:T(8,128)(2,1)S(1)}, u32[]{:S(2)}, u32[]{:S(2)}) collective-permute-start(bf16[288,256]{1,0:T(8,128)(2,1)S(1)} %get-tuple-element.129), channel_id=1, source_target_pairs={{0,16},{4,20},{8,24},{12,28},{16,0},{20,4},{24,8},{28,12},{1,17},{... | collective-permute-start | bytes 442376 | tf_op jit(solution)/shard_map/ppermute | solution.py:447
  146.3 20.1 %collective-permute-start.19 = (bf16[288,256]{1,0:T(8,128)(2,1)S(1)}, bf16[288,256]{1,0:T(8,128)(2,1)S(1)}, u32[]{:S(2)}, u32[]{:S(2)}) collective-permute-start(bf16[288,256]{1,0:T(8,128)(2,1)S(1)} %get-tuple-element.130), channel_id=1, source_target_pairs={{0,20},{4,24},{8,28},{12,0},{16,4},{20,8},{24,12},{28,16},{1,21},{... | collective-permute-start | bytes 442376 | tf_op jit(solution)/shard_map/ppermute | solution.py:447
  147.5 22.7 %collective-permute-start.20 = (bf16[288,256]{1,0:T(8,128)(2,1)S(1)}, bf16[288,256]{1,0:T(8,128)(2,1)S(1)}, u32[]{:S(2)}, u32[]{:S(2)}) collective-permute-start(bf16[288,256]{1,0:T(8,128)(2,1)S(1)} %get-tuple-element.131), channel_id=1, source_target_pairs={{0,24},{4,28},{8,0},{12,4},{16,8},{20,12},{24,16},{28,20},{1,25},{... | collective-permute-start | bytes 442376 | tf_op jit(solution)/shard_map/ppermute | solution.py:447
  148.4 23.4 %collective-permute-start.21 = (bf16[288,256]{1,0:T(8,128)(2,1)S(1)}, bf16[288,256]{1,0:T(8,128)(2,1)S(1)}, u32[]{:S(2)}, u32[]{:S(2)}) collective-permute-start(bf16[288,256]{1,0:T(8,128)(2,1)S(1)} %get-tuple-element.132), channel_id=1, source_target_pairs={{0,28},{4,0},{8,4},{12,8},{16,12},{20,16},{24,20},{28,24},{1,29},{... | collective-permute-start | bytes 442376 | tf_op jit(solution)/shard_map/ppermute | solution.py:447
  171.8 1.6 copy-start.5

commit v4 on v3

--- a/solution.py
+++ b/solution.py
@@ -444,8 +444,10 @@
     routes = [[(i, (i + d) % count) for i in range(count)] for d in range(count)]
 
     def around_ring(by_distance):
-        sent = [lax.ppermute(a, "ctx", route) for a, route in zip(by_distance[1:], routes[1:])]
-        return [by_distance[0], *sent]
+        arrived = list(by_distance)
+        for d in sorted(range(1, count), key=lambda d: abs(2 * d - count)):
+            arrived[d] = lax.ppermute(by_distance[d], "ctx", routes[d])
+        return arrived
 
     here = me.astype(jnp.int32)[None]
     chunk = jax.ShapeDtypeStruct((2, rows, width), bf16)

time: 178 us -> 178 us (level)
  the two profiles are of different devices: /device:TPU:15 before, /device:TPU:11 now
where the time goes in v4:
time: 178 us; the launch traced here: 177 us
  Pallas kernels  70.6 us (40%)
  waiting for transfers between devices  44.8 us (25%)
  starting transfers between devices  42.4 us (24%)
  local copies, waits for them, and re-layouts  13 us (7%)
  other arithmetic  3.6 us (2%)
  between operations  2.72 us (2%)
    pallas_call x4, Pallas kernels, call(): pl.pallas_call(kernel, grid_spec=pltpu.PrefetchScalarGridSpec(num_scalar_...  66.1 us
    ppermute x21, waiting for transfers between devices, around_ring(): arrived[d] = lax.ppermute(by_distance[d], 'ctx', routes[d])  43.6 us
    ppermute x21, starting transfers between devices, around_ring(): arrived[d] = lax.ppermute(by_distance[d], 'ctx', routes[d])  21.8 us
    all_to_all x3, starting transfers between devices, exchange(): return lax.all_to_all(a, 'ctx', 0, 0)  14.7 us
    unnamed x28, local copies, waits for them, and re-layouts  12.2 us
    ppermute x1, starting transfers between devices, on_device(): sums = sums + lax.ppermute(sums, 'dp', [(i, i ^ 1) for i in range(trees)])  5.93 us
    pallas_call x4, Pallas kernels, layout(): pl.pallas_call(kernel, grid_spec=pltpu.PrefetchScalarGridSpec(num_scalar_...  4.48 us
  transfers between devices with their start and end apart: 25, of which 13 were waited for; matrix products, arithmetic and copies ran while one was open for 2% of the time, Pallas kernels for 37%

profile of v4, /device:TPU:11, one launch (start us, length us, event | category | flops | bytes accessed | tf_op | source)
XLA Modules:
  0.0 177.2 jit_solution(14460278149972446657)
XLA Ops:
  0.6 1.0 copy-done.1
  1.7 1.0 copy-done.9
  2.8 1.3 collective-permute-start
  4.1 1.3 collective-permute-start.1
  5.4 0.9 collective-permute-start.2
  6.3 1.3 collective-permute-start.3
  7.7 1.0 collective-permute-start.4
  8.7 0.8 select_reduce_fusion.3
  9.5 0.8 select_reduce_fusion.2
  10.3 0.8 select_reduce_fusion.1
  13.4 1.2 collective-permute-start.5
  14.6 1.4 collective-permute-start.6
  16.0 1.7 copy-done
  17.7 1.0 copy-done.2
  18.8 7.4 %shard_map.119 = (f32[4,5,512]{2,1,0:T(8,128)S(1)}, f32[4,5,512]{2,1,0:T(8,128)S(1)}, f32[4,5,512]{2,1,0:T(8,128)S(1)}) custom-call(s32[2]{0:T(128)S(1)} %pad_add_fusion.mode_ref.refs_0_, bf16[512,2560]{1,0:T(8,128)(2,1)S(1)} %bitcast.28, bf16[512,2560]{1,0:T(8,128)(2,1)} %bitcast.36, bf16[512,2560]{1,0:T(8,128)(2,1)} %bitcast.35, bf16[512,512]{1,0:T(8,128)(2,1)S(1)} %bitcast.30), custom_call_target="tpu_custom_call" | custom-call | flops 2013265920 | bytes 10485760 | tf_op jit(solution)/shard_map/pallas_call | solution.py:212
  26.5 2.3 %collective-permute-done.5.refs_6_ = bf16[2,64,512]{2,1,0:T(8,128)(2,1)S(1)} collective-permute-done((bf16[2,64,512]{2,1,0:T(8,128)(2,1)S(1)}, bf16[2,64,512]{2,1,0:T(8,128)(2,1)S(1)}, u32[]{:S(2)}, u32[]{:S(2)}) %collective-permute-start.5) | collective-permute-done | bytes 131104 | tf_op jit(solution)/shard_map/ppermute | solution.py:449
  28.8 1.2 collective-permute-done.6.refs_7_
  30.0 1.7 shard_map.120
  31.7 0.9 collective-permute-start.9
  32.6 2.6 %collective-permute-start.10 = (bf16[2,2,64,256]{3,2,1,0:T(8,128)(2,1)S(1)}, bf16[2,2,64,256]{3,2,1,0:T(8,128)(2,1)S(1)}, u32[]{:S(2)}, u32[]{:S(2)}) collective-permute-start(bf16[2,2,64,256]{3,2,1,0:T(8,128)(2,1)S(1)} %get-tuple-element.98), channel_id=1, source_target_pairs={{0,16},{4,20},{8,24},{12,28},{16,0},{20,4},{24,8},{28,12},{1,17},{... | collective-permute-start | bytes 393224 | tf_op jit(solution)/shard_map/ppermute | solution.py:449
  35.5 1.8 %collective-permute-start.12 = (bf16[2,2,64,256]{3,2,1,0:T(8,128)(2,1)S(1)}, bf16[2,2,64,256]{3,2,1,0:T(8,128)(2,1)S(1)}, u32[]{:S(2)}, u32[]{:S(2)}) collective-permute-start(bf16[2,2,64,256]{3,2,1,0:T(8,128)(2,1)S(1)} %get-tuple-element.100), channel_id=1, source_target_pairs={{0,24},{4,28},{8,0},{12,4},{16,8},{20,12},{24,16},{28,20},{1,25},{... | collective-permute-start | bytes 393224 | tf_op jit(solution)/shard_map/ppermute | solution.py:449
  38.1 12.4 %collective-permute-done.10.refs_10_ = bf16[2,2,64,256]{3,2,1,0:T(8,128)(2,1)S(1)} collective-permute-done((bf16[2,2,64,256]{3,2,1,0:T(8,128)(2,1)S(1)}, bf16[2,2,64,256]{3,2,1,0:T(8,128)(2,1)S(1)}, u32[]{:S(2)}, u32[]{:S(2)}) %collective-permute-start.10) | collective-permute-done | bytes 131104 | tf_op jit(solution)/shard_map/ppermute | solution.py:449
  50.5 4.8 %collective-permute-done.12.refs_12_ = bf16[2,2,64,256]{3,2,1,0:T(8,128)(2,1)S(1)} collective-permute-done((bf16[2,2,64,256]{3,2,1,0:T(8,128)(2,1)S(1)}, bf16[2,2,64,256]{3,2,1,0:T(8,128)(2,1)S(1)}, u32[]{:S(2)}, u32[]{:S(2)}) %collective-permute-start.12) | collective-permute-done | bytes 131104 | tf_op jit(solution)/shard_map/ppermute | solution.py:449
  55.3 3.6 %all-to-all-start.1 = ((bf16[8,2,2,64,256]{4,3,2,1,0:T(8,128)(2,1)}), bf16[8,2,2,64,256]{4,3,2,1,0:T(8,128)(2,1)S(1)}, u32[]{:S(2)}, u32[]{:S(2)}) async-start(bf16[8,2,2,64,256]{4,3,2,1,0:T(8,128)(2,1)} %get-tuple-element.111), calls=%async_computation.1 | async-start | bytes 2097152 | tf_op jit(solution)/shard_map/all_to_all | solution.py:437
  59.0 21.3 %shard_map.121 = (f32[512,2560]{1,0:T(8,128)}, f32[4,5,512]{2,1,0:T(8,128)S(1)}, bf16[8,2,2,64,256]{4,3,2,1,0:T(8,128)(2,1)}, f32[2,1,256]{2,1,0:T(1,128)S(1)}) custom-call(s32[2]{0:T(128)S(1)} %pad_add_fusion.mode_ref.refs_0_, bf16[512,2560]{1,0:T(8,128)(2,1)} %bitcast.25, bf16[512,2560]{1,0:T(8,128)(2,1)} %bitcast.37, ...), custom_call_target="tpu_custom_call" | custom-call | flops 13421772800 | bytes 5242880 | tf_op jit(solution)/shard_map/pallas_call | solution.py:212
  80.7 1.0 copy-done.7
  81.7 6.3 %all-to-all-start = ((bf16[8,2,2,64,256]{4,3,2,1,0:T(8,128)(2,1)}), bf16[8,2,2,64,256]{4,3,2,1,0:T(8,128)(2,1)S(1)}, u32[]{:S(2)}, u32[]{:S(2)}) async-start(bf16[8,2,2,64,256]{4,3,2,1,0:T(8,128)(2,1)} %get-tuple-element.110), calls=%async_computation | async-start | bytes 2097152 | tf_op jit(solution)/shard_map/all_to_all | solution.py:437
  88.1 1.2 copy-done.8
  89.3 21.2 %shard_map.122 = (f32[512,2560]{1,0:T(8,128)}, f32[4,5,512]{2,1,0:T(8,128)S(1)}, bf16[8,2,2,64,256]{4,3,2,1,0:T(8,128)(2,1)S(1)}, f32[2,1,256]{2,1,0:T(1,128)S(1)}) custom-call(s32[2]{0:T(128)S(1)} %pad_add_fusion.mode_ref.refs_0_, bf16[512,2560]{1,0:T(8,128)(2,1)} %bitcast.26, ...), custom_call_target="tpu_custom_call", output_to_operand_aliasing={{0}: (7, {}), {1}: (8, {})} | custom-call | flops 13421772800 | bytes 5242880 | tf_op jit(solution)/shard_map/pallas_call | solution.py:212
  110.5 1.0 copy-done.6
  111.5 4.7 %all-to-all-start.2 = ((bf16[8,2,2,64,256]{4,3,2,1,0:T(8,128)(2,1)}), bf16[8,2,2,64,256]{4,3,2,1,0:T(8,128)(2,1)S(1)}, u32[]{:S(2)}, u32[]{:S(2)}) async-start(bf16[8,2,2,64,256]{4,3,2,1,0:T(8,128)(2,1)} %copy-done.6), calls=%async_computation.2 | async-start | bytes 2097152 | tf_op jit(solution)/shard_map/all_to_all | solution.py:437
  116.2 16.2 %shard_map.123 = (bf16[512,2560]{1,0:T(8,128)(2,1)}, f32[2,512,512]{2,1,0:T(8,128)S(1)}, f32[1,2560]{1,0:T(1,128)S(1)}, f32[2,1,512]{2,1,0:T(1,128)S(1)}) custom-call(s32[2]{0:T(128)S(1)} %pad_add_fusion.mode_ref.refs_0_, bf16[512,2560]{1,0:T(8,128)(2,1)} %bitcast.27, bf16[512,2560]{1,0:T(8,128)(2,1)} %bitcast.39, ...), custom_call_target="tpu_custom_call" | custom-call | flops 10066329600 | bytes 10485760 | tf_op jit(solution)/shard_map/pallas_call | solution.py:212
  132.3 1.3 copy-done.4
  133.7 5.9 %collective-permute-start.14 = (f32[3584]{0:T(1024)S(1)}, f32[3584]{0:T(1024)S(1)}, u32[]{:S(2)}, u32[]{:S(2)}) collective-permute-start(f32[3584]{0:T(1024)S(1)} %pad_maximum_fusion), channel_id=1, source_target_pairs={{0,1},{1,0},{2,3},{3,2},{4,5},{5,4},{6,7},{7,6},{8,9},{9,8},{10,11... | collective-permute-start | bytes 43016 | tf_op jit(solution)/shard_map/ppermute | solution.py:480
  140.5 0.9 shard_map.124
  141.5 1.2 collective-permute-start.15
  142.7 1.2 collective-permute-start.16
  143.9 1.2 collective-permute-start.17
  145.1 1.2 collective-permute-start.18
  146.3 1.2 collective-permute-start.19
  147.5 1.0 collective-permute-start.20
  148.4 1.0 collective-permute-done.16.refs_2_
  150.6 14.0 %collective-permute-done.17.refs_3_ = bf16[288,256]{1,0:T(8,128)(2,1)S(1)} collective-permute-done((bf16[288,256]{1,0:T(8,128)(2,1)S(1)}, bf16[288,256]{1,0:T(8,128)(2,1)S(1)}, u32[]{:S(2)}, u32[]{:S(2)}) %collective-permute-start.17) | collective-permute-done | bytes 147488 | tf_op jit(solution)/shard_map/ppermute | solution.py:449
  164.6 3.2 %collective-permute-done.18.refs_4_ = bf16[288,256]{1,0:T(8,128)(2,1)S(1)} collective-permute-done((bf16[288,256]{1,0:T(8,128)(2,1)S(1)}, bf16[288,256]{1,0:T(8,128)(2,1)S(1)}, u32[]{:S(2)}, u32[]{:S(2)}) %collective-permute-start.18) | collective-permute-done | bytes 147488 | tf_op jit(solution)/shard_map/ppermute | solution.py:449
  167.7 2.4 %collective-permute-done.20.refs_6_ = bf16[288,256]{1,0:T(8,128)(2,1)S(1)} collective-permute-done((bf16[288,256]{1,0:T(8,128)(2,1)S(1)}, bf16[288,256]{1,0:T(8,128)(2,1)S(1)}, u32[]{:S(2)}, u32[]{:S(2)}) %collective-permute-start.20) | collective-permute-done | bytes 147488 | tf_op jit(solution)/shard_map/ppermute | solution.py:449
  170.1 1.9 %collective-permute-done.21.refs_7_ = bf16[288,256]{1,0:T(8,128)(2,1)S(1)} collective-permute-done((bf16[288,256]{1,0:T(8,128)(2,1)S(1)}, bf16[288,256]{1,0:T(8,128)(2,1)S(1)}, u32[]{:S(2)}, u32[]{:S(2)}) %collective-permute-start.21) | collective-permute-done | bytes 147488 | tf_op jit(solution)/shard_map/ppermute | solution.py:449
  172.0 1.6 copy-done.5
  173.6 1.8 shard_map.125
  (58 shorter events, 5.9 us)
Async XLA Ops:
  0.6 1.0 copy-start.1
  1.7 1.0 copy-start.9
  2.8 10.6 %collective-permute-start = (bf16[2,64,512]{2,1,0:T(8,128)(2,1)S(1)}, bf16[2,64,512]{2,1,0:T(8,128)(2,1)S(1)}, u32[]{:S(2)}, u32[]{:S(2)}) collective-permute-start(bf16[2,64,512]{2,1,0:T(8,128)(2,1)S(1)} %get-tuple-element.72), channel_id=1, source_target_pairs={{0,4},{4,8},{8,12},{12,16},{16,20},{20,24},{24,28},{28,0},{1,5},{5... | collective-permute-start | bytes 393224 | tf_op jit(solution)/shard_map/ppermute | solution.py:449
  4.1 10.5 %collective-permute-start.1 = (bf16[2,64,512]{2,1,0:T(8,128)(2,1)S(1)}, bf16[2,64,512]{2,1,0:T(8,128)(2,1)S(1)}, u32[]{:S(2)}, u32[]{:S(2)}) collective-permute-start(bf16[2,64,512]{2,1,0:T(8,128)(2,1)S(1)} %get-tuple-element.73), channel_id=1, source_target_pairs={{0,8},{4,12},{8,16},{12,20},{16,24},{20,28},{24,0},{28,4},{1,9},{5... | collective-permute-start | bytes 393224 | tf_op jit(solution)/shard_map/ppermute | solution.py:449
  5.4 21.1 %collective-permute-start.2 = (bf16[2,64,512]{2,1,0:T(8,128)(2,1)S(1)}, bf16[2,64,512]{2,1,0:T(8,128)(2,1)S(1)}, u32[]{:S(2)}, u32[]{:S(2)}) collective-permute-start(bf16[2,64,512]{2,1,0:T(8,128)(2,1)S(1)} %get-tuple-element.74), channel_id=1, source_target_pairs={{0,12},{4,16},{8,20},{12,24},{16,28},{20,0},{24,4},{28,8},{1,13},{... | collective-permute-start | bytes 393224 | tf_op jit(solution)/shard_map/ppermute | solution.py:449
  6.3 20.2 %collective-permute-start.3 = (bf16[2,64,512]{2,1,0:T(8,128)(2,1)S(1)}, bf16[2,64,512]{2,1,0:T(8,128)(2,1)S(1)}, u32[]{:S(2)}, u32[]{:S(2)}) collective-permute-start(bf16[2,64,512]{2,1,0:T(8,128)(2,1)S(1)} %get-tuple-element.75), channel_id=1, source_target_pairs={{0,16},{4,20},{8,24},{12,28},{16,0},{20,4},{24,8},{28,12},{1,17},{... | collective-permute-start | bytes 393224 | tf_op jit(solution)/shard_map/ppermute | solution.py:449
  7.7 18.8 %collective-permute-start.4 = (bf16[2,64,512]{2,1,0:T(8,128)(2,1)S(1)}, bf16[2,64,512]{2,1,0:T(8,128)(2,1)S(1)}, u32[]{:S(2)}, u32[]{:S(2)}) collective-permute-start(bf16[2,64,512]{2,1,0:T(8,128)(2,1)S(1)} %get-tuple-element.76), channel_id=1, source_target_pairs={{0,20},{4,24},{8,28},{12,0},{16,4},{20,8},{24,12},{28,16},{1,21},{... | collective-permute-start | bytes 393224 | tf_op jit(solution)/shard_map/ppermute | solution.py:449
  13.4 15.4 %collective-permute-start.5 = (bf16[2,64,512]{2,1,0:T(8,128)(2,1)S(1)}, bf16[2,64,512]{2,1,0:T(8,128)(2,1)S(1)}, u32[]{:S(2)}, u32[]{:S(2)}) collective-permute-start(bf16[2,64,512]{2,1,0:T(8,128)(2,1)S(1)} %get-tuple-element.77), channel_id=1, source_target_pairs={{0,24},{4,28},{8,0},{12,4},{16,8},{20,12},{24,16},{28,20},{1,25},{... | collective-permute-start | bytes 393224 | tf_op jit(solution)/shard_map/ppermute | solution.py:449
  14.6 15.4 %collective-permute-start.6 = (bf16[2,64,512]{2,1,0:T(8,128)(2,1)S(1)}, bf16[2,64,512]{2,1,0:T(8,128)(2,1)S(1)}, u32[]{:S(2)}, u32[]{:S(2)}) collective-permute-start(bf16[2,64,512]{2,1,0:T(8,128)(2,1)S(1)} %get-tuple-element.78), channel_id=1, source_target_pairs={{0,28},{4,0},{8,4},{12,8},{16,12},{20,16},{24,20},{28,24},{1,29},{... | collective-permute-start | bytes 393224 | tf_op jit(solution)/shard_map/ppermute | solution.py:449
  16.0 1.7 copy-start
  17.7 1.0 copy-start.2
  18.8 7.5 %copy-start.11 = (s32[1,8]{1,0:T(1,128)S(1)}, s32[1,8]{1,0:T(1,128)}, u32[]{:S(2)}) copy-start(s32[1,8]{1,0:T(1,128)} %param.13) | copy-start | bytes 100
  31.7 3.8 %collective-permute-start.7 = (bf16[2,2,64,256]{3,2,1,0:T(8,128)(2,1)S(1)}, bf16[2,2,64,256]{3,2,1,0:T(8,128)(2,1)S(1)}, u32[]{:S(2)}, u32[]{:S(2)}) collective-permute-start(bf16[2,2,64,256]{3,2,1,0:T(8,128)(2,1)S(1)} %get-tuple-element.95), channel_id=1, source_target_pairs={{0,4},{4,8},{8,12},{12,16},{16,20},{20,24},{24,28},{28,0},{1,5},{5... | collective-permute-start | bytes 393224 | tf_op jit(solution)/shard_map/ppermute | solution.py:449
  31.7 5.6 %collective-permute-start.8 = (bf16[2,2,64,256]{3,2,1,0:T(8,128)(2,1)S(1)}, bf16[2,2,64,256]{3,2,1,0:T(8,128)(2,1)S(1)}, u32[]{:S(2)}, u32[]{:S(2)}) collective-permute-start(bf16[2,2,64,256]{3,2,1,0:T(8,128)(2,1)S(1)} %get-tuple-element.96), channel_id=1, source_target_pairs={{0,8},{4,12},{8,16},{12,20},{16,24},{20,28},{24,0},{28,4},{1,9},{5... | collective-permute-start | bytes 393224 | tf_op jit(solution)/shard_map/ppermute | solution.py:449
  31.7 6.4 %collective-permute-start.9 = (bf16[2,2,64,256]{3,2,1,0:T(8,128)(2,1)S(1)}, bf16[2,2,64,256]{3,2,1,0:T(8,128)(2,1)S(1)}, u32[]{:S(2)}, u32[]{:S(2)}) collective-permute-start(bf16[2,2,64,256]{3,2,1,0:T(8,128)(2,1)S(1)} %get-tuple-element.97), channel_id=1, source_target_pairs={{0,12},{4,16},{8,20},{12,24},{16,28},{20,0},{24,4},{28,8},{1,13},{... | collective-permute-start | bytes 393224 | tf_op jit(solution)/shard_map/ppermute | solution.py:449
  32.6 17.9 %collective-permute-start.10 = (bf16[2,2,64,256]{3,2,1,0:T(8,128)(2,1)S(1)}, bf16[2,2,64,256]{3,2,1,0:T(8,128)(2,1)S(1)}, u32[]{:S(2)}, u32[]{:S(2)}) collective-permute-start(bf16[2,2,64,256]{3,2,1,0:T(8,128)(2,1)S(1)} %get-tuple-element.98), channel_id=1, source_target_pairs={{0,16},{4,20},{8,24},{12,28},{16,0},{20,4},{24,8},{28,12},{1,17},{... | collective-permute-start | bytes 393224 | tf_op jit(solution)/shard_map/ppermute | solution.py:449
  35.3 15.3 %collective-permute-start.11 = (bf16[2,2,64,256]{3,2,1,0:T(8,128)(2,1)S(1)}, bf16[2,2,64,256]{3,2,1,0:T(8,128)(2,1)S(1)}, u32[]{:S(2)}, u32[]{:S(2)}) collective-permute-start(bf16[2,2,64,256]{3,2,1,0:T(8,128)(2,1)S(1)} %get-tuple-element.99), channel_id=1, source_target_pairs={{0,20},{4,24},{8,28},{12,0},{16,4},{20,8},{24,12},{28,16},{1,21},{... | collective-permute-start | bytes 393224 | tf_op jit(solution)/shard_map/ppermute | solution.py:449
  35.5 19.8 %collective-permute-start.12 = (bf16[2,2,64,256]{3,2,1,0:T(8,128)(2,1)S(1)}, bf16[2,2,64,256]{3,2,1,0:T(8,128)(2,1)S(1)}, u32[]{:S(2)}, u32[]{:S(2)}) collective-permute-start(bf16[2,2,64,256]{3,2,1,0:T(8,128)(2,1)S(1)} %get-tuple-element.100), channel_id=1, source_target_pairs={{0,24},{4,28},{8,0},{12,4},{16,8},{20,12},{24,16},{28,20},{1,25},{... | collective-permute-start | bytes 393224 | tf_op jit(solution)/shard_map/ppermute | solution.py:449
  37.4 18.0 %collective-permute-start.13 = (bf16[2,2,64,256]{3,2,1,0:T(8,128)(2,1)S(1)}, bf16[2,2,64,256]{3,2,1,0:T(8,128)(2,1)S(1)}, u32[]{:S(2)}, u32[]{:S(2)}) collective-permute-start(bf16[2,2,64,256]{3,2,1,0:T(8,128)(2,1)S(1)} %get-tuple-element.101), channel_id=1, source_target_pairs={{0,28},{4,0},{8,4},{12,8},{16,12},{20,16},{24,20},{28,24},{1,29},{... | collective-permute-start | bytes 393224 | tf_op jit(solution)/shard_map/ppermute | solution.py:449
  55.3 25.4 %all-to-all-start.1 = ((bf16[8,2,2,64,256]{4,3,2,1,0:T(8,128)(2,1)}), bf16[8,2,2,64,256]{4,3,2,1,0:T(8,128)(2,1)S(1)}, u32[]{:S(2)}, u32[]{:S(2)}) async-start(bf16[8,2,2,64,256]{4,3,2,1,0:T(8,128)(2,1)} %get-tuple-element.111), calls=%async_computation.1 | async-start | bytes 2097152 | tf_op jit(solution)/shard_map/all_to_all | solution.py:437
  80.7 1.0 copy-start.7
  81.7 29.8 %all-to-all-start = ((bf16[8,2,2,64,256]{4,3,2,1,0:T(8,128)(2,1)}), bf16[8,2,2,64,256]{4,3,2,1,0:T(8,128)(2,1)S(1)}, u32[]{:S(2)}, u32[]{:S(2)}) async-start(bf16[8,2,2,64,256]{4,3,2,1,0:T(8,128)(2,1)} %get-tuple-element.110), calls=%async_computation | async-start | bytes 2097152 | tf_op jit(solution)/shard_map/all_to_all | solution.py:437
  88.1 1.2 copy-start.8
  89.3 26.9 %copy-start.3 = (bf16[1,512,512]{2,1,0:T(8,128)(2,1)S(1)}, bf16[1,512,512]{2,1,0:T(8,128)(2,1)}, u32[]{:S(2)}) copy-start(bf16[1,512,512]{2,1,0:T(8,128)(2,1)} %param.8) | copy-start | bytes 1572868
  89.3 26.9 %copy-start.10 = (bf16[1,512,512]{2,1,0:T(8,128)(2,1)S(1)}, bf16[1,512,512]{2,1,0:T(8,128)(2,1)}, u32[]{:S(2)}) copy-start(bf16[1,512,512]{2,1,0:T(8,128)(2,1)} %param.9) | copy-start | bytes 1572868
  110.5 1.0 copy-start.6
  111.5 29.0 %all-to-all-start.2 = ((bf16[8,2,2,64,256]{4,3,2,1,0:T(8,128)(2,1)}), bf16[8,2,2,64,256]{4,3,2,1,0:T(8,128)(2,1)S(1)}, u32[]{:S(2)}, u32[]{:S(2)}) async-start(bf16[8,2,2,64,256]{4,3,2,1,0:T(8,128)(2,1)} %copy-done.6), calls=%async_computation.2 | async-start | bytes 2097152 | tf_op jit(solution)/shard_map/all_to_all | solution.py:437
  132.3 1.3 copy-start.4
  133.7 6.8 %collective-permute-start.14 = (f32[3584]{0:T(1024)S(1)}, f32[3584]{0:T(1024)S(1)}, u32[]{:S(2)}, u32[]{:S(2)}) collective-permute-start(f32[3584]{0:T(1024)S(1)} %pad_maximum_fusion), channel_id=1, source_target_pairs={{0,1},{1,0},{2,3},{3,2},{4,5},{5,4},{6,7},{7,6},{8,9},{9,8},{10,11... | collective-permute-start | bytes 43016 | tf_op jit(solution)/shard_map/ppermute | solution.py:480
  141.5 6.0 %collective-permute-start.15 = (bf16[288,256]{1,0:T(8,128)(2,1)S(1)}, bf16[288,256]{1,0:T(8,128)(2,1)S(1)}, u32[]{:S(2)}, u32[]{:S(2)}) collective-permute-start(bf16[288,256]{1,0:T(8,128)(2,1)S(1)} %get-tuple-element.126), channel_id=1, source_target_pairs={{0,4},{4,8},{8,12},{12,16},{16,20},{20,24},{24,28},{28,0},{1,5},{5... | collective-permute-start | bytes 442376 | tf_op jit(solution)/shard_map/ppermute | solution.py:449
  142.7 6.8 %collective-permute-start.16 = (bf16[288,256]{1,0:T(8,128)(2,1)S(1)}, bf16[288,256]{1,0:T(8,128)(2,1)S(1)}, u32[]{:S(2)}, u32[]{:S(2)}) collective-permute-start(bf16[288,256]{1,0:T(8,128)(2,1)S(1)} %get-tuple-element.127), channel_id=1, source_target_pairs={{0,8},{4,12},{8,16},{12,20},{16,24},{20,28},{24,0},{28,4},{1,9},{5... | collective-permute-start | bytes 442376 | tf_op jit(solution)/shard_map/ppermute | solution.py:449
  143.9 20.7 %collective-permute-start.17 = (bf16[288,256]{1,0:T(8,128)(2,1)S(1)}, bf16[288,256]{1,0:T(8,128)(2,1)S(1)}, u32[]{:S(2)}, u32[]{:S(2)}) collective-permute-start(bf16[288,256]{1,0:T(8,128)(2,1)S(1)} %get-tuple-element.128), channel_id=1, source_target_pairs={{0,12},{4,16},{8,20},{12,24},{16,28},{20,0},{24,4},{28,8},{1,13},{... | collective-permute-start | bytes 442376 | tf_op jit(solution)/shard_map/ppermute | solution.py:449
  145.1 22.6 %collective-permute-start.18 = (bf16[288,256]{1,0:T(8,128)(2,1)S(1)}, bf16[288,256]{1,0:T(8,128)(2,1)S(1)}, u32[]{:S(2)}, u32[]{:S(2)}) collective-permute-start(bf16[288,256]{1,0:T(8,128)(2,1)S(1)} %get-tuple-element.129), channel_id=1, source_target_pairs={{0,16},{4,20},{8,24},{12,28},{16,0},{20,4},{24,8},{28,12},{1,17},{... | collective-permute-start | bytes 442376 | tf_op jit(solution)/shard_map/ppermute | solution.py:449
  146.3 21.5 %collective-permute-start.19 = (bf16[288,256]{1,0:T(8,128)(2,1)S(1)}, bf16[288,256]{1,0:T(8,128)(2,1)S(1)}, u32[]{:S(2)}, u32[]{:S(2)}) collective-permute-start(bf16[288,256]{1,0:T(8,128)(2,1)S(1)} %get-tuple-element.130), channel_id=1, source_target_pairs={{0,20},{4,24},{8,28},{12,0},{16,4},{20,8},{24,12},{28,16},{1,21},{... | collective-permute-start | bytes 442376 | tf_op jit(solution)/shard_map/ppermute | solution.py:449
  147.5 22.7 %collective-permute-start.20 = (bf16[288,256]{1,0:T(8,128)(2,1)S(1)}, bf16[288,256]{1,0:T(8,128)(2,1)S(1)}, u32[]{:S(2)}, u32[]{:S(2)}) collective-permute-start(bf16[288,256]{1,0:T(8,128)(2,1)S(1)} %get-tuple-element.131), channel_id=1, source_target_pairs={{0,24},{4,28},{8,0},{12,4},{16,8},{20,12},{24,16},{28,20},{1,25},{... | collective-permute-start | bytes 442376 | tf_op jit(solution)/shard_map/ppermute | solution.py:449
  149.5 22.6 %collective-permute-start.21 = (bf16[288,256]{1,0:T(8,128)(2,1)S(1)}, bf16[288,256]{1,0:T(8,128)(2,1)S(1)}, u32[]{:S(2)}, u32[]{:S(2)}) collective-permute-start(bf16[288,256]{1,0:T(8,128)(2,1)S(1)} %get-tuple-element.132), channel_id=1, source_target_pairs={{0,28},{4,0},{8,4},{12,8},{16,12},{20,16},{24,20},{28,24},{1,29},{... | collective-permute-start | bytes 442376 | tf_op jit(solution)/shard_map/ppermute | solution.py:449
  172.0 1.6 copy-start.5
